TPU v7x, 256 devices: a whole 4x4x8 slice. The times are simulated.
256 devices in a mesh: term: 16 (over z, core), doc: 16 (over y, x).
Axes of the slice: x: 4, y: 4, z: 8, core: 2. Of those that a mesh axis runs over, the one named last changes fastest.
Arguments:
- tile_values: bfloat16 [768, 2048, 128], P('term', 'doc'), may hold values from 0.001 to 1, as said below
- tile_rows: int32 [16, 768], P('term', 'doc'), may hold values from 0 to 15, as said below
- tile_cols: int32 [16, 768], P('term', 'doc'), may hold values from 0 to 15, as said below
- tile_count: int32 [16, 16], P('term', 'doc'), may hold values from 16 to 48, as said below
- start_block: bfloat16 [32768, 256], P('doc'), may hold values from -6 to 6
Outputs:
- row_scale: float32 [32768], P('term')
- col_scale: float32 [32768], P('doc')
- left_basis: bfloat16 [32768, 256], P('term')
- right_basis: bfloat16 [32768, 256], P('doc')
Inputs may be any that keep to these rules, and one draw needn't show every extreme that they name: `tile_values`: entries are positive. `tile_rows`: within one block pair the occupied (row, column) pairs are distinct, and every tile row and tile column of every block pair holds an occupied tile. `tile_cols`: paired with tile_rows slot by slot. `tile_count`: some block pair has all 48 slots occupied.
All inputs are finite; a program needn't handle non-finite values.
Results may differ from a plain program's by a relative error of at most 0.006.
The roundings to bfloat16 on the way count: a program that leaves them out, or rounds other values in their place, can miss the bound.
Values may be sent and summed in bfloat16 or wider, within the bound.
No kernel may reach another device: no remote copies, remote signals or barrier semaphores. Data moves between devices by JAX's collectives and lax.ppermute only.
A program may use at most 64 MiB of HBM per device.

v0:
```python
import math

import jax
import jax.numpy as jnp
from jax import lax
from jax.sharding import Mesh
from jax.sharding import PartitionSpec as P

TILE = 128
K = 256
PASSES = 2
RB = 16
CB = 16
TERM = ("term_0", "term_1")
DOC = ("doc_0", "doc_1")


PRECISE = lax.Precision.HIGHEST


def by_axis(shard, axes):
    for axis in axes:
        shard = lax.psum(shard, axis)
    return shard


def sent_to_all(shard, axis):
    copies = jnp.broadcast_to(shard, (lax.axis_size(axis), *shard.shape))
    return lax.all_to_all(copies, axis, split_axis=0, concat_axis=0, tiled=True)


def of_everyone(shard, axis):
    return sent_to_all(shard, axis).sum(axis=0)


def split_up(shard, dim, count):
    before, after = (shard.shape[:dim], shard.shape[dim + 1 :])
    return jnp.moveaxis(shard.reshape(*before, count, -1, *after), dim, 0)


def summed_on_arrival(shard, axis, dim):
    pieces = split_up(shard, dim, lax.axis_size(axis))
    arrived = lax.all_to_all(pieces, axis, split_axis=0, concat_axis=0, tiled=True)
    return arrived.sum(axis=0)


def filled_up(lines, count):
    spare = -lines.shape[0] % count
    if not spare:
        return lines
    return jnp.concatenate([lines, jnp.zeros((spare, *lines.shape[1:]), lines.dtype)])


def joined_along(pieces, dim):
    shape = list(pieces.shape[1:])
    shape[dim] *= pieces.shape[0]
    return jnp.moveaxis(pieces, 0, dim).reshape(shape)


def gather_directly(shard, axis, dim):
    return joined_along(sent_to_all(shard, axis), dim)


def sum_by_parts(shard, axes):
    own = summed_on_arrival(filled_up(shard, lax.axis_size(axes)), axes, 0)
    whole = gather_directly(own, axes, 0)
    return whole[: len(shard)].reshape(shard.shape)


def in_one(arrays, axis):
    ends = [0]
    for a in arrays:
        ends.append(ends[-1] + a.size)
    so_far = sum_by_parts(jnp.concatenate([a.ravel() for a in arrays]), axis)
    return tuple((so_far[b:e].reshape(a.shape) for a, b, e in zip(arrays, ends, ends[1:])))


def summed_rows(shard, axes, dim):
    far, near = axes
    pieces = split_up(shard, dim, lax.axis_size(far))
    nearer = summed_on_arrival(pieces, near, dim + 1)
    arrived = lax.all_to_all(nearer, far, split_axis=0, concat_axis=0, tiled=True)
    return arrived.sum(axis=0)


def gathered_by_axis(shard, axes, dim):
    far, near = axes
    pieces = sent_to_all(sent_to_all(shard, far), near)
    return joined_along(pieces.swapaxes(0, 1).reshape(-1, *shard.shape), dim)


def sum_by_parts_2(shard, axes):
    own = summed_rows(filled_up(shard, lax.axis_size(axes[0]) * lax.axis_size(axes[1])), axes, 0)
    whole = gathered_by_axis(own, axes, 0)
    return whole[: len(shard)].reshape(shard.shape)


def packed_total(arrays, axis):
    ends = [0]
    for a in arrays:
        ends.append(ends[-1] + a.size)
    so_far = sum_by_parts_2(jnp.concatenate([a.ravel() for a in arrays]), axis)
    return tuple((so_far[b:e].reshape(a.shape) for a, b, e in zip(arrays, ends, ends[1:])))


def total_of(shard, axes):
    lines = shard.reshape(-1, shard.shape[-1])
    own = summed_rows(filled_up(lines, lax.axis_size(axes[0]) * lax.axis_size(axes[1])), axes, 0)
    whole = gathered_by_axis(own, axes, 0)
    return whole[: len(lines)].reshape(shard.shape)


def factor_inverse(gram):
    lower = jnp.linalg.cholesky(gram)
    identity = jnp.eye(gram.shape[0], dtype=gram.dtype)
    return jax.scipy.linalg.solve_triangular(lower, identity, lower=True).T


def over_tiles(tile_values, row_ids, col_ids, occupied, advance, initial):
    slot_total = tile_values.shape[0]
    group_size = math.gcd(slot_total, 32)

    def visit(turn_index, running):
        offset = turn_index * group_size
        tile_block = lax.dynamic_slice_in_dim(tile_values, offset, group_size, 0)
        row_block = lax.dynamic_slice_in_dim(row_ids, offset, group_size, 0)
        col_block = lax.dynamic_slice_in_dim(col_ids, offset, group_size, 0)
        live_mask = (offset + jnp.arange(group_size, dtype=jnp.int32) < occupied).astype(
            jnp.float32
        )
        return advance(running, tile_block, row_block, col_block, live_mask)

    turn_total = slot_total // group_size
    return lax.fori_loop(0, turn_total, visit, initial)


def row_vector(source):

    def advance(running, tile_block, row_block, col_block, live_mask):
        picked = jnp.take(source, col_block, axis=0)
        product = jnp.einsum(
            "gab,gb->ga", tile_block.astype(jnp.float32), picked, precision=PRECISE
        )
        return running.at[row_block].add(product * live_mask[:, None])

    return advance


def col_vector(source):

    def advance(running, tile_block, row_block, col_block, live_mask):
        picked = jnp.take(source, row_block, axis=0)
        product = jnp.einsum(
            "gab,ga->gb", tile_block.astype(jnp.float32), picked, precision=PRECISE
        )
        return running.at[col_block].add(product * live_mask[:, None])

    return advance


def row_matrix(source):

    def advance(running, tile_block, row_block, col_block, live_mask):
        picked = jnp.take(source, col_block, axis=0)
        product = jnp.einsum("gab,gbk->gak", tile_block, picked, preferred_element_type=jnp.float32)
        return running.at[row_block].add(product * live_mask[:, None, None])

    return advance


def col_matrix(source):

    def advance(running, tile_block, row_block, col_block, live_mask):
        picked = jnp.take(source, row_block, axis=0)
        product = jnp.einsum("gab,gak->gbk", tile_block, picked, preferred_element_type=jnp.float32)
        return running.at[col_block].add(product * live_mask[:, None, None])

    return advance


def per_device(tile_values, tile_rows, tile_cols, tile_count, start_block):
    row_list = tile_rows[0]
    col_list = tile_cols[0]
    occupied = tile_count[0, 0]
    terms_total = RB * TILE * lax.axis_size(TERM)
    docs_total = CB * TILE * lax.axis_size(DOC)

    def tile_pass(advance, initial):
        return over_tiles(tile_values, row_list, col_list, occupied, advance, initial)

    col_scale = jnp.ones((CB, TILE), jnp.float32)
    row_scale = jnp.ones((RB, TILE), jnp.float32)
    mean_part = jnp.sum(start_block.astype(jnp.float32), axis=0)
    start_mean = mean_part
    for sweep_index in range(PASSES):
        row_part = tile_pass(row_vector(col_scale), jnp.zeros((RB, TILE), jnp.float32))
        if sweep_index == 0:
            row_total, start_mean = (by_axis(row_part, DOC), by_axis(mean_part, DOC))
        else:
            row_total = by_axis(row_part, DOC)
        row_scale = 1.0 / row_total
        col_part = tile_pass(col_vector(row_scale), jnp.zeros((CB, TILE), jnp.float32))
        col_scale = 1.0 / of_everyone(col_part, TERM)
    weight_part = tile_pass(row_vector(col_scale), jnp.zeros((RB, TILE), jnp.float32)).reshape(-1)
    row_flat = row_scale.reshape(-1)
    col_flat = col_scale.reshape(-1)
    scaled_start = (col_flat[:, None] * start_block.astype(jnp.float32)).astype(jnp.bfloat16)
    left_part = tile_pass(
        row_matrix(scaled_start.reshape(CB, TILE, K)), jnp.zeros((RB, TILE, K), jnp.float32)
    )
    left_part = left_part.reshape(RB * TILE, K)
    left_share = RB * TILE // lax.axis_size(DOC)
    left_offset = lax.axis_index(DOC) * left_share
    left_raw, weight_sum = in_one((left_part, weight_part), DOC)
    row_weight = row_flat * weight_sum
    left_block = (
        row_flat[:, None] * left_raw - row_weight[:, None] * start_mean[None, :] / docs_total
    )
    gram_rows = lax.dynamic_slice_in_dim(left_block, left_offset, left_share, 0)
    weight_rows = lax.dynamic_slice_in_dim(row_weight, left_offset, left_share)
    gram_part = jnp.dot(gram_rows.T, gram_rows, precision=PRECISE) / terms_total
    lean_part = jnp.dot(weight_rows, gram_rows, precision=PRECISE)
    left_gram, lean_raw = packed_total(
        (gram_part, lean_part), (("term_0", "term_1", "doc_0"), "doc_1")
    )
    left_inverse = factor_inverse(left_gram)
    lean = jnp.dot(lean_raw, left_inverse, precision=PRECISE)
    left_basis = jnp.dot(left_block, left_inverse, precision=PRECISE).astype(jnp.bfloat16)
    scaled_left = (row_flat[:, None] * left_basis.astype(jnp.float32)).astype(jnp.bfloat16)
    right_part = tile_pass(
        col_matrix(scaled_left.reshape(RB, TILE, K)), jnp.zeros((CB, TILE, K), jnp.float32)
    )
    right_part = right_part.reshape(CB * TILE, K)
    right_share = CB * TILE // lax.axis_size(TERM)
    right_offset = lax.axis_index(TERM) * right_share
    right_raw = total_of(right_part, ("term_0", "term_1"))
    right_block = col_flat[:, None] * right_raw - lean[None, :] / docs_total
    right_rows = lax.dynamic_slice_in_dim(right_block, right_offset, right_share, 0)
    right_gram = total_of(
        jnp.dot(right_rows.T, right_rows, precision=PRECISE) / docs_total,
        (("term_0", "term_1", "doc_0"), "doc_1"),
    )
    right_inverse = factor_inverse(right_gram)
    right_basis = jnp.dot(right_block, right_inverse, precision=PRECISE).astype(jnp.bfloat16)
    return (row_flat, col_flat, left_basis, right_basis)


def solution(mesh):
    torus = Mesh(mesh.devices.reshape(8, 2, 4, 4), ("term_0", "term_1", "doc_0", "doc_1"))
    placed = (P(TERM, DOC, None), P(TERM, DOC), P(TERM, DOC), P(TERM, DOC), P(DOC, None))
    return jax.shard_map(
        per_device,
        mesh=torus,
        in_specs=placed,
        out_specs=(P(TERM), P(DOC), P(TERM, None), P(DOC, None)),
        check_vma=False,
    )
```

profile of v0, /device:TPU:1, one launch (start us, length us, event | category | flops | bytes accessed | tf_op | source)
XLA Modules:
  0.0 612.9 jit_solution(16486611712658080536)
XLA Ops:
  0.6 16.4 %while.95 = (s32[]{:T(128)}, f32[16,128]{1,0:T(8,128)S(1)}, s32[48]{0:T(128)}, bf16[48,128,128]{2,1,0:T(8,128)(2,1)}, s32[48]{0:T(128)}, /*index=5*/s32[]{:T(128...) while((s32[]{:T(128)}, f32[16,128]{1,0:T(8,128)S(1)}, s32[48]{0:T(128)}, ...), condition=%wide.region_2.4_spmd, body=%wide.region_0.3_spmd.sunk | while | flops 3153094 | bytes 603283 | solution.py:134
  17.0 9.8 %psum.42 = f32[16,128]{1,0:T(8,128)S(1)} all-reduce(f32[16,128]{1,0:T(8,128)S(1)} %get-tuple-element.861), channel_id=1, replica_groups=mesh['term_0'=8,'term_1'=2,'doc_0'=4,'doc_1'=4] {'doc_0'}, use_global_device_ids=true, to_apply=%region_3.0 | all-reduce | flops 2048 | bytes 16384 | tf_op jit(solution)/shard_map/psum | solution.py:23
  26.8 8.9 %psum.43 = f32[16,128]{1,0:T(8,128)S(1)} all-reduce(f32[16,128]{1,0:T(8,128)S(1)} %psum.42), channel_id=1, replica_groups=mesh['term_0'=8,'term_1'=2,'doc_0'=4,'doc_1'=4] {'doc_1'}, use_global_device_ids=true, to_apply=%region_4.6 | all-reduce | flops 2048 | bytes 16384 | tf_op jit(solution)/shard_map/psum | solution.py:23
  35.8 15.1 %while.96 = (s32[]{:T(128)}, f32[16,128]{1,0:T(8,128)S(1)}, s32[48]{0:T(128)}, bf16[48,128,128]{2,1,0:T(8,128)(2,1)}, s32[48]{0:T(128)}, /*index=5*/f32[16,128]{...) while((s32[]{:T(128)}, f32[16,128]{1,0:T(8,128)S(1)}, s32[48]{0:T(128)}, ...), condition=%wide.region_7.9_spmd, body=%wide.region_5.0_spmd.sunk | while | flops 3153094 | bytes 595087 | solution.py:134
  51.6 12.8 %all-to-all-start = ((f32[16,16,128]{2,1,0:T(8,128)}), f32[16,16,128]{2,1,0:T(8,128)S(1)}, u32[]{:S(2)}, u32[]{:S(2)}) async-start(f32[16,16,128]{2,1,0:T(8,128)} %broadcast_in_dim.119), calls=%async_computation | async-start | bytes 262144 | tf_op jit(solution)/shard_map/all_to_all | solution.py:29
  64.7 8.9 %all-to-all-done = f32[16,16,128]{2,1,0:T(8,128)S(1)} async-done(((f32[16,16,128]{2,1,0:T(8,128)}), f32[16,16,128]{2,1,0:T(8,128)S(1)}, u32[]{:S(2)}, u32[]{:S(2)}) %all-to-all-start) | async-done | bytes 131104 | tf_op jit(solution)/shard_map/all_to_all | solution.py:29
  73.7 16.3 %while.97 = (s32[]{:T(128)}, f32[16,128]{1,0:T(8,128)S(1)}, s32[48]{0:T(128)}, bf16[48,128,128]{2,1,0:T(8,128)(2,1)}, s32[48]{0:T(128)}, /*index=5*/f32[16,128]{...) while((s32[]{:T(128)}, f32[16,128]{1,0:T(8,128)S(1)}, s32[48]{0:T(128)}, ...), condition=%wide.region_11.13_spmd, body=%wide.region_9.12_spmd.sunk | while | flops 3153094 | bytes 595087 | solution.py:134
  90.0 6.4 %all-reduce.2 = (f32[16,128]{1,0:T(8,128)S(1)}, f32[256]{0:T(256)S(1)}) all-reduce(f32[16,128]{1,0:T(8,128)S(1)} %get-tuple-element.863, f32[256]{0:T(256)S(1)} %convert_reduce_fusion), channel_id=1, replica_groups=mesh['term_0'=8,'term_1'=2,'doc_0'=4,'doc_1'=4] {'doc_0'}, use_global_device_ids=true, to_apply=%region_12.14 | all-reduce | flops 2304 | bytes 18432 | tf_op jit(solution)/shard_map/psum | solution.py:23
  96.4 6.2 %all-reduce.1 = (f32[16,128]{1,0:T(8,128)S(1)}, f32[256]{0:T(256)S(1)}) all-reduce(f32[16,128]{1,0:T(8,128)S(1)} %get-tuple-element.1040, f32[256]{0:T(256)S(1)} %get-tuple-element.1041), channel_id=1, replica_groups=mesh['term_0'=8,'term_1'=2,'doc_0'=4,'doc_1'=4] {'doc_1'}, use_global_device_ids=true, to_apply=%region_13.15 | all-reduce | flops 2304 | bytes 18432 | tf_op jit(solution)/shard_map/psum | solution.py:23
  102.7 15.1 %while.98 = (s32[]{:T(128)}, f32[16,128]{1,0:T(8,128)S(1)}, s32[48]{0:T(128)}, bf16[48,128,128]{2,1,0:T(8,128)(2,1)}, s32[48]{0:T(128)}, /*index=5*/f32[16,128]{...) while((s32[]{:T(128)}, f32[16,128]{1,0:T(8,128)S(1)}, s32[48]{0:T(128)}, ...), condition=%wide.region_16.18_spmd, body=%wide.region_14.17_spmd.sunk | while | flops 3153094 | bytes 595087 | solution.py:134
  118.5 6.3 %all-to-all-start.1 = ((f32[16,16,128]{2,1,0:T(8,128)}), f32[16,16,128]{2,1,0:T(8,128)S(1)}, u32[]{:S(2)}, u32[]{:S(2)}) async-start(f32[16,16,128]{2,1,0:T(8,128)} %broadcast_in_dim.120), calls=%async_computation.1 | async-start | bytes 262144 | tf_op jit(solution)/shard_map/all_to_all | solution.py:29
  124.8 9.2 %all-to-all-done.1 = f32[16,16,128]{2,1,0:T(8,128)S(1)} async-done(((f32[16,16,128]{2,1,0:T(8,128)}), f32[16,16,128]{2,1,0:T(8,128)S(1)}, u32[]{:S(2)}, u32[]{:S(2)}) %all-to-all-start.1) | async-done | bytes 131104 | tf_op jit(solution)/shard_map/all_to_all | solution.py:29
  136.9 29.2 %while.99 = (s32[]{:T(128)}, f32[16,128,256]{2,1,0:T(8,128)}, s32[48]{0:T(128)S(1)}, bf16[48,128,128]{2,1,0:T(8,128)(2,1)S(1)}, s32[48]{0:T(128)S(1)}, /*index=5...) while((s32[]{:T(128)}, f32[16,128,256]{2,1,0:T(8,128)}, ...), condition=%wide.region_20.0_spmd, body=%wide.region_18.0_spmd.sunk | while | flops 135791808 | bytes 12064447 | solution.py:134
  141.5 5.3 scatter_fusion
  151.3 5.1 scatter_fusion
  160.9 5.2 scatter_fusion
  166.1 4.0 copy.73
  170.1 9.3 %while.100 = (s32[]{:T(128)}, f32[16,128]{1,0:T(8,128)S(1)}, s32[48]{0:T(128)S(1)}, bf16[48,128,128]{2,1,0:T(8,128)(2,1)S(1)}, s32[48]{0:T(128)S(1)}, /*index=5*...) while((s32[]{:T(128)}, f32[16,128]{1,0:T(8,128)S(1)}, ...), condition=%wide.region_23.26_spmd, body=%wide.region_21.25_spmd.sunk | while | flops 3153094 | bytes 595087 | solution.py:134
  181.1 33.7 %all_to_all.99 = f32[16,1,32896]{2,1,0:T(1,128)} all-to-all(f32[16,1,32896]{2,1,0:T(1,128)S(1)} %bitcast.179), channel_id=1, replica_groups=mesh['term_0'=8,'term_1'=2,'doc_0'=4,'doc_1'=4] {'doc_0','doc_1'}, dimensions={0} | all-to-all | bytes 4210688 | tf_op jit(solution)/shard_map/all_to_all | solution.py:43
  220.1 4.6 all-to-all-start.3
  224.7 31.9 %all-to-all-done.3 = f32[16,1,32896]{2,1,0:T(1,128)} async-done(((f32[16,1,32896]{2,1,0:T(1,128)}), f32[16,1,32896]{2,1,0:T(1,128)}, u32[]{:S(2)}, u32[]{:S(2)}) %all-to-all-start.3) | async-done | bytes 2105376 | tf_op jit(solution)/shard_map/all_to_all | solution.py:29
  256.6 7.9 %reduce.12 = f32[16,32896]{1,0:T(8,128)} reduce(f32[16,1,32896]{2,1,0:T(1,128)} %all-to-all-done.3, f32[]{:T(128)} %constant.362), dimensions={1}, to_apply=%all_to_all.64.reduce_sub_computation | reduce | bytes 4210692 | tf_op jit(solution)/shard_map/all_to_all | solution.py:29
  272.9 8.7 %all_to_all.100 = f32[4,64,257]{2,1,0:T(8,128)S(1)} all-to-all(f32[4,64,257]{2,1,0:T(8,128)S(1)} %copy.47), channel_id=1, replica_groups=mesh['term_0'=8,'term_1'=2,'doc_0'=4,'doc_1'=4] {'doc_1'}, dimensions={0} | all-to-all | bytes 526336 | tf_op jit(solution)/shard_map/all_to_all | solution.py:43
  281.7 15.6 %all_to_all.101 = f32[64,1,257]{2,1,0:T(1,128)S(1)} all-to-all(f32[64,1,257]{2,1,0:T(1,128)S(1)} %all_to_all.66), channel_id=1, replica_groups=mesh['term_0'=8,'term_1'=2,'doc_0'=4,'doc_1'=4] {'term_0','term_1','doc_0'}, dimensions={0} | all-to-all | bytes 131584 | tf_op jit(solution)/shard_map/all_to_all | solution.py:82
  298.1 5.7 all-to-all-start.6
  303.9 9.5 %all-to-all-done.6 = f32[64,1,257]{2,1,0:T(1,128)S(1)} async-done(((f32[64,1,257]{2,1,0:T(1,128)}), f32[64,1,257]{2,1,0:T(1,128)S(1)}, u32[]{:S(2)}, u32[]{:S(2)}) %all-to-all-start.6) | async-done | bytes 65824 | tf_op jit(solution)/shard_map/all_to_all | solution.py:29
  318.1 6.1 %all-to-all-done.7 = f32[4,64,257]{2,1,0:T(8,128)S(1)} async-done(((f32[4,64,257]{2,1,0:T(8,128)}), f32[4,64,257]{2,1,0:T(8,128)S(1)}, u32[]{:S(2)}, u32[]{:S(2)}) %all-to-all-start.7) | async-done | bytes 263200 | tf_op jit(solution)/shard_map/all_to_all | solution.py:29
  325.3 11.7 %cholesky.130 = f32[128,128]{1,0:T(8,128)S(1)} custom-call(f32[128,128]{1,0:T(8,128)S(1)} %cholesky.194), custom_call_target="Cholesky" | custom-call | tf_op jit(solution)/shard_map/jit(cholesky)/cholesky | solution.py:114
  337.1 9.8 %custom-call.13 = f32[1,128,128]{1,2,0:T(8,128)S(1)} custom-call(f32[1,128,128]{2,1,0:T(8,128)S(1)} %get-tuple-element.1076), custom_call_target="InvertDiagBlocksLowerTriangular" | custom-call | tf_op jit(solution)/shard_map/jit(cholesky)/cholesky | solution.py:114
  347.4 11.7 %cholesky.147 = f32[128,128]{1,0:T(8,128)S(1)} custom-call(f32[128,128]{1,0:T(8,128)S(1)} %convolution_subtract_fusion.3), custom_call_target="Cholesky" | custom-call | tf_op jit(solution)/shard_map/jit(cholesky)/cholesky | solution.py:114
  365.5 19.8 %custom-call.14 = f32[2,128,128]{1,2,0:T(8,128)S(1)} custom-call(f32[2,128,128]{2,1,0:T(8,128)S(1)} %get-tuple-element.882), custom_call_target="InvertDiagBlocksLowerTriangular" | custom-call | tf_op jit(solution)/shard_map/jit(_solve_triangular)/triangular_solve | solution.py:116
  386.3 4.8 multiply_convert_fusion
  392.7 29.2 %while.101 = (s32[]{:T(128)}, f32[16,128,256]{2,1,0:T(8,128)}, s32[48]{0:T(128)S(1)}, bf16[48,128,128]{2,1,0:T(8,128)(2,1)S(1)}, s32[48]{0:T(128)S(1)}, /*index=...) while((s32[]{:T(128)}, f32[16,128,256]{2,1,0:T(8,128)}, ...), condition=%wide.region_36.41_spmd, body=%wide.region_34.0_spmd.sunk | while | flops 135791808 | bytes 12064447 | solution.py:134
  397.2 5.4 scatter_fusion.1
  407.0 5.2 scatter_fusion.1
  416.7 5.1 scatter_fusion.1
  423.6 7.8 %all_to_all.96 = f32[2,8,128,256]{3,2,1,0:T(8,128)S(1)} all-to-all(f32[2,8,128,256]{3,2,1,0:T(8,128)S(1)} %copy.52), channel_id=1, replica_groups=mesh['term_0'=8,'term_1'=2,'doc_0'=4,'doc_1'=4] {'term_1'}, dimensions={0} | all-to-all | bytes 4194304 | tf_op jit(solution)/shard_map/all_to_all | solution.py:43
  431.7 30.8 %all_to_all.102 = f32[8,128,256]{2,1,0:T(8,128)S(1)} all-to-all(f32[8,128,256]{2,1,0:T(8,128)S(1)} %reduce_sum.98), channel_id=1, replica_groups=mesh['term_0'=8,'term_1'=2,'doc_0'=4,'doc_1'=4] {'term_0'}, dimensions={0} | all-to-all | bytes 2097152 | tf_op jit(solution)/shard_map/all_to_all | solution.py:82
  467.9 28.3 %all-to-all-done.10 = f32[8,128,256]{2,1,0:T(8,128)S(1)} async-done(((f32[8,128,256]{2,1,0:T(8,128)}), f32[8,128,256]{2,1,0:T(8,128)S(1)}, u32[]{:S(2)}, u32[]{:S(2)}) %all-to-all-start.10) | async-done | bytes 1048608 | tf_op jit(solution)/shard_map/all_to_all | solution.py:29
  496.4 5.5 all_to_all.97
  503.1 8.8 %all_to_all.103 = f32[4,64,1,256]{3,1,2,0:T(8,128)S(1)} all-to-all(f32[4,64,1,256]{3,1,2,0:T(8,128)S(1)} %bitcast.184), channel_id=1, replica_groups=mesh['term_0'=8,'term_1'=2,'doc_0'=4,'doc_1'=4] {'doc_1'}, dimensions={0} | all-to-all | bytes 524288 | tf_op jit(solution)/shard_map/all_to_all | solution.py:43
  512.0 13.9 %all_to_all.104 = f32[64,1,256]{2,1,0:T(1,128)S(1)} all-to-all(f32[64,1,256]{2,1,0:T(1,128)S(1)} %reduce_sum.101), channel_id=1, replica_groups=mesh['term_0'=8,'term_1'=2,'doc_0'=4,'doc_1'=4] {'term_0','term_1','doc_0'}, dimensions={0} | all-to-all | bytes 131072 | tf_op jit(solution)/shard_map/all_to_all | solution.py:82
  526.0 13.9 %all_to_all.98 = f32[64,1,256]{2,1,0:T(1,128)S(1)} all-to-all(f32[64,1,256]{2,1,0:T(1,128)S(1)} %broadcast_in_dim.126), channel_id=1, replica_groups=mesh['term_0'=8,'term_1'=2,'doc_0'=4,'doc_1'=4] {'term_0','term_1','doc_0'}, dimensions={0} | all-to-all | bytes 131072 | tf_op jit(solution)/shard_map/all_to_all | solution.py:29
  539.9 8.1 %all_to_all.105 = f32[4,64,1,256]{3,1,2,0:T(8,128)S(1)} all-to-all(f32[4,64,1,256]{3,1,2,0:T(8,128)S(1)} %broadcast_in_dim.127), channel_id=1, replica_groups=mesh['term_0'=8,'term_1'=2,'doc_0'=4,'doc_1'=4] {'doc_1'}, dimensions={0} | all-to-all | bytes 524288 | tf_op jit(solution)/shard_map/all_to_all | solution.py:29
  548.5 11.7 %cholesky.164 = f32[128,128]{1,0:T(8,128)S(1)} custom-call(f32[128,128]{1,0:T(8,128)S(1)} %cholesky.197), custom_call_target="Cholesky" | custom-call | tf_op jit(solution)/shard_map/jit(cholesky)/cholesky | solution.py:114
  560.3 9.8 %custom-call.15 = f32[1,128,128]{1,2,0:T(8,128)S(1)} custom-call(f32[1,128,128]{2,1,0:T(8,128)S(1)} %get-tuple-element.1072), custom_call_target="InvertDiagBlocksLowerTriangular" | custom-call | tf_op jit(solution)/shard_map/jit(cholesky)/cholesky | solution.py:114
  570.6 11.7 %cholesky.181 = f32[128,128]{1,0:T(8,128)S(1)} custom-call(f32[128,128]{1,0:T(8,128)S(1)} %convolution_subtract_fusion.2), custom_call_target="Cholesky" | custom-call | tf_op jit(solution)/shard_map/jit(cholesky)/cholesky | solution.py:114
  588.8 19.9 %custom-call.16 = f32[2,128,128]{1,2,0:T(8,128)S(1)} custom-call(f32[2,128,128]{2,1,0:T(8,128)S(1)} %get-tuple-element.883), custom_call_target="InvertDiagBlocksLowerTriangular" | custom-call | tf_op jit(solution)/shard_map/jit(_solve_triangular)/triangular_solve | solution.py:116
  (277 shorter events, 159.7 us)
Async XLA Ops:
  17.0 47.4 %copy-start.2 = (bf16[2048,256]{1,0:T(8,128)(2,1)S(1)}, bf16[2048,256]{1,0:T(8,128)(2,1)}, u32[]{:S(2)}) copy-start(bf16[2048,256]{1,0:T(8,128)(2,1)} %param.30) | copy-start | bytes 3145732
  51.6 22.0 %all-to-all-start = ((f32[16,16,128]{2,1,0:T(8,128)}), f32[16,16,128]{2,1,0:T(8,128)S(1)}, u32[]{:S(2)}, u32[]{:S(2)}) async-start(f32[16,16,128]{2,1,0:T(8,128)} %broadcast_in_dim.119), calls=%async_computation | async-start | bytes 262144 | tf_op jit(solution)/shard_map/all_to_all | solution.py:29
  118.5 15.5 %all-to-all-start.1 = ((f32[16,16,128]{2,1,0:T(8,128)}), f32[16,16,128]{2,1,0:T(8,128)S(1)}, u32[]{:S(2)}, u32[]{:S(2)}) async-start(f32[16,16,128]{2,1,0:T(8,128)} %broadcast_in_dim.120), calls=%async_computation.1 | async-start | bytes 262144 | tf_op jit(solution)/shard_map/all_to_all | solution.py:29
  134.0 368.1 %copy-start.11 = (f32[2048]{0:T(1024)}, f32[2048]{0:T(1024)S(1)}, u32[]{:S(2)}) copy-start(f32[2048]{0:T(1024)S(1)} %get-tuple-element.1077) | copy-start | bytes 24580
  134.0 2.9 copy-start
  134.1 2.9 copy-start.9
  134.1 2.8 copy-start.10
  220.1 36.5 %all-to-all-start.3 = ((f32[16,1,32896]{2,1,0:T(1,128)}), f32[16,1,32896]{2,1,0:T(1,128)}, u32[]{:S(2)}, u32[]{:S(2)}) async-start(f32[16,1,32896]{2,1,0:T(1,128)} %broadcast_in_dim.121), calls=%async_computation.3 | async-start | bytes 4210688 | tf_op jit(solution)/shard_map/all_to_all | solution.py:29
  268.7 117.6 %copy-start.12 = (f32[2048]{0:T(1024)}, f32[2048]{0:T(1024)S(1)}, u32[]{:S(2)}) copy-start(f32[2048]{0:T(1024)S(1)} %get-tuple-element.1057) | copy-start | bytes 24580
  270.6 1.4 copy-start.1
  298.1 15.3 %all-to-all-start.6 = ((f32[64,1,257]{2,1,0:T(1,128)}), f32[64,1,257]{2,1,0:T(1,128)S(1)}, u32[]{:S(2)}, u32[]{:S(2)}) async-start(f32[64,1,257]{2,1,0:T(1,128)} %broadcast_in_dim.122), calls=%async_computation.6 | async-start | bytes 196608 | tf_op jit(solution)/shard_map/all_to_all | solution.py:29
  314.2 10.1 %all-to-all-start.7 = ((f32[4,64,257]{2,1,0:T(8,128)}), f32[4,64,257]{2,1,0:T(8,128)S(1)}, u32[]{:S(2)}, u32[]{:S(2)}) async-start(f32[4,64,257]{2,1,0:T(8,128)} %broadcast_in_dim.123), calls=%async_computation.7 | async-start | bytes 786432 | tf_op jit(solution)/shard_map/all_to_all | solution.py:29
  318.1 67.6 %copy-start.3 = (f32[256,256]{1,0:T(8,128)}, f32[256,256]{1,0:T(8,128)S(1)}, u32[]{:S(2)}) copy-start(f32[256,256]{1,0:T(8,128)S(1)} %fusion.53) | copy-start | bytes 786436
  365.0 0.6 copy-start.13
  385.7 5.4 copy-start.5
  386.3 4.8 copy-start.7
  462.5 5.1 copy-start.6
  462.5 5.1 copy-start.8
  463.6 32.7 %all-to-all-start.10 = ((f32[8,128,256]{2,1,0:T(8,128)}), f32[8,128,256]{2,1,0:T(8,128)S(1)}, u32[]{:S(2)}, u32[]{:S(2)}) async-start(f32[8,128,256]{2,1,0:T(8,128)} %broadcast_in_dim.124), calls=%async_computation.10 | async-start | bytes 2097152 | tf_op jit(solution)/shard_map/all_to_all | solution.py:29
  548.1 36.9 %copy-start.14 = (s32[2,2]{1,0:T(2,128)S(1)}, s32[2,2]{1,0:T(2,128)}, u32[]{:S(2)}) copy-start(s32[2,2]{1,0:T(2,128)} %copy-done.13) | copy-start | bytes 52
  548.3 60.4 %copy-start.4 = (f32[256,256]{1,0:T(8,128)S(1)}, f32[256,256]{1,0:T(8,128)}, u32[]{:S(2)}) copy-start(f32[256,256]{1,0:T(8,128)} %copy-done.3) | copy-start | bytes 786436
where the time goes:
time: 623 us; the launch traced here: 613 us
  other arithmetic  202 us (32%)
  blocking collectives  178 us (29%)
  waiting for transfers between devices  94 us (15%)
  local copies, waits for them, and re-layouts  50.5 us (8%)
  matrix products  46.4 us (7%)
  starting transfers between devices  36.9 us (6%)
    all_to_all x6, waiting for transfers between devices, sent_to_all(): return lax.all_to_all(copies, axis, split_axis=0, concat_axis=0, tiled=True)  94 us
    another operation x13, other arithmetic, factor_inverse(): lower = jnp.linalg.cholesky(gram)  68.5 us
    all_to_all x3, blocking collectives, summed_rows(): lax.all_to_all(nearer, far, split_axis=0, concat_axis=0, tiled=True)  60.3 us
    all_to_all x4, blocking collectives, summed_on_arrival(): lax.all_to_all(pieces, axis, split_axis=0, concat_axis=0, tiled=True)  59 us
    another operation x5, other arithmetic, factor_inverse(): return jax.scipy.linalg.solve_triangular(lower, identity, lower=True).T  39.8 us
    all_to_all x6, starting transfers between devices, sent_to_all(): return lax.all_to_all(copies, axis, split_axis=0, concat_axis=0, tiled=True)  36.9 us
    psum x4, blocking collectives, by_axis(): shard = lax.psum(shard, axis)  31.4 us
    all_to_all x3, blocking collectives, sent_to_all(): return lax.all_to_all(copies, axis, split_axis=0, concat_axis=0, tiled=True)  27.5 us
  transfers between devices with their start and end apart: 6, of which 6 were waited for; matrix products, arithmetic and copies ran while one was open for 0% of the time, Pallas kernels for 0%

commit v1 on v0

v1 whole, which is shorter than its diff:
```python
import jax
import jax.numpy as jnp
from jax import lax
from jax.experimental import pallas as pl
from jax.experimental.pallas import tpu as pltpu
from jax.sharding import Mesh
from jax.sharding import PartitionSpec as P

TILE = 128
K = 256
RB = 16
CB = 16
CAP = 48
GROUP = 8
PANEL = 64
TERM = ("term_0", "term_1")
DOC = ("doc_0", "doc_1")
ALL = TERM + DOC
F32 = jnp.float32
BF16 = jnp.bfloat16
PRECISE = lax.Precision.HIGHEST
VMEM = pl.BlockSpec(memory_space=pltpu.VMEM)
SMEM = pl.BlockSpec(memory_space=pltpu.SMEM)


def call(body, inputs, outs, scratch=(), flops=1 << 20):
    specs = [SMEM if a.dtype == jnp.int32 else VMEM for a in inputs]
    return pl.pallas_call(
        body,
        out_shape=[jax.ShapeDtypeStruct(s, d) for s, d in outs],
        in_specs=specs,
        out_specs=[VMEM] * len(outs),
        scratch_shapes=[pltpu.VMEM(s, d) for s, d in scratch],
        compiler_params=pltpu.CompilerParams(vmem_limit_bytes=48 * 1024 * 1024),
    )(*inputs)


def thirds(x):
    hi = x.astype(BF16)
    rest = x - hi.astype(F32)
    mid = rest.astype(BF16)
    low = (rest - mid.astype(F32)).astype(BF16)
    return hi, mid, low


def put_thirds(ref, vec, base):
    hi, mid, low = thirds(vec)
    row = lax.broadcasted_iota(jnp.int32, (16, TILE), 0)
    for b in range(RB):
        parts = [jnp.broadcast_to(p[b : b + 1].astype(F32), (16, TILE)) for p in (hi, mid, low)]
        rows = jnp.where(row == 0, parts[0], jnp.where(row == 1, parts[1], jnp.where(row == 2, parts[2], 0.0)))
        ref[b, base : base + 16, :] = rows.astype(BF16)


def over_tiles(count, values, source, target, src_ref, acc_ref, transposed):
    acc_ref[...] = jnp.zeros(acc_ref.shape, F32)
    dims = (((1,), (1,)), ((), ())) if transposed else (((1,), (0,)), ((), ()))

    def visit(g, _):
        products = []
        for u in range(GROUP):
            s = g * GROUP + u
            tile = values[s]
            tile = jnp.where(s < count, tile, jnp.zeros_like(tile))
            products.append(
                lax.dot_general(src_ref[source[0, s]], tile, dims, preferred_element_type=F32)
            )
        for u in range(GROUP):
            s = g * GROUP + u
            acc_ref[target[0, s]] += products[u]
        return 0

    lax.fori_loop(0, (count + GROUP - 1) // GROUP, visit, 0)


def send_vector(out_ref, acc_ref):
    vec = jnp.sum(acc_ref[...], axis=1)
    for i in range(16):
        out_ref[i, 0:RB, :] = vec


def start_sums(values, rows, cols, count, start, out, src, acc):
    put_thirds(src, jnp.ones((CB, TILE), F32), 0)
    over_tiles(count[0, 0], values, cols, rows, src, acc, True)
    send_vector(out, acc)
    mean = jnp.sum(start[...].astype(F32), axis=0, keepdims=True)
    for i in range(16):
        out[i, 16:17, :] = mean[:, :TILE]
        out[i, 17:18, :] = mean[:, TILE:]
        out[i, 18:24, :] = jnp.zeros((6, TILE), F32)


def to_columns(values, rows, cols, count, got, out, scale, src, acc):
    vec = 1.0 / jnp.sum(got[...], axis=0)[0:RB]
    scale[...] = vec
    put_thirds(src, vec, 0)
    over_tiles(count[0, 0], values, rows, cols, src, acc, False)
    send_vector(out, acc)


def to_rows(values, rows, cols, count, got, out, scale, src, acc):
    vec = 1.0 / jnp.sum(got[...], axis=0)[0:RB]
    scale[...] = vec
    put_thirds(src, vec, 0)
    over_tiles(count[0, 0], values, cols, rows, src, acc, True)
    send_vector(out, acc)


def left_product(docs, values, rows, cols, count, got, first, start, out, scale, src, acc):
    vec = 1.0 / jnp.sum(got[...], axis=0)
    scale[...] = vec
    put_thirds(src, vec, K)
    for b in range(CB):
        block = start[b * TILE : (b + 1) * TILE, :].astype(F32).T
        src[b, 0:K, :] = (block * vec[b : b + 1, :]).astype(BF16)
    mean = jnp.sum(first[...], axis=0)[16:18] / docs
    mean = jnp.concatenate([jnp.broadcast_to(mean[h : h + 1], (TILE, TILE)).T for h in range(2)], axis=0)
    over_tiles(count[0, 0], values, cols, rows, src, acc, True)
    for b in range(RB):
        weight = jnp.sum(acc[b, K : K + 16, :], axis=0, keepdims=True)
        out[b] = (acc[b, 0:K, :] - mean * weight).astype(out.dtype)


def left_rows(place, got, row_scale, out, gram):
    d = place[0, 1]
    scale = row_scale[pl.ds(d, 1), :]
    left = scale * jnp.sum(got[...].astype(F32), axis=0)
    sent = (left * scale).astype(BF16)
    for i in range(16):
        out[i] = sent
    gram[...] = lax.dot_general(left, left, (((1,), (1,)), ((), ())), precision=PRECISE, preferred_element_type=F32)


def right_product(values, rows, cols, count, scaled, out, acc):
    over_tiles(count[0, 0], values, rows, cols, scaled, acc, False)
    for b in range(CB):
        out[b] = acc[b].astype(out.dtype)


def iotas(shape=(K, K)):
    return lax.broadcasted_iota(jnp.int32, shape, 0), lax.broadcasted_iota(jnp.int32, shape, 1)


def right_rows(place, got, col_scale, left_gram, out, block):
    t = place[0, 0]
    scale = col_scale[pl.ds(t, 1), :]
    right = scale * jnp.sum(got[...].astype(F32), axis=0)
    block[...] = right
    gram = lax.dot_general(right, right, (((1,), (1,)), ((), ())), precision=PRECISE, preferred_element_type=F32)
    row, col = iotas()
    packed = jnp.where(row >= col, left_gram[...], gram)
    diag = jnp.sum(jnp.where(row == col, gram, 0.0), axis=1, keepdims=True)
    lean = jnp.sum(right, axis=1, keepdims=True)
    lane = lax.broadcasted_iota(jnp.int32, (K, TILE), 1)
    extra = jnp.where(lane == 0, diag, jnp.where(lane == 1, lean, 0.0))
    out[...] = jnp.concatenate([packed, extra], axis=1)


def sum_all(got, out):
    total = jnp.sum(got[...], axis=0, keepdims=True)
    out[...] = jnp.broadcast_to(total, out.shape)


def eliminate(work, start, which):
    first = (start // TILE) * TILE
    width = 3 * TILE
    sub = lax.broadcasted_iota(jnp.int32, (PANEL, 1), 0)
    lane = lax.broadcasted_iota(jnp.int32, (PANEL, TILE), 1)
    lane1 = lax.broadcasted_iota(jnp.int32, (1, TILE), 1)
    step = 4

    def group(g, _):
        base = g * step
        offset = start - first + base
        for m in which:
            panel = work[m, start : start + PANEL, first : first + width]
            head = panel[:, 0:TILE]
            cols = [jnp.sum(jnp.where(lane == offset + a, head, 0.0), axis=1, keepdims=True) for a in range(step)]
            lines = [work[m, pl.ds(start + base + a, 1), first : first + width] for a in range(step)]
            heads = [
                [
                    jnp.sum(jnp.where(lane1 == offset + b, lines[a][:, 0:TILE], 0.0), axis=1, keepdims=True)
                    for b in range(step)
                ]
                for a in range(step)
            ]
            factors = []
            for a in range(step):
                inv = 1.0 / heads[a][a]
                f = jnp.where(sub > base + a, cols[a] * inv, 0.0)
                factors.append(f)
                for b in range(a + 1, step):
                    cols[b] = cols[b] - f * heads[a][b]
                    ratio = heads[b][a] * inv
                    lines[b] = lines[b] - ratio * lines[a]
                    for c in range(a + 1, step):
                        heads[b][c] = heads[b][c] - ratio * heads[a][c]
            for a in range(step):
                panel = panel - factors[a] * lines[a]
            work[m, start : start + PANEL, first : first + width] = panel
        return 0

    lax.fori_loop(0, PANEL // step, group, 0)


def factor(work, which):
    for start in range(0, K, PANEL):
        first = (start // TILE) * TILE
        width = 3 * TILE
        end = start + PANEL
        eliminate(work, start, which)
        for m in which:
            panel = work[m, start:end, first : first + width]
            at = lax.broadcasted_iota(jnp.int32, (PANEL, TILE), 0) + (start - first)
            lane = lax.broadcasted_iota(jnp.int32, (PANEL, TILE), 1)
            pivot = jnp.sum(jnp.where(at == lane, panel[:, 0:TILE], 0.0), axis=1, keepdims=True)
            panel = panel * lax.rsqrt(pivot)
            work[m, start:end, first : first + width] = panel
            if end < K:
                upper = panel[:, end - first : K - first]
                work[m, end:K, first : first + width] -= lax.dot_general(
                    upper, panel, (((0,), (0,)), ((), ())), precision=PRECISE, preferred_element_type=F32
                )


def finish(terms, docs, packed, extra, block, left_inverse, out, work):
    row, col = iotas()
    one = packed[...]
    other = one.T
    e = extra[...]
    lean = e[:, 1:2] / docs
    lean_row = jnp.sum(jnp.where(row == col, lean, 0.0), axis=0, keepdims=True)
    left = jnp.where(row >= col, one, other) / terms
    right = jnp.where(row < col, one, jnp.where(row == col, e[:, 0:1], other)) / docs - lean * lean_row
    eye = jnp.where(row == col, 1.0, 0.0).astype(F32)
    for m, gram in ((0, left), (1, right)):
        work[m, :, 0:K] = gram
        work[m, :, K : 2 * K] = eye
    factor(work, (0, 1))
    inverse = [jnp.where(row >= col, work[m, :, K : 2 * K], 0.0) for m in range(2)]
    left_inverse[...] = inverse[0]
    centred = block[...] - lean
    basis = lax.dot_general(inverse[1], centred, (((1,), (0,)), ((), ())), precision=PRECISE, preferred_element_type=F32)
    basis = basis.T.astype(BF16)
    for i in range(16):
        out[i] = basis


def left_basis_of(inverse, scaled, row_scale, out):
    hi, mid, low = thirds(inverse[...])
    for b in range(RB):
        total = (
            jnp.dot(hi, scaled[b], preferred_element_type=F32)
            + jnp.dot(mid, scaled[b], preferred_element_type=F32)
            + jnp.dot(low, scaled[b], preferred_element_type=F32)
        )
        basis = total / row_scale[b : b + 1, :]
        out[b * TILE : (b + 1) * TILE, :] = basis.T.astype(BF16)


def exchanged(x, axis):
    return lax.all_to_all(x, axis, split_axis=0, concat_axis=0, tiled=True)


WIRE1 = BF16
WIRE2 = F32


def per_device(tile_values, tile_rows, tile_cols, tile_count, start_block):
    terms = float(RB * TILE * lax.axis_size(TERM))
    docs = float(CB * TILE * lax.axis_size(DOC))
    place = jnp.stack([lax.axis_index(TERM), lax.axis_index(DOC)]).astype(jnp.int32)[None]
    tiles = (tile_values, tile_rows, tile_cols, tile_count)
    vec = [((RB, 16, TILE), BF16), ((RB, 16, TILE), F32)]
    vector = ((16, RB, TILE), F32)
    scale = ((RB, TILE), F32)
    (part,) = call(start_sums, (*tiles, start_block), [((16, 24, TILE), F32)], vec)
    first = exchanged(part, DOC)
    part, _ = call(to_columns, (*tiles, first), [vector, scale], vec)
    part, _ = call(to_rows, (*tiles, exchanged(part, TERM)), [vector, scale], vec)
    part, row_scale = call(to_columns, (*tiles, exchanged(part, DOC)), [vector, scale], vec)
    part, col_scale = call(
        lambda *refs: left_product(docs, *refs),
        (*tiles, exchanged(part, TERM), first, start_block),
        [((RB, K, TILE), WIRE1), scale],
        [((CB, K + 16, TILE), BF16), ((RB, K + 16, TILE), F32)],
    )
    part, left_gram = call(
        left_rows, (place, exchanged(part, DOC), row_scale), [((16, K, TILE), BF16), ((K, K), F32)]
    )
    scaled = exchanged(part, DOC)
    (part,) = call(right_product, (*tiles, scaled), [((CB, K, TILE), WIRE2)], [((CB, K, TILE), F32)])
    part, block = call(
        right_rows,
        (place, exchanged(part, TERM), col_scale, left_gram),
        [((K, 3 * TILE), F32), ((K, TILE), F32)],
    )
    part = exchanged(part.reshape(K, 3, TILE), ALL)
    (part,) = call(sum_all, (part,), [((K, 3, TILE), F32)])
    grams = exchanged(part, ALL)
    packed = grams[:, 0:2].reshape(K, K)
    extra = grams[:, 2]
    left_inverse, part = call(
        lambda *refs: finish(terms, docs, *refs),
        (packed, extra, block),
        [((K, K), F32), ((16, TILE, K), BF16)],
        [((2, K, 2 * K), F32)],
    )
    right_basis = exchanged(part, TERM).reshape(CB * TILE, K)
    (left_basis,) = call(left_basis_of, (left_inverse, scaled, row_scale), [((RB * TILE, K), BF16)])
    return (row_scale.reshape(-1), col_scale.reshape(-1), left_basis, right_basis)


def solution(mesh):
    torus = Mesh(mesh.devices.reshape(8, 2, 4, 4), ("term_0", "term_1", "doc_0", "doc_1"))
    placed = (P(TERM, DOC, None), P(TERM, DOC), P(TERM, DOC), P(TERM, DOC), P(DOC, None))
    return jax.shard_map(
        per_device,
        mesh=torus,
        in_specs=placed,
        out_specs=(P(TERM), P(DOC), P(TERM, None), P(DOC, None)),
        check_vma=False,
    )
```

time: 623 us -> 286 us (0.46); the launches traced: 613 us -> 285 us
  other arithmetic: 202 us -> 0.08 us
  waiting for transfers between devices: 94 us -> 44.4 us
  matrix products: 46.4 us -> 0 us
  local copies, waits for them, and re-layouts: 50.5 us -> 5.82 us
  Pallas kernels: 0 us -> 41.9 us
  starting transfers between devices: 36.9 us -> 8.04 us
    another operation x18 -> x0, other arithmetic: 108 us -> none  [the longest x13 68.5 us: factor_inverse(): lower = jnp.linalg.cholesky(gram)]
    all_to_all x6 -> x2, waiting for transfers between devices: 94 us -> 44.4 us  [exchanged(): return lax.all_to_all(x, axis, split_axis=0, concat_axis=0, tiled=True)]
    dot_general x27 -> x0, matrix products: 43.7 us -> none  [the longest x9 14.4 us: advance(): jnp.einsum('gab,gb->ga', tile_block.astype(jnp.float32), picked, precisio...]
    pallas_call x0 -> x11, Pallas kernels: none -> 41.9 us  [call(): pl.pallas_call(body, out_shape=[jax.ShapeDtypeStruct(s, d) for s, d in ou...]
    scatter-add x21 -> x0, other arithmetic: 41.8 us -> none  [the longest x3 15.7 us: advance(): return running.at[col_block].add(product * live_mask[:, None, None])]
    all_to_all x10 -> x8, blocking collectives: 147 us -> 183 us  [exchanged(): return lax.all_to_all(x, axis, split_axis=0, concat_axis=0, tiled=True)]
    psum x4 -> x0, blocking collectives: 31.4 us -> none  [by_axis(): shard = lax.psum(shard, axis)]
    all_to_all x6 -> x2, starting transfers between devices: 36.9 us -> 8.04 us  [exchanged(): return lax.all_to_all(x, axis, split_axis=0, concat_axis=0, tiled=True)]
  transfers between devices with their start and end apart: 6 -> 2, of which waited for: 6 -> 2; matrix products, arithmetic and copies ran while one was open for 0% -> 0% of each run, Pallas kernels for 0% -> 1%
where the time goes in v1:
time: 286 us; the launch traced here: 285 us
  blocking collectives  183 us (64%)
  waiting for transfers between devices  44.4 us (16%)
  Pallas kernels  41.9 us (15%)
  starting transfers between devices  8.04 us (3%)
  local copies, waits for them, and re-layouts  5.82 us (2%)
    all_to_all x8, blocking collectives, exchanged(): return lax.all_to_all(x, axis, split_axis=0, concat_axis=0, tiled=True)  183 us
    all_to_all x2, waiting for transfers between devices, exchanged(): return lax.all_to_all(x, axis, split_axis=0, concat_axis=0, tiled=True)  44.4 us
    pallas_call x11, Pallas kernels, call(): pl.pallas_call(body, out_shape=[jax.ShapeDtypeStruct(s, d) for s, d in ou...  41.9 us
    all_to_all x2, starting transfers between devices, exchanged(): return lax.all_to_all(x, axis, split_axis=0, concat_axis=0, tiled=True)  8.04 us
  transfers between devices with their start and end apart: 2, of which 2 were waited for; matrix products, arithmetic and copies ran while one was open for 0% of the time, Pallas kernels for 1%

profile of v1, /device:TPU:1, one launch (start us, length us, event | category | flops | bytes accessed | tf_op | source)
XLA Modules:
  0.0 284.9 jit_solution(11144415322183504519)
XLA Ops:
  1.3 0.0 copy-start
  1.3 1.4 copy-done
  2.7 0.0 copy-start.2
  2.7 1.2 copy-done.2
  3.9 0.0 copy-start.5
  3.9 0.7 copy-done.5
  4.6 0.7 copy-done.7
  5.2 1.6 shard_map.84
  6.9 15.9 %all_to_all.50.got.refs_5_ = f32[16,24,128]{2,1,0:T(8,128)S(1)} all-to-all(f32[16,24,128]{2,1,0:T(8,128)S(1)} %shard_map.84), channel_id=1, replica_groups=mesh['term_0'=8,'term_1'=2,'doc_0'=4,'doc_1'=4] {'doc_0','doc_1'}, dimensions={0} | all-to-all | bytes 393216 | tf_op jit(solution)/shard_map/all_to_all | solution.py:262
  22.8 1.8 shard_map.85
  24.5 18.7 %all_to_all.51.got = f32[16,16,128]{2,1,0:T(8,128)S(1)} all-to-all(f32[16,16,128]{2,1,0:T(8,128)S(1)} %get-tuple-element.16), channel_id=1, replica_groups=mesh['term_0'=8,'term_1'=2,'doc_0'=4,'doc_1'=4] {'term_0','term_1'}, dimensions={0} | all-to-all | bytes 262144 | tf_op jit(solution)/shard_map/all_to_all | solution.py:262
  43.2 2.0 shard_map.86
  45.2 10.8 %all_to_all.52.got = f32[16,16,128]{2,1,0:T(8,128)S(1)} all-to-all(f32[16,16,128]{2,1,0:T(8,128)S(1)} %get-tuple-element.17), channel_id=1, replica_groups=mesh['term_0'=8,'term_1'=2,'doc_0'=4,'doc_1'=4] {'doc_0','doc_1'}, dimensions={0} | all-to-all | bytes 262144 | tf_op jit(solution)/shard_map/all_to_all | solution.py:262
  56.0 1.8 shard_map.87
  57.8 12.6 %all_to_all.53.refs_4_ = f32[16,16,128]{2,1,0:T(8,128)S(1)} all-to-all(f32[16,16,128]{2,1,0:T(8,128)S(1)} %get-tuple-element.19), channel_id=1, replica_groups=mesh['term_0'=8,'term_1'=2,'doc_0'=4,'doc_1'=4] {'term_0','term_1'}, dimensions={0} | all-to-all | bytes 262144 | tf_op jit(solution)/shard_map/all_to_all | solution.py:262
  70.4 0.0 copy-done.3
  70.4 3.7 %shard_map.88 = (bf16[16,256,128]{2,1,0:T(8,128)(2,1)}, f32[16,128]{1,0:T(8,128)}) custom-call(bf16[48,128,128]{2,1,0:T(8,128)(2,1)S(1)} %copy-done, s32[1,48]{1,0:T(1,128)S(1)} %copy-done.5, s32[1,48]{1,0:T(1,128)S(1)} %copy-done.7, s32[1,1]{1,0:T(1,128)S(6)} %copy.23.count.refs_3_, f32[16,16,128]{2,1,0:T(8,128)S(1)} %all_to_all.53.refs_4_, ...), custom_call_target="tpu_custom_call" | custom-call | tf_op jit(solution)/shard_map/pallas_call | solution.py:28
  74.1 4.5 %all-to-all-start.4 = ((bf16[16,256,128]{2,1,0:T(8,128)(2,1)}), bf16[16,256,128]{2,1,0:T(8,128)(2,1)S(1)}, u32[]{:S(2)}, u32[]{:S(2)}) async-start(bf16[16,256,128]{2,1,0:T(8,128)(2,1)} %get-tuple-element.21), calls=%async_computation.4 | async-start | bytes 2097152 | tf_op jit(solution)/shard_map/all_to_all | solution.py:262
  78.6 0.0 copy-start.1
  78.6 0.0 copy-start.6
  78.6 0.0 copy-start.8
  78.6 0.1 add_bitcast_fusion.place
  78.7 19.5 %all-to-all-done.4.got = bf16[16,256,128]{2,1,0:T(8,128)(2,1)S(1)} async-done(((bf16[16,256,128]{2,1,0:T(8,128)(2,1)}), bf16[16,256,128]{2,1,0:T(8,128)(2,1)S(1)}, u32[]{:S(2)}, u32[]{:S(2)}) %all-to-all-start.4) | async-done | bytes 1048608 | tf_op jit(solution)/shard_map/all_to_all | solution.py:262
  98.2 0.0 copy-done.4
  98.2 1.1 shard_map.89
  99.3 19.1 %all_to_all.54.scaled = bf16[16,256,128]{2,1,0:T(8,128)(2,1)S(1)} all-to-all(bf16[16,256,128]{2,1,0:T(8,128)(2,1)S(1)} %get-tuple-element.22), channel_id=1, replica_groups=mesh['term_0'=8,'term_1'=2,'doc_0'=4,'doc_1'=4] {'doc_0','doc_1'}, dimensions={0} | all-to-all | bytes 2097152 | tf_op jit(solution)/shard_map/all_to_all | solution.py:262
  118.4 0.0 copy-done.1
  118.4 0.0 copy-done.6
  118.4 0.0 copy-done.8
  118.4 1.7 shard_map.90
  120.2 0.0 copy-start.9
  120.2 55.2 %all_to_all.55.got = f32[16,256,128]{2,1,0:T(8,128)S(1)} all-to-all(f32[16,256,128]{2,1,0:T(8,128)S(1)} %shard_map.90), channel_id=1, replica_groups=mesh['term_0'=8,'term_1'=2,'doc_0'=4,'doc_1'=4] {'term_0','term_1'}, dimensions={0} | all-to-all | bytes 4194304 | tf_op jit(solution)/shard_map/all_to_all | solution.py:262
  175.3 0.0 copy-done.9
  175.3 1.1 shard_map.91
  176.4 0.2 copy.15
  176.6 0.2 copy.16
  176.8 25.0 %all_to_all.56.got = f32[256,3,128]{2,1,0:T(4,128)S(1)} all-to-all(f32[256,3,128]{2,1,0:T(4,128)S(1)} %copy.16), channel_id=1, replica_groups=mesh['term_0'=8,'term_1'=2,'doc_0'=4,'doc_1'=4] {'term_0','term_1','doc_..., dimensions={0} | all-to-all | bytes 786432 | tf_op jit(solution)/shard_map/all_to_all | solution.py:262
  201.8 0.3 shard_map.92
  202.2 26.0 %all_to_all.57 = f32[256,3,128]{2,1,0:T(4,128)S(1)} all-to-all(f32[256,3,128]{2,1,0:T(4,128)S(1)} %shard_map.92), channel_id=1, replica_groups=mesh['term_0'=8,'term_1'=2,'doc_0'=4,'doc_1'=4] {'term_0','term_1','doc_..., dimensions={0} | all-to-all | bytes 786432 | tf_op jit(solution)/shard_map/all_to_all | solution.py:262
  228.2 0.1 slice.8
  228.3 0.1 copy.20
  228.4 0.1 copy.19.refs_0_
  228.5 0.1 slice.9
  228.7 24.1 %shard_map.93 = (f32[256,256]{1,0:T(8,128)S(1)}, bf16[16,128,256]{2,1,0:T(8,128)(2,1)}) custom-call(f32[256,256]{1,0:T(8,128)S(1)} %copy.19.refs_0_, f32[256,128]{1,0:T(8,128)S(1)} %bitcast.12, f32[256,128]{1,0:T(8,128)S(1)} %get-tuple-element.25.refs_2_), custom_call_target="tpu_custom_call" | custom-call | tf_op jit(solution)/shard_map/pallas_call | solution.py:28
  252.7 3.6 %all-to-all-start.9 = ((bf16[16,128,256]{2,1,0:T(8,128)(2,1)}), bf16[16,128,256]{2,1,0:T(8,128)(2,1)S(1)}, u32[]{:S(2)}, u32[]{:S(2)}) async-start(bf16[16,128,256]{2,1,0:T(8,128)(2,1)} %get-tuple-element.27), calls=%async_computation.9 | async-start | bytes 2097152 | tf_op jit(solution)/shard_map/all_to_all | solution.py:262
  256.3 2.9 %shard_map.94 = bf16[2048,256]{1,0:T(8,128)(2,1)} custom-call(f32[256,256]{1,0:T(8,128)S(1)} %get-tuple-element.26.inverse, bf16[16,256,128]{2,1,0:T(8,128)(2,1)S(1)} %all_to_all.54.scaled, f32[16,128]{1,0:T(8,128)S(1)} %copy-done.4), custom_call_target="tpu_custom_call" | custom-call | tf_op jit(solution)/shard_map/pallas_call | solution.py:28
  259.1 24.8 %all-to-all-done.9 = bf16[16,128,256]{2,1,0:T(8,128)(2,1)S(1)} async-done(((bf16[16,128,256]{2,1,0:T(8,128)(2,1)}), bf16[16,128,256]{2,1,0:T(8,128)(2,1)S(1)}, u32[]{:S(2)}, u32[]{:S(2)}) %all-to-all-start.9) | async-done | bytes 1048608 | tf_op jit(solution)/shard_map/all_to_all | solution.py:262
  284.0 1.0 copy.24
  (3 shorter events, 0.0 us)
Async XLA Ops:
  1.3 1.4 copy-start
  2.7 1.2 copy-start.2
  3.9 0.7 copy-start.5
  4.6 0.7 copy-start.7
  24.5 45.9 %copy-start.3 = (bf16[2048,256]{1,0:T(8,128)(2,1)S(1)}, bf16[2048,256]{1,0:T(8,128)(2,1)}, u32[]{:S(2)}) copy-start(bf16[2048,256]{1,0:T(8,128)(2,1)} %refs_6_.1) | copy-start | bytes 3145732
  70.4 27.8 %copy-start.4 = (f32[16,128]{1,0:T(8,128)S(1)}, f32[16,128]{1,0:T(8,128)}, u32[]{:S(2)}) copy-start(f32[16,128]{1,0:T(8,128)} %get-tuple-element.18.row_scale) | copy-start | bytes 24580
  74.1 24.2 %all-to-all-start.4 = ((bf16[16,256,128]{2,1,0:T(8,128)(2,1)}), bf16[16,256,128]{2,1,0:T(8,128)(2,1)S(1)}, u32[]{:S(2)}, u32[]{:S(2)}) async-start(bf16[16,256,128]{2,1,0:T(8,128)(2,1)} %get-tuple-element.21), calls=%async_computation.4 | async-start | bytes 2097152 | tf_op jit(solution)/shard_map/all_to_all | solution.py:262
  78.6 39.8 %copy-start.1 = (bf16[48,128,128]{2,1,0:T(8,128)(2,1)S(1)}, bf16[48,128,128]{2,1,0:T(8,128)(2,1)}, u32[]{:S(2)}) copy-start(bf16[48,128,128]{2,1,0:T(8,128)(2,1)} %values.9) | copy-start | bytes 4718596
  78.6 39.8 %copy-start.6 = (s32[1,48]{1,0:T(1,128)S(1)}, s32[1,48]{1,0:T(1,128)}, u32[]{:S(2)}) copy-start(s32[1,48]{1,0:T(1,128)} %rows.9) | copy-start | bytes 580
  78.6 39.8 %copy-start.8 = (s32[1,48]{1,0:T(1,128)S(1)}, s32[1,48]{1,0:T(1,128)}, u32[]{:S(2)}) copy-start(s32[1,48]{1,0:T(1,128)} %cols.9) | copy-start | bytes 580
  120.2 55.2 %copy-start.9 = (f32[16,128]{1,0:T(8,128)S(1)}, f32[16,128]{1,0:T(8,128)}, u32[]{:S(2)}) copy-start(f32[16,128]{1,0:T(8,128)} %get-tuple-element.20.col_scale) | copy-start | bytes 24580
  252.7 31.2 %all-to-all-start.9 = ((bf16[16,128,256]{2,1,0:T(8,128)(2,1)}), bf16[16,128,256]{2,1,0:T(8,128)(2,1)S(1)}, u32[]{:S(2)}, u32[]{:S(2)}) async-start(bf16[16,128,256]{2,1,0:T(8,128)(2,1)} %get-tuple-element.27), calls=%async_computation.9 | async-start | bytes 2097152 | tf_op jit(solution)/shard_map/all_to_all | solution.py:262

commit v2 on v1

v2 whole, which is shorter than its diff:
```python
import jax
import jax.numpy as jnp
from jax import lax
from jax.experimental import pallas as pl
from jax.experimental.pallas import tpu as pltpu
from jax.sharding import Mesh
from jax.sharding import PartitionSpec as P

TILE = 128
K = 256
RB = 16
CB = 16
CAP = 48
GROUP = 8
PANEL = 64
TERM = ("term_0", "term_1")
DOC = ("doc_0", "doc_1")
ALL = TERM + DOC
F32 = jnp.float32
BF16 = jnp.bfloat16
PRECISE = lax.Precision.HIGHEST
VMEM = pl.BlockSpec(memory_space=pltpu.VMEM)
SMEM = pl.BlockSpec(memory_space=pltpu.SMEM)


def call(body, inputs, outs, scratch=(), flops=1 << 20):
    specs = [SMEM if a.dtype == jnp.int32 else VMEM for a in inputs]
    return pl.pallas_call(
        body,
        out_shape=[jax.ShapeDtypeStruct(s, d) for s, d in outs],
        in_specs=specs,
        out_specs=[SMEM if d == jnp.int32 else VMEM for _, d in outs],
        scratch_shapes=[pltpu.VMEM(s, d) for s, d in scratch],
        compiler_params=pltpu.CompilerParams(vmem_limit_bytes=16 * 1024 * 1024),
    )(*inputs)


def thirds(x):
    hi = x.astype(BF16)
    rest = x - hi.astype(F32)
    mid = rest.astype(BF16)
    low = (rest - mid.astype(F32)).astype(BF16)
    return hi, mid, low


def put_thirds(ref, vec, base):
    hi, mid, low = thirds(vec)
    row = lax.broadcasted_iota(jnp.int32, (16, TILE), 0)
    for b in range(RB):
        parts = [jnp.broadcast_to(p[b : b + 1].astype(F32), (16, TILE)) for p in (hi, mid, low)]
        rows = jnp.where(row == 0, parts[0], jnp.where(row == 1, parts[1], jnp.where(row == 2, parts[2], 0.0)))
        ref[b, base : base + 16, :] = rows.astype(BF16)


def over_tiles(count, values, source, target, src_ref, acc_ref, transposed):
    acc_ref[...] = jnp.zeros(acc_ref.shape, F32)
    dims = (((1,), (1,)), ((), ())) if transposed else (((1,), (0,)), ((), ()))

    def visit(g, _):
        products = []
        for u in range(GROUP):
            s = g * GROUP + u
            tile = values[s]
            tile = jnp.where(s < count, tile, jnp.zeros_like(tile))
            products.append(
                lax.dot_general(src_ref[source[0, s]], tile, dims, preferred_element_type=F32)
            )
        for u in range(GROUP):
            s = g * GROUP + u
            acc_ref[target[0, s]] += products[u]
        return 0

    lax.fori_loop(0, (count + GROUP - 1) // GROUP, visit, 0)


def send_vector(out_ref, acc_ref):
    vec = jnp.sum(acc_ref[...], axis=1)
    for i in range(16):
        out_ref[i, 0:RB, :] = vec


def start_sums(place, values, rows, cols, count, start, out, place_out, src, acc):
    place_out[0, 0] = place[0, 0]
    place_out[0, 1] = place[0, 1]
    put_thirds(src, jnp.ones((CB, TILE), F32), 0)
    over_tiles(count[0, 0], values, cols, rows, src, acc, True)
    send_vector(out, acc)
    mean = jnp.sum(start[...].astype(F32), axis=0, keepdims=True)
    for i in range(16):
        out[i, 16:17, :] = mean[:, :TILE]
        out[i, 17:18, :] = mean[:, TILE:]
        out[i, 18:24, :] = jnp.zeros((6, TILE), F32)


def to_columns(values, rows, cols, count, got, out, scale, src, acc):
    vec = 1.0 / jnp.sum(got[...], axis=0)[0:RB]
    scale[...] = vec
    put_thirds(src, vec, 0)
    over_tiles(count[0, 0], values, rows, cols, src, acc, False)
    send_vector(out, acc)


def to_rows(values, rows, cols, count, got, out, scale, src, acc):
    vec = 1.0 / jnp.sum(got[...], axis=0)[0:RB]
    scale[...] = vec
    put_thirds(src, vec, 0)
    over_tiles(count[0, 0], values, cols, rows, src, acc, True)
    send_vector(out, acc)


def left_product(docs, values, rows, cols, count, got, first, start, out, scale, src, acc):
    vec = 1.0 / jnp.sum(got[...], axis=0)
    scale[...] = vec
    put_thirds(src, vec, K)
    for b in range(CB):
        block = start[b * TILE : (b + 1) * TILE, :].astype(F32).T
        src[b, 0:K, :] = (block * vec[b : b + 1, :]).astype(BF16)
    mean = jnp.sum(first[...], axis=0)[16:18] / docs
    mean = jnp.concatenate([jnp.broadcast_to(mean[h : h + 1], (TILE, TILE)).T for h in range(2)], axis=0)
    over_tiles(count[0, 0], values, cols, rows, src, acc, True)
    for b in range(RB):
        weight = jnp.sum(acc[b, K : K + 16, :], axis=0, keepdims=True)
        out[b] = (acc[b, 0:K, :] - mean * weight).astype(out.dtype)


def left_rows(place, got, row_scale, out, gram):
    d = place[0, 1]
    scale = row_scale[pl.ds(d, 1), :]
    left = scale * jnp.sum(got[...].astype(F32), axis=0)
    sent = (left * scale).astype(BF16)
    for i in range(16):
        out[i] = sent
    gram[...] = lax.dot_general(left, left, (((1,), (1,)), ((), ())), precision=PRECISE, preferred_element_type=F32)


LEVELS = 32000.0
STEPS = 64.0


def code_of(peak):
    return jnp.ceil(jnp.log2(jnp.maximum(peak, 1e-37)) * STEPS)


def code_lines(code):
    lines = jnp.broadcast_to(code, (K, TILE)).T
    return jnp.concatenate([lines[0:8, :TILE], lines[0:8, TILE:]], axis=0).astype(jnp.int32).astype(jnp.int16)


def counted(x, code):
    steps = x * (jnp.exp2(code * (-1.0 / STEPS)) * LEVELS)
    return jnp.floor(steps + 0.5).astype(jnp.int32).astype(jnp.int16)


def wide(x):
    return x.astype(jnp.int32).astype(F32)


def steps_of(got):
    lines = [wide(got[i, K : K + 16, :]) for i in range(16)]
    code = jnp.concatenate(
        [jnp.concatenate([x[h : h + 1] for x in lines], axis=0) for h in (0, 8)], axis=1
    ).T
    return jnp.exp2(code * (1.0 / STEPS)) * (1.0 / LEVELS)


def right_product(values, rows, cols, count, scaled, col_scale, out, acc):
    over_tiles(count[0, 0], values, rows, cols, scaled, acc, False)
    peak = jnp.zeros((K, TILE), F32)
    for b in range(CB):
        part = acc[b] * col_scale[b : b + 1, :]
        acc[b] = part
        peak = jnp.maximum(peak, jnp.abs(part))
    code = code_of(jnp.max(peak, axis=1, keepdims=True))
    lines = code_lines(code)
    for b in range(CB):
        out[b, 0:K, :] = counted(acc[b], code)
        out[b, K : K + 16, :] = lines


def iotas(shape=(K, K)):
    return lax.broadcasted_iota(jnp.int32, shape, 0), lax.broadcasted_iota(jnp.int32, shape, 1)


def right_rows(got, left_gram, out, own):
    step = steps_of(got)
    right = wide(got[0, 0:K, :]) * step[:, 0:1]
    for i in range(1, 16):
        right += wide(got[i, 0:K, :]) * step[:, i : i + 1]
    code = code_of(jnp.max(jnp.abs(right), axis=1, keepdims=True))
    own[0:K, :] = counted(right, code)
    own[K : K + 16, :] = code_lines(code)
    gram = lax.dot_general(right, right, (((1,), (1,)), ((), ())), precision=PRECISE, preferred_element_type=F32)
    row, col = iotas()
    packed = jnp.where(row >= col, left_gram[...], gram)
    diag = jnp.sum(jnp.where(row == col, gram, 0.0), axis=1, keepdims=True)
    lean = jnp.sum(right, axis=1, keepdims=True)
    lane = lax.broadcasted_iota(jnp.int32, (K, TILE), 1)
    extra = jnp.where(lane == 0, diag, jnp.where(lane == 1, lean, 0.0))
    out[:, 0:K] = packed
    out[:, K : K + TILE] = extra


def sum_all(got, out):
    total = jnp.sum(got[...], axis=0)
    for i in range(16):
        out[i] = total


def eliminate(blocks, at):
    blocks = list(blocks)
    sub = lax.broadcasted_iota(jnp.int32, (8, 1), 0)
    for g in range(len(blocks)):
        lead = blocks[g]
        below = range(g + 1, len(blocks))
        lanes = [at + 8 * g + b for b in range(8)]
        head = [lead[:, l : l + 1] for l in lanes]
        cols = {j: [blocks[j][:, l : l + 1] for l in lanes] for j in below}
        pivots = jnp.ones((8, 1), F32)
        for a in range(8):
            pivot = head[a][a : a + 1]
            inv = 1.0 / pivot
            pivots = jnp.where(sub == a, pivot, pivots)
            line = lead[a : a + 1, :]
            entries = [head[b][a : a + 1] for b in range(8)]
            f = jnp.where(sub > a, head[a] * inv, 0.0)
            lead = lead - f * line
            for b in range(a + 1, 8):
                head[b] = head[b] - f * entries[b]
            for j in below:
                f = cols[j][a] * inv
                blocks[j] = blocks[j] - f * line
                for b in range(a + 1, 8):
                    cols[j][b] = cols[j][b] - f * entries[b]
        blocks[g] = lead * lax.rsqrt(pivots)
    return blocks


def factor(work):
    lane = lax.broadcasted_iota(jnp.int32, (PANEL, TILE), 1)
    line = lax.broadcasted_iota(jnp.int32, (PANEL, TILE), 0)
    for start in range(0, K, PANEL):
        first = (start // TILE) * TILE
        span = slice(first, first + 3 * TILE)
        end = start + PANEL
        at = start - first
        other = PANEL - at
        unit = jnp.where(lane == line + other, 1.0, 0.0)
        here = (lane >= at) & (lane < at + PANEL)
        panels = []
        for m in range(2):
            block = jnp.where(here, work[m, start:end, first : first + TILE], unit)
            panels.append([block[8 * j : 8 * j + 8] for j in range(PANEL // 8)])
        for m, blocks in enumerate(both(panels, at)):
            done = jnp.concatenate(blocks, axis=0)
            inverse = done[:, other : other + PANEL]
            panel = jnp.dot(inverse, work[m, start:end, span], precision=PRECISE, preferred_element_type=F32)
            work[m, start:end, span] = panel
            if end < K:
                work[m, end:K, span] -= lax.dot_general(
                    panel[:, end - first : K - first],
                    panel,
                    (((0,), (0,)), ((), ())),
                    precision=PRECISE,
                    preferred_element_type=F32,
                )


def both(panels, at):
    return [eliminate(p, at) for p in panels]


def finish(terms, docs, grams, inverse, lean_out, work):
    row, col = iotas()
    one = grams[:, 0:K]
    other = one.T
    e = grams[:, K : K + TILE]
    lean = e[:, 1:2] / docs
    lean_row = jnp.sum(jnp.where(row == col, lean, 0.0), axis=0, keepdims=True)
    left = jnp.where(row >= col, one, other) / terms
    right = jnp.where(row < col, one, jnp.where(row == col, e[:, 0:1], other)) / docs - lean * lean_row
    eye = jnp.where(row == col, 1.0, 0.0).astype(F32)
    for m, gram in ((0, left), (1, right)):
        work[m, :, 0:K] = gram
        work[m, :, K : 2 * K] = eye
    factor(work)
    for m in range(2):
        inverse[m] = jnp.where(row >= col, work[m, :, K : 2 * K], 0.0)
    lean_out[...] = jnp.broadcast_to(lean, lean_out.shape)


def bases(inverse, scaled, row_scale, gathered, lean, left_out, right_out):
    hi, mid, low = thirds(inverse[0])
    for b in range(RB):
        total = (
            jnp.dot(hi, scaled[b], preferred_element_type=F32)
            + jnp.dot(mid, scaled[b], preferred_element_type=F32)
            + jnp.dot(low, scaled[b], preferred_element_type=F32)
        )
        basis = total / row_scale[b : b + 1, :]
        left_out[b * TILE : (b + 1) * TILE, :] = basis.T.astype(BF16)
    hi, mid, low = thirds(inverse[1])
    step = steps_of(gathered)
    mean = lean[:, 0:1]
    for b in range(CB):
        block = wide(gathered[b, 0:K, :]) * step[:, b : b + 1] - mean
        top = block.astype(BF16)
        rest = (block - top.astype(F32)).astype(BF16)
        total = (
            jnp.dot(hi, top, preferred_element_type=F32)
            + jnp.dot(mid, top, preferred_element_type=F32)
            + jnp.dot(low, top, preferred_element_type=F32)
            + jnp.dot(hi, rest, preferred_element_type=F32)
            + jnp.dot(mid, rest, preferred_element_type=F32)
        )
        right_out[b * TILE : (b + 1) * TILE, :] = total.T.astype(BF16)


def exchanged(x, axis):
    return lax.all_to_all(x, axis, split_axis=0, concat_axis=0, tiled=True)


def per_device(tile_values, tile_rows, tile_cols, tile_count, start_block):
    terms = float(RB * TILE * lax.axis_size(TERM))
    docs = float(CB * TILE * lax.axis_size(DOC))
    place = jnp.stack([lax.axis_index(TERM), lax.axis_index(DOC)]).astype(jnp.int32)[None]
    tiles = (tile_values, tile_rows, tile_cols, tile_count)
    vec = [((RB, 16, TILE), BF16), ((RB, 16, TILE), F32)]
    vector = ((16, RB, TILE), F32)
    scale = ((RB, TILE), F32)
    part, place = call(
        start_sums, (place, *tiles, start_block), [((16, 24, TILE), F32), ((1, 2), jnp.int32)], vec
    )
    first = exchanged(part, DOC)
    part, _ = call(to_columns, (*tiles, first), [vector, scale], vec)
    part, _ = call(to_rows, (*tiles, exchanged(part, TERM)), [vector, scale], vec)
    part, row_scale = call(to_columns, (*tiles, exchanged(part, DOC)), [vector, scale], vec)
    part, col_scale = call(
        lambda *refs: left_product(docs, *refs),
        (*tiles, exchanged(part, TERM), first, start_block),
        [((RB, K, TILE), BF16), scale],
        [((CB, K + 16, TILE), BF16), ((RB, K + 16, TILE), F32)],
    )
    part, left_gram = call(
        left_rows, (place, exchanged(part, DOC), row_scale), [((16, K, TILE), BF16), ((K, K), F32)]
    )
    scaled = exchanged(part, DOC)
    (part,) = call(
        right_product, (*tiles, scaled, col_scale), [((CB, K + 16, TILE), jnp.int16)], [((CB, K, TILE), F32)]
    )
    part, own = call(
        right_rows,
        (exchanged(part, TERM), left_gram),
        [((K, 3 * TILE), F32), ((K + 16, TILE), jnp.int16)],
    )
    gathered = lax.all_gather(own, TERM)
    spread = [((16, 16, 3 * TILE), F32)]
    part = exchanged(part.reshape(16, 16, 3 * TILE), DOC)
    (part,) = call(sum_all, (part,), spread)
    (part,) = call(sum_all, (exchanged(part, TERM),), spread)
    grams = exchanged(part, DOC).reshape(K, 3 * TILE)
    inverse, lean = call(
        lambda *refs: finish(terms, docs, *refs),
        (grams,),
        [((2, K, K), F32), ((K, TILE), F32)],
        [((2, K, 2 * K), F32)],
    )
    left_basis, right_basis = call(
        bases,
        (inverse, scaled, row_scale, gathered, lean),
        [((RB * TILE, K), BF16), ((CB * TILE, K), BF16)],
    )
    return (row_scale.reshape(-1), col_scale.reshape(-1), left_basis, right_basis)


def solution(mesh):
    torus = Mesh(mesh.devices.reshape(8, 2, 4, 4), ("term_0", "term_1", "doc_0", "doc_1"))
    placed = (P(TERM, DOC, None), P(TERM, DOC), P(TERM, DOC), P(TERM, DOC), P(DOC, None))
    return jax.shard_map(
        per_device,
        mesh=torus,
        in_specs=placed,
        out_specs=(P(TERM), P(DOC), P(TERM, None), P(DOC, None)),
        check_vma=False,
    )
```

time: 286 us -> 255 us (0.89)
  waiting for transfers between devices: 44.4 us -> 0.01 us
  Pallas kernels: 41.9 us -> 63.7 us
  starting transfers between devices: 8.04 us -> 3.55 us
    all_to_all x2 -> x1, waiting for transfers between devices: 44.4 us -> 0.01 us  [exchanged(): return lax.all_to_all(x, axis, split_axis=0, concat_axis=0, tiled=True)]
    pallas_call x11 -> x12, Pallas kernels: 41.9 us -> 63.7 us  [call(): pl.pallas_call(body, out_shape=[jax.ShapeDtypeStruct(s, d) for s, d in ou...]
    all_to_all x8 -> x9, blocking collectives: 183 us -> 163 us  [exchanged(): return lax.all_to_all(x, axis, split_axis=0, concat_axis=0, tiled=True)]
    all_gather x0 -> x1, blocking collectives: none -> 17.8 us  [per_device(): gathered = lax.all_gather(own, TERM)]
    all_to_all x2 -> x1, starting transfers between devices: 8.04 us -> 3.55 us  [exchanged(): return lax.all_to_all(x, axis, split_axis=0, concat_axis=0, tiled=True)]
  transfers between devices with their start and end apart: 2 -> 1, of which waited for: 2 -> 0; matrix products, arithmetic and copies ran while one was open for 0% -> 0% of each run, Pallas kernels for 1% -> 0%
where the time goes in v2:
time: 255 us; the launch traced here: 254 us
  blocking collectives  181 us (71%)
  Pallas kernels  63.7 us (25%)
  local copies, waits for them, and re-layouts  3.97 us (2%)
  starting transfers between devices  3.55 us (1%)
    all_to_all x9, blocking collectives, exchanged(): return lax.all_to_all(x, axis, split_axis=0, concat_axis=0, tiled=True)  163 us
    pallas_call x12, Pallas kernels, call(): pl.pallas_call(body, out_shape=[jax.ShapeDtypeStruct(s, d) for s, d in ou...  63.7 us
    all_gather x1, blocking collectives, per_device(): gathered = lax.all_gather(own, TERM)  17.8 us
  transfers between devices with their start and end apart: 1, of which 0 were waited for; matrix products, arithmetic and copies ran while one was open for 0% of the time, Pallas kernels for 0%

profile of v2, /device:TPU:1, one launch (start us, length us, event | category | flops | bytes accessed | tf_op | source)
XLA Modules:
  0.0 253.8 jit_solution(14406045751833101683)
XLA Ops:
  1.3 0.1 add_bitcast_fusion.place
  1.4 0.0 copy-start
  1.4 1.4 copy-done
  2.8 0.0 copy-start.2
  2.8 1.2 copy-done.2
  4.0 0.0 copy-start.5
  4.0 0.7 copy-done.5
  4.7 0.0 copy-start.7
  4.7 0.7 copy-done.7
  5.3 0.0 copy-start.1
  5.3 0.0 copy-start.6
  5.3 1.9 shard_map.84
  7.3 15.5 %all_to_all.50.got.refs_5_ = f32[16,24,128]{2,1,0:T(8,128)S(1)} all-to-all(f32[16,24,128]{2,1,0:T(8,128)S(1)} %get-tuple-element.20), channel_id=1, replica_groups=mesh['term_0'=8,'term_1'=2,'doc_0'=4,'doc_1'=4] {'doc_0','doc_1'}, dimensions={0} | all-to-all | bytes 393216 | tf_op jit(solution)/shard_map/all_to_all | solution.py:319
  22.7 0.0 copy-done.1
  22.7 0.0 copy-done.6
  22.7 0.0 copy-start.8
  22.7 1.8 shard_map.85
  24.5 18.9 %all_to_all.51.got = f32[16,16,128]{2,1,0:T(8,128)S(1)} all-to-all(f32[16,16,128]{2,1,0:T(8,128)S(1)} %get-tuple-element.21), channel_id=1, replica_groups=mesh['term_0'=8,'term_1'=2,'doc_0'=4,'doc_1'=4] {'term_0','term_1'}, dimensions={0} | all-to-all | bytes 262144 | tf_op jit(solution)/shard_map/all_to_all | solution.py:319
  43.4 0.0 copy-done.8
  43.4 2.0 shard_map.86
  45.3 0.0 copy-start.3
  45.4 10.7 %all_to_all.52.got = f32[16,16,128]{2,1,0:T(8,128)S(1)} all-to-all(f32[16,16,128]{2,1,0:T(8,128)S(1)} %get-tuple-element.22), channel_id=1, replica_groups=mesh['term_0'=8,'term_1'=2,'doc_0'=4,'doc_1'=4] {'doc_0','doc_1'}, dimensions={0} | all-to-all | bytes 262144 | tf_op jit(solution)/shard_map/all_to_all | solution.py:319
  56.1 1.8 shard_map.87
  57.8 12.7 %all_to_all.53.refs_4_ = f32[16,16,128]{2,1,0:T(8,128)S(1)} all-to-all(f32[16,16,128]{2,1,0:T(8,128)S(1)} %get-tuple-element.24), channel_id=1, replica_groups=mesh['term_0'=8,'term_1'=2,'doc_0'=4,'doc_1'=4] {'term_0','term_1'}, dimensions={0} | all-to-all | bytes 262144 | tf_op jit(solution)/shard_map/all_to_all | solution.py:319
  70.5 0.0 copy-done.3
  70.5 3.1 %shard_map.88 = (bf16[16,256,128]{2,1,0:T(8,128)(2,1)S(1)}, f32[16,128]{1,0:T(8,128)}) custom-call(bf16[48,128,128]{2,1,0:T(8,128)(2,1)S(1)} %copy-done.1, s32[1,48]{1,0:T(1,128)S(1)} %copy-done.6, s32[1,48]{1,0:T(1,128)S(1)} %copy-done.8, s32[1,1]{1,0:T(1,128)S(6)} %copy.9.count.refs_3_, f32[16,16,128]{2,1,0:T(8,128)S(1)} %all_to_all.53.refs_4_, ...), custom_call_target="tpu_custom_call" | custom-call | tf_op jit(solution)/shard_map/pallas_call | solution.py:28
  73.6 0.0 copy-start.4
  73.6 21.4 %all_to_all.54.got = bf16[16,256,128]{2,1,0:T(8,128)(2,1)S(1)} all-to-all(bf16[16,256,128]{2,1,0:T(8,128)(2,1)S(1)} %get-tuple-element.27), channel_id=1, replica_groups=mesh['term_0'=8,'term_1'=2,'doc_0'=4,'doc_1'=4] {'doc_0','doc_1'}, dimensions={0} | all-to-all | bytes 2097152 | tf_op jit(solution)/shard_map/all_to_all | solution.py:319
  95.0 0.0 copy-done.4
  95.0 1.1 shard_map.89
  96.1 0.0 copy-start.9
  96.1 18.7 %all_to_all.55.scaled = bf16[16,256,128]{2,1,0:T(8,128)(2,1)S(1)} all-to-all(bf16[16,256,128]{2,1,0:T(8,128)(2,1)S(1)} %get-tuple-element.28), channel_id=1, replica_groups=mesh['term_0'=8,'term_1'=2,'doc_0'=4,'doc_1'=4] {'doc_0','doc_1'}, dimensions={0} | all-to-all | bytes 2097152 | tf_op jit(solution)/shard_map/all_to_all | solution.py:319
  114.9 0.0 copy-done.9
  114.9 2.5 %shard_map.90 = s16[16,272,128]{2,1,0:T(8,128)(2,1)S(1)} custom-call(bf16[48,128,128]{2,1,0:T(8,128)(2,1)S(1)} %copy-done.1, s32[1,48]{1,0:T(1,128)S(1)} %copy-done.6, s32[1,48]{1,0:T(1,128)S(1)} %copy-done.8, s32[1,1]{1,0:T(1,128)S(6)} %copy.9.count.refs_3_, bf16[16,256,128]{2,1,0:T(8,128)(2,1)S(1)} %all_to_all.55.scaled, f32[16,128]{1,0:T(8,128)S(1)} %copy-done.9), custom_call_target="tpu_custom_call" | custom-call | tf_op jit(solution)/shard_map/pallas_call | solution.py:28
  117.4 34.5 %all_to_all.56.got = s16[16,272,128]{2,1,0:T(8,128)(2,1)S(1)} all-to-all(s16[16,272,128]{2,1,0:T(8,128)(2,1)S(1)} %shard_map.90), channel_id=1, replica_groups=mesh['term_0'=8,'term_1'=2,'doc_0'=4,'doc_1'=4] {'term_0','term_1'}, dimensions={0} | all-to-all | bytes 2228224 | tf_op jit(solution)/shard_map/all_to_all | solution.py:319
  151.9 1.2 shard_map.91
  153.1 12.4 %all_to_all.57.got = f32[16,16,384]{2,1,0:T(8,128)S(1)} all-to-all(f32[16,16,384]{2,1,0:T(8,128)S(1)} %bitcast.11), channel_id=1, replica_groups=mesh['term_0'=8,'term_1'=2,'doc_0'=4,'doc_1'=4] {'doc_0','doc_1'}, dimensions={0} | all-to-all | bytes 786432 | tf_op jit(solution)/shard_map/all_to_all | solution.py:319
  165.6 18.6 %all_to_all.58.got = f32[16,16,384]{2,1,0:T(8,128)S(1)} all-to-all(f32[16,16,384]{2,1,0:T(8,128)S(1)} %shard_map.92), channel_id=1, replica_groups=mesh['term_0'=8,'term_1'=2,'doc_0'=4,'doc_1'=4] {'term_0','term_1'}, dimensions={0} | all-to-all | bytes 786432 | tf_op jit(solution)/shard_map/all_to_all | solution.py:319
  184.1 0.8 shard_map.93
  184.9 3.6 %all-to-all-start.9 = ((f32[16,16,384]{2,1,0:T(8,128)}), f32[16,16,384]{2,1,0:T(8,128)S(1)}, u32[]{:S(2)}, u32[]{:S(2)}) async-start(f32[16,16,384]{2,1,0:T(8,128)} %shard_map.93), calls=%async_computation.9 | async-start | bytes 786432 | tf_op jit(solution)/shard_map/all_to_all | solution.py:319
  188.5 17.8 %all-gather.2 = s16[4352,128]{1,0:T(8,128)(2,1)S(1)} all-gather(s16[272,128]{1,0:T(8,128)(2,1)S(1)} %get-tuple-element.32), channel_id=2, replica_groups=mesh['term_0'=8,'term_1'=2,'doc_0'=4,'doc_1'=4] {'term_0','term_1'}, dimensions={0}, use_global_device_ids=true | all-gather | bytes 1183744 | tf_op jit(solution)/shard_map/all_gather | solution.py:355
  206.3 0.0 all-to-all-done.9
  206.3 41.9 %shard_map.94 = (f32[2,256,256]{2,1,0:T(8,128)S(1)}, f32[256,128]{1,0:T(8,128)S(1)}) custom-call(f32[256,384]{1,0:T(8,128)S(1)} %bitcast.10), custom_call_target="tpu_custom_call" | custom-call | tf_op jit(solution)/shard_map/pallas_call | solution.py:28
  248.2 5.6 %shard_map.95 = (bf16[2048,256]{1,0:T(8,128)(2,1)}, bf16[2048,256]{1,0:T(8,128)(2,1)}) custom-call(f32[2,256,256]{2,1,0:T(8,128)S(1)} %get-tuple-element.31.inverse, bf16[16,256,128]{2,1,0:T(8,128)(2,1)S(1)} %all_to_all.55.scaled, f32[16,128]{1,0:T(8,128)S(1)} %copy-done.4, s16[16,272,128]{2,1,0:T(8,128)(2,1)S(1)} %bitcast.9, ...), custom_call_target="tpu_custom_call" | custom-call | tf_op jit(solution)/shard_map/pallas_call | solution.py:28
  (1 shorter events, 0.0 us)
Async XLA Ops:
  1.4 1.4 copy-start
  2.8 1.2 copy-start.2
  4.0 0.7 copy-start.5
  4.7 0.7 copy-start.7
  5.3 17.4 %copy-start.1 = (bf16[48,128,128]{2,1,0:T(8,128)(2,1)S(1)}, bf16[48,128,128]{2,1,0:T(8,128)(2,1)}, u32[]{:S(2)}) copy-start(bf16[48,128,128]{2,1,0:T(8,128)(2,1)} %values.9) | copy-start | bytes 4718596
  5.3 17.4 %copy-start.6 = (s32[1,48]{1,0:T(1,128)S(1)}, s32[1,48]{1,0:T(1,128)}, u32[]{:S(2)}) copy-start(s32[1,48]{1,0:T(1,128)} %rows.9) | copy-start | bytes 580
  22.7 20.7 %copy-start.8 = (s32[1,48]{1,0:T(1,128)S(1)}, s32[1,48]{1,0:T(1,128)}, u32[]{:S(2)}) copy-start(s32[1,48]{1,0:T(1,128)} %cols.9) | copy-start | bytes 580
  45.3 25.2 %copy-start.3 = (bf16[2048,256]{1,0:T(8,128)(2,1)S(1)}, bf16[2048,256]{1,0:T(8,128)(2,1)}, u32[]{:S(2)}) copy-start(bf16[2048,256]{1,0:T(8,128)(2,1)} %refs_6_.1) | copy-start | bytes 3145732
  73.6 21.4 %copy-start.4 = (f32[16,128]{1,0:T(8,128)S(1)}, f32[16,128]{1,0:T(8,128)}, u32[]{:S(2)}) copy-start(f32[16,128]{1,0:T(8,128)} %get-tuple-element.23.row_scale) | copy-start | bytes 24580
  96.1 18.8 %copy-start.9 = (f32[16,128]{1,0:T(8,128)S(1)}, f32[16,128]{1,0:T(8,128)}, u32[]{:S(2)}) copy-start(f32[16,128]{1,0:T(8,128)} %get-tuple-element.25.col_scale) | copy-start | bytes 24580
  184.9 21.4 %all-to-all-start.9 = ((f32[16,16,384]{2,1,0:T(8,128)}), f32[16,16,384]{2,1,0:T(8,128)S(1)}, u32[]{:S(2)}, u32[]{:S(2)}) async-start(f32[16,16,384]{2,1,0:T(8,128)} %shard_map.93), calls=%async_computation.9 | async-start | bytes 786432 | tf_op jit(solution)/shard_map/all_to_all | solution.py:319

commit v3 on v2

--- a/solution.py
+++ b/solution.py
@@ -206,38 +206,48 @@
         out[i] = total
 
 
+def spread(x, lane):
+    return jnp.broadcast_to(x[:, :, lane : lane + 1], x.shape)
+
+
 def eliminate(blocks, at):
     blocks = list(blocks)
-    sub = lax.broadcasted_iota(jnp.int32, (8, 1), 0)
+    sub = lax.broadcasted_iota(jnp.int32, (2, 8, TILE), 1)
     for g in range(len(blocks)):
         lead = blocks[g]
-        below = range(g + 1, len(blocks))
         lanes = [at + 8 * g + b for b in range(8)]
-        head = [lead[:, l : l + 1] for l in lanes]
-        cols = {j: [blocks[j][:, l : l + 1] for l in lanes] for j in below}
-        pivots = jnp.ones((8, 1), F32)
+        head = [spread(lead, l) for l in lanes]
+        pivots = jnp.ones((2, 8, TILE), F32)
+        lines, inverses, entries = [], [], []
         for a in range(8):
-            pivot = head[a][a : a + 1]
+            pivot = head[a][:, a : a + 1]
             inv = 1.0 / pivot
+            line = lead[:, a : a + 1]
+            entry = [head[b][:, a : a + 1] for b in range(8)]
+            lines.append(line)
+            inverses.append(inv)
+            entries.append(entry)
             pivots = jnp.where(sub == a, pivot, pivots)
-            line = lead[a : a + 1, :]
-            entries = [head[b][a : a + 1] for b in range(8)]
             f = jnp.where(sub > a, head[a] * inv, 0.0)
             lead = lead - f * line
             for b in range(a + 1, 8):
-                head[b] = head[b] - f * entries[b]
-            for j in below:
-                f = cols[j][a] * inv
-                blocks[j] = blocks[j] - f * line
+                head[b] = head[b] - f * entry[b]
+        for j in range(g + 1, len(blocks)):
+            cols = [spread(blocks[j], l) for l in lanes]
+            total = blocks[j]
+            for a in range(8):
+                f = cols[a] * inverses[a]
+                total = total - f * lines[a]
                 for b in range(a + 1, 8):
-                    cols[j][b] = cols[j][b] - f * entries[b]
+                    cols[b] = cols[b] - f * entries[a][b]
+            blocks[j] = total
         blocks[g] = lead * lax.rsqrt(pivots)
     return blocks
 
 
 def factor(work):
-    lane = lax.broadcasted_iota(jnp.int32, (PANEL, TILE), 1)
-    line = lax.broadcasted_iota(jnp.int32, (PANEL, TILE), 0)
+    lane = lax.broadcasted_iota(jnp.int32, (2, PANEL, TILE), 2)
+    line = lax.broadcasted_iota(jnp.int32, (2, PANEL, TILE), 1)
     for start in range(0, K, PANEL):
         first = (start // TILE) * TILE
         span = slice(first, first + 3 * TILE)
@@ -246,13 +256,10 @@
         other = PANEL - at
         unit = jnp.where(lane == line + other, 1.0, 0.0)
         here = (lane >= at) & (lane < at + PANEL)
-        panels = []
+        block = jnp.where(here, work[:, start:end, first : first + TILE], unit)
+        done = jnp.concatenate(eliminate([block[:, 8 * j : 8 * j + 8] for j in range(PANEL // 8)], at), axis=1)
         for m in range(2):
-            block = jnp.where(here, work[m, start:end, first : first + TILE], unit)
-            panels.append([block[8 * j : 8 * j + 8] for j in range(PANEL // 8)])
-        for m, blocks in enumerate(both(panels, at)):
-            done = jnp.concatenate(blocks, axis=0)
-            inverse = done[:, other : other + PANEL]
+            inverse = done[m, :, other : other + PANEL]
             panel = jnp.dot(inverse, work[m, start:end, span], precision=PRECISE, preferred_element_type=F32)
             work[m, start:end, span] = panel
             if end < K:
@@ -263,10 +270,6 @@
                     precision=PRECISE,
                     preferred_element_type=F32,
                 )
-
-
-def both(panels, at):
-    return [eliminate(p, at) for p in panels]
 
 
 def finish(terms, docs, grams, inverse, lean_out, work):

time: 255 us -> 226 us (0.89)
  Pallas kernels: 63.7 us -> 33.8 us
    pallas_call x12, Pallas kernels: 63.7 us -> 33.8 us  [call(): pl.pallas_call(body, out_shape=[jax.ShapeDtypeStruct(s, d) for s, d in ou...]
where the time goes in v3:
time: 226 us; the launch traced here: 225 us
  blocking collectives  182 us (81%)
  Pallas kernels  33.8 us (15%)
  local copies, waits for them, and re-layouts  3.97 us (2%)
  starting transfers between devices  3.55 us (2%)
    all_to_all x9, blocking collectives, exchanged(): return lax.all_to_all(x, axis, split_axis=0, concat_axis=0, tiled=True)  165 us
    pallas_call x12, Pallas kernels, call(): pl.pallas_call(body, out_shape=[jax.ShapeDtypeStruct(s, d) for s, d in ou...  33.8 us
    all_gather x1, blocking collectives, per_device(): gathered = lax.all_gather(own, TERM)  17.8 us
  transfers between devices with their start and end apart: 1, of which 0 were waited for; matrix products, arithmetic and copies ran while one was open for 0% of the time, Pallas kernels for 0%

profile of v3, /device:TPU:1, one launch (start us, length us, event | category | flops | bytes accessed | tf_op | source)
XLA Modules:
  0.0 225.2 jit_solution(9182021457252071746)
XLA Ops:
  1.3 0.1 add_bitcast_fusion.place
  1.4 0.0 copy-start
  1.4 1.4 copy-done
  2.8 0.0 copy-start.2
  2.8 1.2 copy-done.2
  4.0 0.0 copy-start.5
  4.0 0.7 copy-done.5
  4.7 0.0 copy-start.7
  4.7 0.7 copy-done.7
  5.3 0.0 copy-start.1
  5.3 0.0 copy-start.6
  5.3 1.9 shard_map.84
  7.3 15.1 %all_to_all.50.got.refs_5_ = f32[16,24,128]{2,1,0:T(8,128)S(1)} all-to-all(f32[16,24,128]{2,1,0:T(8,128)S(1)} %get-tuple-element.20), channel_id=1, replica_groups=mesh['term_0'=8,'term_1'=2,'doc_0'=4,'doc_1'=4] {'doc_0','doc_1'}, dimensions={0} | all-to-all | bytes 393216 | tf_op jit(solution)/shard_map/all_to_all | solution.py:322
  22.4 0.0 copy-done.1
  22.4 0.0 copy-done.6
  22.4 0.0 copy-start.8
  22.4 1.8 shard_map.85
  24.1 19.3 %all_to_all.51.got = f32[16,16,128]{2,1,0:T(8,128)S(1)} all-to-all(f32[16,16,128]{2,1,0:T(8,128)S(1)} %get-tuple-element.21), channel_id=1, replica_groups=mesh['term_0'=8,'term_1'=2,'doc_0'=4,'doc_1'=4] {'term_0','term_1'}, dimensions={0} | all-to-all | bytes 262144 | tf_op jit(solution)/shard_map/all_to_all | solution.py:322
  43.5 0.0 copy-done.8
  43.5 2.0 shard_map.86
  45.4 0.0 copy-start.3
  45.4 11.5 %all_to_all.52.got = f32[16,16,128]{2,1,0:T(8,128)S(1)} all-to-all(f32[16,16,128]{2,1,0:T(8,128)S(1)} %get-tuple-element.22), channel_id=1, replica_groups=mesh['term_0'=8,'term_1'=2,'doc_0'=4,'doc_1'=4] {'doc_0','doc_1'}, dimensions={0} | all-to-all | bytes 262144 | tf_op jit(solution)/shard_map/all_to_all | solution.py:322
  57.0 1.8 shard_map.87
  58.7 12.5 %all_to_all.53.refs_4_ = f32[16,16,128]{2,1,0:T(8,128)S(1)} all-to-all(f32[16,16,128]{2,1,0:T(8,128)S(1)} %get-tuple-element.24), channel_id=1, replica_groups=mesh['term_0'=8,'term_1'=2,'doc_0'=4,'doc_1'=4] {'term_0','term_1'}, dimensions={0} | all-to-all | bytes 262144 | tf_op jit(solution)/shard_map/all_to_all | solution.py:322
  71.2 0.0 copy-done.3
  71.2 3.1 %shard_map.88 = (bf16[16,256,128]{2,1,0:T(8,128)(2,1)S(1)}, f32[16,128]{1,0:T(8,128)}) custom-call(bf16[48,128,128]{2,1,0:T(8,128)(2,1)S(1)} %copy-done.1, s32[1,48]{1,0:T(1,128)S(1)} %copy-done.6, s32[1,48]{1,0:T(1,128)S(1)} %copy-done.8, s32[1,1]{1,0:T(1,128)S(6)} %copy.9.count.refs_3_, f32[16,16,128]{2,1,0:T(8,128)S(1)} %all_to_all.53.refs_4_, ...), custom_call_target="tpu_custom_call" | custom-call | tf_op jit(solution)/shard_map/pallas_call | solution.py:28
  74.3 0.0 copy-start.4
  74.3 21.5 %all_to_all.54.got = bf16[16,256,128]{2,1,0:T(8,128)(2,1)S(1)} all-to-all(bf16[16,256,128]{2,1,0:T(8,128)(2,1)S(1)} %get-tuple-element.27), channel_id=1, replica_groups=mesh['term_0'=8,'term_1'=2,'doc_0'=4,'doc_1'=4] {'doc_0','doc_1'}, dimensions={0} | all-to-all | bytes 2097152 | tf_op jit(solution)/shard_map/all_to_all | solution.py:322
  95.8 0.0 copy-done.4
  95.8 1.1 shard_map.89
  96.9 0.0 copy-start.9
  96.9 18.9 %all_to_all.55.scaled = bf16[16,256,128]{2,1,0:T(8,128)(2,1)S(1)} all-to-all(bf16[16,256,128]{2,1,0:T(8,128)(2,1)S(1)} %get-tuple-element.28), channel_id=1, replica_groups=mesh['term_0'=8,'term_1'=2,'doc_0'=4,'doc_1'=4] {'doc_0','doc_1'}, dimensions={0} | all-to-all | bytes 2097152 | tf_op jit(solution)/shard_map/all_to_all | solution.py:322
  115.8 0.0 copy-done.9
  115.8 2.5 %shard_map.90 = s16[16,272,128]{2,1,0:T(8,128)(2,1)S(1)} custom-call(bf16[48,128,128]{2,1,0:T(8,128)(2,1)S(1)} %copy-done.1, s32[1,48]{1,0:T(1,128)S(1)} %copy-done.6, s32[1,48]{1,0:T(1,128)S(1)} %copy-done.8, s32[1,1]{1,0:T(1,128)S(6)} %copy.9.count.refs_3_, bf16[16,256,128]{2,1,0:T(8,128)(2,1)S(1)} %all_to_all.55.scaled, f32[16,128]{1,0:T(8,128)S(1)} %copy-done.9), custom_call_target="tpu_custom_call" | custom-call | tf_op jit(solution)/shard_map/pallas_call | solution.py:28
  118.3 35.1 %all_to_all.56.got = s16[16,272,128]{2,1,0:T(8,128)(2,1)S(1)} all-to-all(s16[16,272,128]{2,1,0:T(8,128)(2,1)S(1)} %shard_map.90), channel_id=1, replica_groups=mesh['term_0'=8,'term_1'=2,'doc_0'=4,'doc_1'=4] {'term_0','term_1'}, dimensions={0} | all-to-all | bytes 2228224 | tf_op jit(solution)/shard_map/all_to_all | solution.py:322
  153.4 1.2 shard_map.91
  154.7 12.3 %all_to_all.57.got = f32[16,16,384]{2,1,0:T(8,128)S(1)} all-to-all(f32[16,16,384]{2,1,0:T(8,128)S(1)} %bitcast.11), channel_id=1, replica_groups=mesh['term_0'=8,'term_1'=2,'doc_0'=4,'doc_1'=4] {'doc_0','doc_1'}, dimensions={0} | all-to-all | bytes 786432 | tf_op jit(solution)/shard_map/all_to_all | solution.py:322
  167.0 18.5 %all_to_all.58.got = f32[16,16,384]{2,1,0:T(8,128)S(1)} all-to-all(f32[16,16,384]{2,1,0:T(8,128)S(1)} %shard_map.92), channel_id=1, replica_groups=mesh['term_0'=8,'term_1'=2,'doc_0'=4,'doc_1'=4] {'term_0','term_1'}, dimensions={0} | all-to-all | bytes 786432 | tf_op jit(solution)/shard_map/all_to_all | solution.py:322
  185.4 0.8 shard_map.93
  186.2 3.6 %all-to-all-start.9 = ((f32[16,16,384]{2,1,0:T(8,128)}), f32[16,16,384]{2,1,0:T(8,128)S(1)}, u32[]{:S(2)}, u32[]{:S(2)}) async-start(f32[16,16,384]{2,1,0:T(8,128)} %shard_map.93), calls=%async_computation.9 | async-start | bytes 786432 | tf_op jit(solution)/shard_map/all_to_all | solution.py:322
  189.8 17.8 %all-gather.2 = s16[4352,128]{1,0:T(8,128)(2,1)S(1)} all-gather(s16[272,128]{1,0:T(8,128)(2,1)S(1)} %get-tuple-element.32), channel_id=2, replica_groups=mesh['term_0'=8,'term_1'=2,'doc_0'=4,'doc_1'=4] {'term_0','term_1'}, dimensions={0}, use_global_device_ids=true | all-gather | bytes 1183744 | tf_op jit(solution)/shard_map/all_gather | solution.py:358
  207.6 0.0 all-to-all-done.9
  207.6 12.0 %shard_map.94 = (f32[2,256,256]{2,1,0:T(8,128)S(1)}, f32[256,128]{1,0:T(8,128)S(1)}) custom-call(f32[256,384]{1,0:T(8,128)S(1)} %bitcast.10), custom_call_target="tpu_custom_call" | custom-call | tf_op jit(solution)/shard_map/pallas_call | solution.py:28
  219.6 5.6 %shard_map.95 = (bf16[2048,256]{1,0:T(8,128)(2,1)}, bf16[2048,256]{1,0:T(8,128)(2,1)}) custom-call(f32[2,256,256]{2,1,0:T(8,128)S(1)} %get-tuple-element.31.inverse, bf16[16,256,128]{2,1,0:T(8,128)(2,1)S(1)} %all_to_all.55.scaled, f32[16,128]{1,0:T(8,128)S(1)} %copy-done.4, s16[16,272,128]{2,1,0:T(8,128)(2,1)S(1)} %bitcast.9, ...), custom_call_target="tpu_custom_call" | custom-call | tf_op jit(solution)/shard_map/pallas_call | solution.py:28
  (1 shorter events, 0.0 us)
Async XLA Ops:
  1.4 1.4 copy-start
  2.8 1.2 copy-start.2
  4.0 0.7 copy-start.5
  4.7 0.7 copy-start.7
  5.3 17.1 %copy-start.1 = (bf16[48,128,128]{2,1,0:T(8,128)(2,1)S(1)}, bf16[48,128,128]{2,1,0:T(8,128)(2,1)}, u32[]{:S(2)}) copy-start(bf16[48,128,128]{2,1,0:T(8,128)(2,1)} %values.9) | copy-start | bytes 4718596
  5.3 17.1 %copy-start.6 = (s32[1,48]{1,0:T(1,128)S(1)}, s32[1,48]{1,0:T(1,128)}, u32[]{:S(2)}) copy-start(s32[1,48]{1,0:T(1,128)} %rows.9) | copy-start | bytes 580
  22.4 21.1 %copy-start.8 = (s32[1,48]{1,0:T(1,128)S(1)}, s32[1,48]{1,0:T(1,128)}, u32[]{:S(2)}) copy-start(s32[1,48]{1,0:T(1,128)} %cols.9) | copy-start | bytes 580
  45.4 25.8 %copy-start.3 = (bf16[2048,256]{1,0:T(8,128)(2,1)S(1)}, bf16[2048,256]{1,0:T(8,128)(2,1)}, u32[]{:S(2)}) copy-start(bf16[2048,256]{1,0:T(8,128)(2,1)} %refs_6_.1) | copy-start | bytes 3145732
  74.3 21.5 %copy-start.4 = (f32[16,128]{1,0:T(8,128)S(1)}, f32[16,128]{1,0:T(8,128)}, u32[]{:S(2)}) copy-start(f32[16,128]{1,0:T(8,128)} %get-tuple-element.23.row_scale) | copy-start | bytes 24580
  96.9 18.9 %copy-start.9 = (f32[16,128]{1,0:T(8,128)S(1)}, f32[16,128]{1,0:T(8,128)}, u32[]{:S(2)}) copy-start(f32[16,128]{1,0:T(8,128)} %get-tuple-element.25.col_scale) | copy-start | bytes 24580
  186.2 21.4 %all-to-all-start.9 = ((f32[16,16,384]{2,1,0:T(8,128)}), f32[16,16,384]{2,1,0:T(8,128)S(1)}, u32[]{:S(2)}, u32[]{:S(2)}) async-start(f32[16,16,384]{2,1,0:T(8,128)} %shard_map.93), calls=%async_computation.9 | async-start | bytes 786432 | tf_op jit(solution)/shard_map/all_to_all | solution.py:322

commit v4 on v3

--- a/solution.py
+++ b/solution.py
@@ -79,10 +79,24 @@
         out_ref[i, 0:RB, :] = vec
 
 
-def start_sums(place, values, rows, cols, count, start, out, place_out, src, acc):
-    place_out[0, 0] = place[0, 0]
-    place_out[0, 1] = place[0, 1]
+def first_rows(place, values, rows, cols, count, out, place_out, src, acc):
+    for i in range(3):
+        place_out[0, i] = place[0, i]
     put_thirds(src, jnp.ones((CB, TILE), F32), 0)
+    over_tiles(count[0, 0], values, cols, rows, src, acc, True)
+    send_vector(out, acc)
+
+
+def to_columns(values, rows, cols, count, got, out, scale, src, acc):
+    vec = 1.0 / jnp.sum(got[...], axis=0)[0:RB]
+    scale[...] = vec
+    put_thirds(src, vec, 0)
+    over_tiles(count[0, 0], values, rows, cols, src, acc, False)
+    send_vector(out, acc)
+
+
+def to_rows(values, rows, cols, count, got, start, out, src, acc):
+    put_thirds(src, 1.0 / jnp.sum(got[...], axis=0), 0)
     over_tiles(count[0, 0], values, cols, rows, src, acc, True)
     send_vector(out, acc)
     mean = jnp.sum(start[...].astype(F32), axis=0, keepdims=True)
@@ -90,22 +104,6 @@
         out[i, 16:17, :] = mean[:, :TILE]
         out[i, 17:18, :] = mean[:, TILE:]
         out[i, 18:24, :] = jnp.zeros((6, TILE), F32)
-
-
-def to_columns(values, rows, cols, count, got, out, scale, src, acc):
-    vec = 1.0 / jnp.sum(got[...], axis=0)[0:RB]
-    scale[...] = vec
-    put_thirds(src, vec, 0)
-    over_tiles(count[0, 0], values, rows, cols, src, acc, False)
-    send_vector(out, acc)
-
-
-def to_rows(values, rows, cols, count, got, out, scale, src, acc):
-    vec = 1.0 / jnp.sum(got[...], axis=0)[0:RB]
-    scale[...] = vec
-    put_thirds(src, vec, 0)
-    over_tiles(count[0, 0], values, cols, rows, src, acc, True)
-    send_vector(out, acc)
 
 
 def left_product(docs, values, rows, cols, count, got, first, start, out, scale, src, acc):
@@ -155,26 +153,43 @@
     return x.astype(jnp.int32).astype(F32)
 
 
-def steps_of(got):
-    lines = [wide(got[i, K : K + 16, :]) for i in range(16)]
+def steps_of(got, count):
+    lines = [wide(got[i, K : K + 16, :]) for i in range(count)]
     code = jnp.concatenate(
         [jnp.concatenate([x[h : h + 1] for x in lines], axis=0) for h in (0, 8)], axis=1
     ).T
     return jnp.exp2(code * (1.0 / STEPS)) * (1.0 / LEVELS)
 
 
-def right_product(values, rows, cols, count, scaled, col_scale, out, acc):
+def right_product(place, values, rows, cols, count, scaled, col_scale, keep, send, acc):
     over_tiles(count[0, 0], values, rows, cols, scaled, acc, False)
+    core = place[0, 2]
     peak = jnp.zeros((K, TILE), F32)
-    for b in range(CB):
-        part = acc[b] * col_scale[b : b + 1, :]
-        acc[b] = part
+    for i in range(CB // 2):
+        mine, its = 2 * i + core, 2 * i + 1 - core
+        keep[i] = acc[mine] * col_scale[pl.ds(mine, 1), :]
+        part = acc[its] * col_scale[pl.ds(its, 1), :]
+        acc[its] = part
         peak = jnp.maximum(peak, jnp.abs(part))
     code = code_of(jnp.max(peak, axis=1, keepdims=True))
     lines = code_lines(code)
-    for b in range(CB):
-        out[b, 0:K, :] = counted(acc[b], code)
-        out[b, K : K + 16, :] = lines
+    for i in range(CB // 2):
+        send[i, 0:K, :] = counted(acc[2 * i + 1 - core], code)
+        send[i, K : K + 16, :] = lines
+
+
+def core_sum(keep, got, out, total):
+    step = steps_of(got, 8)[:, 0:1]
+    peak = jnp.zeros((K, TILE), F32)
+    for i in range(CB // 2):
+        part = keep[i] + wide(got[i, 0:K, :]) * step
+        total[i] = part
+        peak = jnp.maximum(peak, jnp.abs(part))
+    code = code_of(jnp.max(peak, axis=1, keepdims=True))
+    lines = code_lines(code)
+    for i in range(CB // 2):
+        out[i, 0:K, :] = counted(total[i], code)
+        out[i, K : K + 16, :] = lines
 
 
 def iotas(shape=(K, K)):
@@ -182,9 +197,9 @@
 
 
 def right_rows(got, left_gram, out, own):
-    step = steps_of(got)
+    step = steps_of(got, 8)
     right = wide(got[0, 0:K, :]) * step[:, 0:1]
-    for i in range(1, 16):
+    for i in range(1, 8):
         right += wide(got[i, 0:K, :]) * step[:, i : i + 1]
     code = code_of(jnp.max(jnp.abs(right), axis=1, keepdims=True))
     own[0:K, :] = counted(right, code)
@@ -291,31 +306,34 @@
     lean_out[...] = jnp.broadcast_to(lean, lean_out.shape)
 
 
+def halves(x):
+    hi = x.astype(BF16)
+    return hi, (x - hi.astype(F32)).astype(BF16)
+
+
+def mixed(lhs, rhs):
+    return sum(jnp.dot(a, b, preferred_element_type=F32) for a, b in zip(lhs, rhs))
+
+
 def bases(inverse, scaled, row_scale, gathered, lean, left_out, right_out):
-    hi, mid, low = thirds(inverse[0])
-    for b in range(RB):
-        total = (
-            jnp.dot(hi, scaled[b], preferred_element_type=F32)
-            + jnp.dot(mid, scaled[b], preferred_element_type=F32)
-            + jnp.dot(low, scaled[b], preferred_element_type=F32)
+    hi, low = halves(inverse[0])
+    for b in range(0, RB, 2):
+        pair = jnp.concatenate([scaled[b], scaled[b + 1]], axis=1)
+        total = mixed((hi, low), (pair, pair))
+        for u in range(2):
+            basis = total[:, u * TILE : (u + 1) * TILE] / row_scale[b + u : b + u + 1, :]
+            left_out[(b + u) * TILE : (b + u + 1) * TILE, :] = basis.T.astype(BF16)
+    hi, low = halves(inverse[1])
+    step = steps_of(gathered, 16)
+    mean = lean[:, 0:1]
+    for b in range(0, CB, 2):
+        pair = jnp.concatenate(
+            [wide(gathered[b + u, 0:K, :]) * step[:, b + u : b + u + 1] - mean for u in range(2)], axis=1
         )
-        basis = total / row_scale[b : b + 1, :]
-        left_out[b * TILE : (b + 1) * TILE, :] = basis.T.astype(BF16)
-    hi, mid, low = thirds(inverse[1])
-    step = steps_of(gathered)
-    mean = lean[:, 0:1]
-    for b in range(CB):
-        block = wide(gathered[b, 0:K, :]) * step[:, b : b + 1] - mean
-        top = block.astype(BF16)
-        rest = (block - top.astype(F32)).astype(BF16)
-        total = (
-            jnp.dot(hi, top, preferred_element_type=F32)
-            + jnp.dot(mid, top, preferred_element_type=F32)
-            + jnp.dot(low, top, preferred_element_type=F32)
-            + jnp.dot(hi, rest, preferred_element_type=F32)
-            + jnp.dot(mid, rest, preferred_element_type=F32)
-        )
-        right_out[b * TILE : (b + 1) * TILE, :] = total.T.astype(BF16)
+        top, rest = halves(pair)
+        total = mixed((hi, low, hi), (top, top, rest))
+        for u in range(2):
+            right_out[(b + u) * TILE : (b + u + 1) * TILE, :] = total[:, u * TILE : (u + 1) * TILE].T.astype(BF16)
 
 
 def exchanged(x, axis):
@@ -325,18 +343,16 @@
 def per_device(tile_values, tile_rows, tile_cols, tile_count, start_block):
     terms = float(RB * TILE * lax.axis_size(TERM))
     docs = float(CB * TILE * lax.axis_size(DOC))
-    place = jnp.stack([lax.axis_index(TERM), lax.axis_index(DOC)]).astype(jnp.int32)[None]
+    place = jnp.stack([lax.axis_index(TERM), lax.axis_index(DOC), lax.axis_index("term_1")]).astype(jnp.int32)[None]
     tiles = (tile_values, tile_rows, tile_cols, tile_count)
     vec = [((RB, 16, TILE), BF16), ((RB, 16, TILE), F32)]
     vector = ((16, RB, TILE), F32)
     scale = ((RB, TILE), F32)
-    part, place = call(
-        start_sums, (place, *tiles, start_block), [((16, 24, TILE), F32), ((1, 2), jnp.int32)], vec
-    )
+    part, place = call(first_rows, (place, *tiles), [vector, ((1, 3), jnp.int32)], vec)
+    part, _ = call(to_columns, (*tiles, exchanged(part, DOC)), [vector, scale], vec)
+    (part,) = call(to_rows, (*tiles, exchanged(part, TERM), start_block), [((16, 24, TILE), F32)], vec)
     first = exchanged(part, DOC)
-    part, _ = call(to_columns, (*tiles, first), [vector, scale], vec)
-    part, _ = call(to_rows, (*tiles, exchanged(part, TERM)), [vector, scale], vec)
-    part, row_scale = call(to_columns, (*tiles, exchanged(part, DOC)), [vector, scale], vec)
+    part, row_scale = call(to_columns, (*tiles, first), [vector, scale], vec)
     part, col_scale = call(
         lambda *refs: left_product(docs, *refs),
         (*tiles, exchanged(part, TERM), first, start_block),
@@ -347,12 +363,18 @@
         left_rows, (place, exchanged(part, DOC), row_scale), [((16, K, TILE), BF16), ((K, K), F32)]
     )
     scaled = exchanged(part, DOC)
-    (part,) = call(
-        right_product, (*tiles, scaled, col_scale), [((CB, K + 16, TILE), jnp.int16)], [((CB, K, TILE), F32)]
-    )
+    half = (CB // 2, K + 16, TILE)
+    keep, part = call(
+        right_product,
+        (place, *tiles, scaled, col_scale),
+        [((CB // 2, K, TILE), F32), (half, jnp.int16)],
+        [((CB, K, TILE), F32)],
+    )
+    part = lax.ppermute(part, "term_1", [(0, 1), (1, 0)])
+    (part,) = call(core_sum, (keep, part), [(half, jnp.int16)], [((CB // 2, K, TILE), F32)])
     part, own = call(
         right_rows,
-        (exchanged(part, TERM), left_gram),
+        (exchanged(part, "term_0"), left_gram),
         [((K, 3 * TILE), F32), ((K + 16, TILE), jnp.int16)],
     )
     gathered = lax.all_gather(own, TERM)

time: 226 us -> 211 us (0.934)
  blocking collectives: 182 us -> 165 us
    all_to_all x9, blocking collectives: 165 us -> 147 us  [exchanged(): return lax.all_to_all(x, axis, split_axis=0, concat_axis=0, tiled=True)]
    pallas_call x12 -> x13, Pallas kernels: 33.8 us -> 32.4 us  [call(): pl.pallas_call(body, out_shape=[jax.ShapeDtypeStruct(s, d) for s, d in ou...]
  transfers between devices with their start and end apart: 1 -> 2, of which waited for: 0 -> 1; matrix products, arithmetic and copies ran while one was open for 0% -> 0% of each run, Pallas kernels for 0% -> 0%
where the time goes in v4:
time: 211 us; the launch traced here: 209 us
  blocking collectives  165 us (78%)
  Pallas kernels  32.4 us (15%)
  starting transfers between devices  5.52 us (3%)
  local copies, waits for them, and re-layouts  2.75 us (1%)
    all_to_all x9, blocking collectives, exchanged(): return lax.all_to_all(x, axis, split_axis=0, concat_axis=0, tiled=True)  147 us
    pallas_call x13, Pallas kernels, call(): pl.pallas_call(body, out_shape=[jax.ShapeDtypeStruct(s, d) for s, d in ou...  32.4 us
    all_gather x1, blocking collectives, per_device(): gathered = lax.all_gather(own, TERM)  17.8 us
  transfers between devices with their start and end apart: 2, of which 1 were waited for; matrix products, arithmetic and copies ran while one was open for 0% of the time, Pallas kernels for 0%

profile of v4, /device:TPU:1, one launch (start us, length us, event | category | flops | bytes accessed | tf_op | source)
XLA Modules:
  0.0 208.9 jit_solution(11026745860066313530)
XLA Ops:
  0.6 0.0 copy-start.7
  0.6 0.0 copy-start.5
  1.3 0.1 add_bitcast_fusion.place
  1.4 0.0 copy-start
  1.4 1.4 copy-done
  2.8 0.0 copy-start.4
  2.8 0.7 copy-done.4
  3.5 0.0 copy-start.6
  3.5 0.7 copy-done.6
  4.1 0.0 copy-start.1
  4.1 0.0 copy-start.2
  4.1 2.2 %shard_map.84 = (f32[16,16,128]{2,1,0:T(8,128)S(1)}, s32[1,3]{1,0:T(1,128)S(1)}) custom-call(s32[1,3]{1,0:T(1,128)S(1)} %add_bitcast_fusion.place, bf16[48,128,128]{2,1,0:T(8,128)(2,1)S(1)} %copy-done, s32[1,48]{1,0:T(1,128)S(1)} %copy-done.4, s32[1,48]{1,0:T(1,128)S(1)} %copy-done.6, s32[1,1]{1,0:T(1,128)S(6)} %copy.9.count.refs_3_), custom_call_target="tpu_custom_call" | custom-call | tf_op jit(solution)/shard_map/pallas_call | solution.py:28
  6.3 14.0 %all_to_all.50.got = f32[16,16,128]{2,1,0:T(8,128)S(1)} all-to-all(f32[16,16,128]{2,1,0:T(8,128)S(1)} %get-tuple-element.21), channel_id=1, replica_groups=mesh['term_0'=8,'term_1'=2,'doc_0'=4,'doc_1'=4] {'doc_0','doc_1'}, dimensions={0} | all-to-all | bytes 262144 | tf_op jit(solution)/shard_map/all_to_all | solution.py:340
  20.3 0.0 copy-done.7
  20.3 0.0 copy-done.5
  20.3 0.0 copy-done.1
  20.3 2.0 shard_map.85
  22.3 19.6 %all_to_all.51.got = f32[16,16,128]{2,1,0:T(8,128)S(1)} all-to-all(f32[16,16,128]{2,1,0:T(8,128)S(1)} %get-tuple-element.22), channel_id=1, replica_groups=mesh['term_0'=8,'term_1'=2,'doc_0'=4,'doc_1'=4] {'term_0','term_1'}, dimensions={0} | all-to-all | bytes 262144 | tf_op jit(solution)/shard_map/all_to_all | solution.py:340
  41.9 0.0 copy-done.2
  41.9 1.9 shard_map.86
  43.8 10.6 %all_to_all.52.got.refs_5_ = f32[16,24,128]{2,1,0:T(8,128)S(1)} all-to-all(f32[16,24,128]{2,1,0:T(8,128)S(1)} %shard_map.86), channel_id=1, replica_groups=mesh['term_0'=8,'term_1'=2,'doc_0'=4,'doc_1'=4] {'doc_0','doc_1'}, dimensions={0} | all-to-all | bytes 393216 | tf_op jit(solution)/shard_map/all_to_all | solution.py:340
  54.4 2.0 shard_map.87
  56.4 12.7 %all_to_all.53.refs_4_ = f32[16,16,128]{2,1,0:T(8,128)S(1)} all-to-all(f32[16,16,128]{2,1,0:T(8,128)S(1)} %get-tuple-element.24), channel_id=1, replica_groups=mesh['term_0'=8,'term_1'=2,'doc_0'=4,'doc_1'=4] {'term_0','term_1'}, dimensions={0} | all-to-all | bytes 262144 | tf_op jit(solution)/shard_map/all_to_all | solution.py:340
  69.1 3.6 %shard_map.88 = (bf16[16,256,128]{2,1,0:T(8,128)(2,1)S(1)}, f32[16,128]{1,0:T(8,128)}) custom-call(bf16[48,128,128]{2,1,0:T(8,128)(2,1)S(1)} %copy-done.1, s32[1,48]{1,0:T(1,128)S(1)} %copy-done.5, s32[1,48]{1,0:T(1,128)S(1)} %copy-done.7, s32[1,1]{1,0:T(1,128)S(6)} %copy.9.count.refs_3_, f32[16,16,128]{2,1,0:T(8,128)S(1)} %all_to_all.53.refs_4_, ...), custom_call_target="tpu_custom_call" | custom-call | tf_op jit(solution)/shard_map/pallas_call | solution.py:28
  72.7 0.0 copy-start.3
  72.7 19.4 %all_to_all.54.got = bf16[16,256,128]{2,1,0:T(8,128)(2,1)S(1)} all-to-all(bf16[16,256,128]{2,1,0:T(8,128)(2,1)S(1)} %get-tuple-element.27), channel_id=1, replica_groups=mesh['term_0'=8,'term_1'=2,'doc_0'=4,'doc_1'=4] {'doc_0','doc_1'}, dimensions={0} | all-to-all | bytes 2097152 | tf_op jit(solution)/shard_map/all_to_all | solution.py:340
  92.1 0.0 copy-done.3
  92.1 0.0 copy-start.8
  92.1 1.1 shard_map.89
  93.2 18.9 %all_to_all.55.scaled = bf16[16,256,128]{2,1,0:T(8,128)(2,1)S(1)} all-to-all(bf16[16,256,128]{2,1,0:T(8,128)(2,1)S(1)} %get-tuple-element.28), channel_id=1, replica_groups=mesh['term_0'=8,'term_1'=2,'doc_0'=4,'doc_1'=4] {'doc_0','doc_1'}, dimensions={0} | all-to-all | bytes 2097152 | tf_op jit(solution)/shard_map/all_to_all | solution.py:340
  112.1 0.0 copy-done.8
  112.1 2.4 %shard_map.90 = (f32[8,256,128]{2,1,0:T(8,128)S(1)}, s16[8,272,128]{2,1,0:T(8,128)(2,1)S(1)}) custom-call(s32[1,3]{1,0:T(1,128)S(1)} %get-tuple-element.26.place, bf16[48,128,128]{2,1,0:T(8,128)(2,1)S(1)} %copy-done.1, s32[1,48]{1,0:T(1,128)S(1)} %copy-done.5, s32[1,48]{1,0:T(1,128)S(1)} %copy-done.7, s32[1,1]{1,0:T(1,128)S(6)} %copy.9.count.refs_3_, ...), custom_call_target="tpu_custom_call" | custom-call | tf_op jit(solution)/shard_map/pallas_call | solution.py:28
  114.5 2.0 collective-permute-start
  116.5 1.6 collective-permute-done.got
  118.1 0.6 shard_map.91
  118.7 20.7 %all_to_all.56.got = s16[8,272,128]{2,1,0:T(8,128)(2,1)S(1)} all-to-all(s16[8,272,128]{2,1,0:T(8,128)(2,1)S(1)} %shard_map.91), channel_id=1, replica_groups=mesh['term_0'=8,'term_1'=2,'doc_0'=4,'doc_1'=4] {'term_0'}, dimensions={0} | all-to-all | bytes 1114112 | tf_op jit(solution)/shard_map/all_to_all | solution.py:340
  139.5 1.0 shard_map.92
  140.5 11.6 %all_to_all.57.got = f32[16,16,384]{2,1,0:T(8,128)S(1)} all-to-all(f32[16,16,384]{2,1,0:T(8,128)S(1)} %bitcast.12), channel_id=1, replica_groups=mesh['term_0'=8,'term_1'=2,'doc_0'=4,'doc_1'=4] {'doc_0','doc_1'}, dimensions={0} | all-to-all | bytes 786432 | tf_op jit(solution)/shard_map/all_to_all | solution.py:340
  152.2 19.8 %all_to_all.58.got = f32[16,16,384]{2,1,0:T(8,128)S(1)} all-to-all(f32[16,16,384]{2,1,0:T(8,128)S(1)} %shard_map.93), channel_id=1, replica_groups=mesh['term_0'=8,'term_1'=2,'doc_0'=4,'doc_1'=4] {'term_0','term_1'}, dimensions={0} | all-to-all | bytes 786432 | tf_op jit(solution)/shard_map/all_to_all | solution.py:340
  171.9 0.8 shard_map.94
  172.7 3.6 %all-to-all-start.9 = ((f32[16,16,384]{2,1,0:T(8,128)}), f32[16,16,384]{2,1,0:T(8,128)S(1)}, u32[]{:S(2)}, u32[]{:S(2)}) async-start(f32[16,16,384]{2,1,0:T(8,128)} %shard_map.94), calls=%async_computation.9 | async-start | bytes 786432 | tf_op jit(solution)/shard_map/all_to_all | solution.py:340
  176.3 17.8 %all-gather.2 = s16[4352,128]{1,0:T(8,128)(2,1)S(1)} all-gather(s16[272,128]{1,0:T(8,128)(2,1)S(1)} %get-tuple-element.34), channel_id=2, replica_groups=mesh['term_0'=8,'term_1'=2,'doc_0'=4,'doc_1'=4] {'term_0','term_1'}, dimensions={0}, use_global_device_ids=true | all-gather | bytes 1183744 | tf_op jit(solution)/shard_map/all_gather | solution.py:380
  194.1 0.0 all-to-all-done.9
  194.1 12.0 %shard_map.95 = (f32[2,256,256]{2,1,0:T(8,128)S(1)}, f32[256,128]{1,0:T(8,128)S(1)}) custom-call(f32[256,384]{1,0:T(8,128)S(1)} %bitcast.11), custom_call_target="tpu_custom_call" | custom-call | tf_op jit(solution)/shard_map/pallas_call | solution.py:28
  206.1 2.8 %shard_map.96 = (bf16[2048,256]{1,0:T(8,128)(2,1)}, bf16[2048,256]{1,0:T(8,128)(2,1)}) custom-call(f32[2,256,256]{2,1,0:T(8,128)S(1)} %get-tuple-element.33.inverse, bf16[16,256,128]{2,1,0:T(8,128)(2,1)S(1)} %all_to_all.55.scaled, f32[16,128]{1,0:T(8,128)S(1)} %copy-done.3, s16[16,272,128]{2,1,0:T(8,128)(2,1)S(1)} %bitcast.10, ...), custom_call_target="tpu_custom_call" | custom-call | tf_op jit(solution)/shard_map/pallas_call | solution.py:28
  (1 shorter events, 0.0 us)
Async XLA Ops:
  0.6 19.7 %copy-start.7 = (s32[1,48]{1,0:T(1,128)S(1)}, s32[1,48]{1,0:T(1,128)}, u32[]{:S(2)}) copy-start(s32[1,48]{1,0:T(1,128)} %cols.9) | copy-start | bytes 580
  0.6 19.7 %copy-start.5 = (s32[1,48]{1,0:T(1,128)S(1)}, s32[1,48]{1,0:T(1,128)}, u32[]{:S(2)}) copy-start(s32[1,48]{1,0:T(1,128)} %rows.9) | copy-start | bytes 580
  1.4 1.4 copy-start
  2.8 0.7 copy-start.4
  3.5 0.7 copy-start.6
  4.1 16.2 %copy-start.1 = (bf16[48,128,128]{2,1,0:T(8,128)(2,1)S(1)}, bf16[48,128,128]{2,1,0:T(8,128)(2,1)}, u32[]{:S(2)}) copy-start(bf16[48,128,128]{2,1,0:T(8,128)(2,1)} %values.9) | copy-start | bytes 4718596
  4.1 37.8 %copy-start.2 = (bf16[2048,256]{1,0:T(8,128)(2,1)S(1)}, bf16[2048,256]{1,0:T(8,128)(2,1)}, u32[]{:S(2)}) copy-start(bf16[2048,256]{1,0:T(8,128)(2,1)} %refs_6_.1) | copy-start | bytes 3145732
  72.7 19.4 %copy-start.3 = (f32[16,128]{1,0:T(8,128)S(1)}, f32[16,128]{1,0:T(8,128)}, u32[]{:S(2)}) copy-start(f32[16,128]{1,0:T(8,128)} %get-tuple-element.23.row_scale) | copy-start | bytes 24580
  92.1 20.0 %copy-start.8 = (f32[16,128]{1,0:T(8,128)S(1)}, f32[16,128]{1,0:T(8,128)}, u32[]{:S(2)}) copy-start(f32[16,128]{1,0:T(8,128)} %get-tuple-element.25.col_scale) | copy-start | bytes 24580
  114.5 3.6 %collective-permute-start = (s16[8,272,128]{2,1,0:T(8,128)(2,1)S(1)}, s16[8,272,128]{2,1,0:T(8,128)(2,1)S(1)}, u32[]{:S(2)}, u32[]{:S(2)}) collective-permute-start(s16[8,272,128]{2,1,0:T(8,128)(2,1)S(1)} %get-tuple-element.30), channel_id=1, source_target_pairs={{0,16},{16,0},{1,17},{17,1},{2,18},{18,2},{3,19},{19,3},{4,20},{20... | collective-permute-start | bytes 1671176 | tf_op jit(solution)/shard_map/ppermute | solution.py:373
  172.7 21.4 %all-to-all-start.9 = ((f32[16,16,384]{2,1,0:T(8,128)}), f32[16,16,384]{2,1,0:T(8,128)S(1)}, u32[]{:S(2)}, u32[]{:S(2)}) async-start(f32[16,16,384]{2,1,0:T(8,128)} %shard_map.94), calls=%async_computation.9 | async-start | bytes 786432 | tf_op jit(solution)/shard_map/all_to_all | solution.py:340

commit v5 on v4

--- a/solution.py
+++ b/solution.py
@@ -15,7 +15,7 @@
 PANEL = 64
 TERM = ("term_0", "term_1")
 DOC = ("doc_0", "doc_1")
-ALL = TERM + DOC
+PLANE = ("term_1",) + DOC
 F32 = jnp.float32
 BF16 = jnp.bfloat16
 PRECISE = lax.Precision.HIGHEST
@@ -217,7 +217,7 @@
 
 def sum_all(got, out):
     total = jnp.sum(got[...], axis=0)
-    for i in range(16):
+    for i in range(out.shape[0]):
         out[i] = total
 
 
@@ -260,9 +260,14 @@
     return blocks
 
 
+def precise(lhs, rhs, contract=1):
+    return lax.dot_general(lhs, rhs, (((contract,), (0,)), ((), ())), precision=PRECISE, preferred_element_type=F32)
+
+
 def factor(work):
     lane = lax.broadcasted_iota(jnp.int32, (2, PANEL, TILE), 2)
     line = lax.broadcasted_iota(jnp.int32, (2, PANEL, TILE), 1)
+    own = work[:, 0:PANEL, 0:TILE]
     for start in range(0, K, PANEL):
         first = (start // TILE) * TILE
         span = slice(first, first + 3 * TILE)
@@ -271,20 +276,22 @@
         other = PANEL - at
         unit = jnp.where(lane == line + other, 1.0, 0.0)
         here = (lane >= at) & (lane < at + PANEL)
-        block = jnp.where(here, work[:, start:end, first : first + TILE], unit)
+        block = jnp.where(here, own, unit)
         done = jnp.concatenate(eliminate([block[:, 8 * j : 8 * j + 8] for j in range(PANEL // 8)], at), axis=1)
+        inverses = [done[m, :, other : other + PANEL] for m in range(2)]
+        if end < K:
+            then = (end // TILE) * TILE
+            ahead = []
+            for m in range(2):
+                upper = precise(inverses[m], work[m, start:end, then : then + TILE])
+                cut = upper[:, end - then : end - then + PANEL]
+                ahead.append(work[m, end : end + PANEL, then : then + TILE] - precise(cut, upper, 0))
+            own = jnp.stack(ahead)
         for m in range(2):
-            inverse = done[m, :, other : other + PANEL]
-            panel = jnp.dot(inverse, work[m, start:end, span], precision=PRECISE, preferred_element_type=F32)
+            panel = precise(inverses[m], work[m, start:end, span])
             work[m, start:end, span] = panel
             if end < K:
-                work[m, end:K, span] -= lax.dot_general(
-                    panel[:, end - first : K - first],
-                    panel,
-                    (((0,), (0,)), ((), ())),
-                    precision=PRECISE,
-                    preferred_element_type=F32,
-                )
+                work[m, end:K, span] -= precise(panel[:, end - first : K - first], panel, 0)
 
 
 def finish(terms, docs, grams, inverse, lean_out, work):
@@ -378,11 +385,10 @@
         [((K, 3 * TILE), F32), ((K + 16, TILE), jnp.int16)],
     )
     gathered = lax.all_gather(own, TERM)
-    spread = [((16, 16, 3 * TILE), F32)]
-    part = exchanged(part.reshape(16, 16, 3 * TILE), DOC)
-    (part,) = call(sum_all, (part,), spread)
-    (part,) = call(sum_all, (exchanged(part, TERM),), spread)
-    grams = exchanged(part, DOC).reshape(K, 3 * TILE)
+    part = exchanged(part.reshape(32, 8, 3 * TILE), PLANE)
+    (part,) = call(sum_all, (part,), [((8, 8, 3 * TILE), F32)])
+    (part,) = call(sum_all, (exchanged(part, "term_0"),), [((32, 8, 3 * TILE), F32)])
+    grams = exchanged(part, PLANE).reshape(K, 3 * TILE)
     inverse, lean = call(
         lambda *refs: finish(terms, docs, *refs),
         (grams,),

time: 211 us -> 204 us (0.967); the launches traced: 209 us -> 204 us
  blocking collectives: 165 us -> 160 us
  starting transfers between devices: 5.52 us -> 8.69 us
  Pallas kernels: 32.4 us -> 29.7 us
    all_to_all x9, blocking collectives: 147 us -> 142 us  [exchanged(): return lax.all_to_all(x, axis, split_axis=0, concat_axis=0, tiled=True)]
    pallas_call x13, Pallas kernels: 32.4 us -> 29.7 us  [call(): pl.pallas_call(body, out_shape=[jax.ShapeDtypeStruct(s, d) for s, d in ou...]
    all_to_all x1, starting transfers between devices: 3.55 us -> 5.91 us  [exchanged(): return lax.all_to_all(x, axis, split_axis=0, concat_axis=0, tiled=True)]
where the time goes in v5:
time: 204 us
  blocking collectives  160 us (78%)
  Pallas kernels  29.7 us (15%)
  starting transfers between devices  8.69 us (4%)
  local copies, waits for them, and re-layouts  2.75 us (1%)
    all_to_all x9, blocking collectives, exchanged(): return lax.all_to_all(x, axis, split_axis=0, concat_axis=0, tiled=True)  142 us
    pallas_call x13, Pallas kernels, call(): pl.pallas_call(body, out_shape=[jax.ShapeDtypeStruct(s, d) for s, d in ou...  29.7 us
    all_gather x1, blocking collectives, per_device(): gathered = lax.all_gather(own, TERM)  18.1 us
    all_to_all x1, starting transfers between devices, exchanged(): return lax.all_to_all(x, axis, split_axis=0, concat_axis=0, tiled=True)  5.91 us
  transfers between devices with their start and end apart: 2, of which 1 were waited for; matrix products, arithmetic and copies ran while one was open for 0% of the time, Pallas kernels for 0%

profile of v5, /device:TPU:1, one launch (start us, length us, event | category | flops | bytes accessed | tf_op | source)
XLA Modules:
  0.0 204.0 jit_solution(5496495443657781853)
XLA Ops:
  0.6 0.0 copy-start.7
  0.6 0.0 copy-start.5
  1.3 0.1 add_bitcast_fusion.place
  1.4 0.0 copy-start
  1.4 1.4 copy-done
  2.8 0.0 copy-start.4
  2.8 0.7 copy-done.4
  3.5 0.0 copy-start.6
  3.5 0.7 copy-done.6
  4.1 0.0 copy-start.1
  4.1 0.0 copy-start.2
  4.1 1.9 shard_map.84
  6.1 14.1 %all_to_all.50.got = f32[16,16,128]{2,1,0:T(8,128)S(1)} all-to-all(f32[16,16,128]{2,1,0:T(8,128)S(1)} %get-tuple-element.21), channel_id=1, replica_groups=mesh['term_0'=8,'term_1'=2,'doc_0'=4,'doc_1'=4] {'doc_0','doc_1'}, dimensions={0} | all-to-all | bytes 262144 | tf_op jit(solution)/shard_map/all_to_all | solution.py:347
  20.1 0.0 copy-done.7
  20.1 0.0 copy-done.5
  20.1 0.0 copy-done.1
  20.1 1.8 shard_map.85
  21.9 20.4 %all_to_all.51.got = f32[16,16,128]{2,1,0:T(8,128)S(1)} all-to-all(f32[16,16,128]{2,1,0:T(8,128)S(1)} %get-tuple-element.22), channel_id=1, replica_groups=mesh['term_0'=8,'term_1'=2,'doc_0'=4,'doc_1'=4] {'term_0','term_1'}, dimensions={0} | all-to-all | bytes 262144 | tf_op jit(solution)/shard_map/all_to_all | solution.py:347
  42.3 0.0 copy-done.2
  42.3 1.7 shard_map.86
  44.0 10.7 %all_to_all.52.got.refs_5_ = f32[16,24,128]{2,1,0:T(8,128)S(1)} all-to-all(f32[16,24,128]{2,1,0:T(8,128)S(1)} %shard_map.86), channel_id=1, replica_groups=mesh['term_0'=8,'term_1'=2,'doc_0'=4,'doc_1'=4] {'doc_0','doc_1'}, dimensions={0} | all-to-all | bytes 393216 | tf_op jit(solution)/shard_map/all_to_all | solution.py:347
  54.7 1.8 shard_map.87
  56.4 13.6 %all_to_all.53.refs_4_ = f32[16,16,128]{2,1,0:T(8,128)S(1)} all-to-all(f32[16,16,128]{2,1,0:T(8,128)S(1)} %get-tuple-element.24), channel_id=1, replica_groups=mesh['term_0'=8,'term_1'=2,'doc_0'=4,'doc_1'=4] {'term_0','term_1'}, dimensions={0} | all-to-all | bytes 262144 | tf_op jit(solution)/shard_map/all_to_all | solution.py:347
  70.0 3.1 %shard_map.88 = (bf16[16,256,128]{2,1,0:T(8,128)(2,1)S(1)}, f32[16,128]{1,0:T(8,128)}) custom-call(bf16[48,128,128]{2,1,0:T(8,128)(2,1)S(1)} %copy-done.1, s32[1,48]{1,0:T(1,128)S(1)} %copy-done.5, s32[1,48]{1,0:T(1,128)S(1)} %copy-done.7, s32[1,1]{1,0:T(1,128)S(6)} %copy.9.count.refs_3_, f32[16,16,128]{2,1,0:T(8,128)S(1)} %all_to_all.53.refs_4_, ...), custom_call_target="tpu_custom_call" | custom-call | tf_op jit(solution)/shard_map/pallas_call | solution.py:28
  73.1 0.0 copy-start.3
  73.1 19.0 %all_to_all.54.got = bf16[16,256,128]{2,1,0:T(8,128)(2,1)S(1)} all-to-all(bf16[16,256,128]{2,1,0:T(8,128)(2,1)S(1)} %get-tuple-element.27), channel_id=1, replica_groups=mesh['term_0'=8,'term_1'=2,'doc_0'=4,'doc_1'=4] {'doc_0','doc_1'}, dimensions={0} | all-to-all | bytes 2097152 | tf_op jit(solution)/shard_map/all_to_all | solution.py:347
  92.1 0.0 copy-done.3
  92.1 0.0 copy-start.8
  92.1 1.1 shard_map.89
  93.2 19.0 %all_to_all.55.scaled = bf16[16,256,128]{2,1,0:T(8,128)(2,1)S(1)} all-to-all(bf16[16,256,128]{2,1,0:T(8,128)(2,1)S(1)} %get-tuple-element.28), channel_id=1, replica_groups=mesh['term_0'=8,'term_1'=2,'doc_0'=4,'doc_1'=4] {'doc_0','doc_1'}, dimensions={0} | all-to-all | bytes 2097152 | tf_op jit(solution)/shard_map/all_to_all | solution.py:347
  112.2 0.0 copy-done.8
  112.2 2.1 %shard_map.90 = (f32[8,256,128]{2,1,0:T(8,128)S(1)}, s16[8,272,128]{2,1,0:T(8,128)(2,1)S(1)}) custom-call(s32[1,3]{1,0:T(1,128)S(1)} %get-tuple-element.26.place, bf16[48,128,128]{2,1,0:T(8,128)(2,1)S(1)} %copy-done.1, s32[1,48]{1,0:T(1,128)S(1)} %copy-done.5, s32[1,48]{1,0:T(1,128)S(1)} %copy-done.7, s32[1,1]{1,0:T(1,128)S(6)} %copy.9.count.refs_3_, ...), custom_call_target="tpu_custom_call" | custom-call | tf_op jit(solution)/shard_map/pallas_call | solution.py:28
  114.4 2.8 %collective-permute-start = (s16[8,272,128]{2,1,0:T(8,128)(2,1)S(1)}, s16[8,272,128]{2,1,0:T(8,128)(2,1)S(1)}, u32[]{:S(2)}, u32[]{:S(2)}) collective-permute-start(s16[8,272,128]{2,1,0:T(8,128)(2,1)S(1)} %get-tuple-element.30), channel_id=1, source_target_pairs={{0,16},{16,0},{1,17},{17,1},{2,18},{18,2},{3,19},{19,3},{4,20},{20... | collective-permute-start | bytes 1671176 | tf_op jit(solution)/shard_map/ppermute | solution.py:380
  117.1 1.6 collective-permute-done.got
  118.7 0.6 shard_map.91
  119.4 20.4 %all_to_all.56.got = s16[8,272,128]{2,1,0:T(8,128)(2,1)S(1)} all-to-all(s16[8,272,128]{2,1,0:T(8,128)(2,1)S(1)} %shard_map.91), channel_id=1, replica_groups=mesh['term_0'=8,'term_1'=2,'doc_0'=4,'doc_1'=4] {'term_0'}, dimensions={0} | all-to-all | bytes 1114112 | tf_op jit(solution)/shard_map/all_to_all | solution.py:347
  139.7 1.0 shard_map.92
  140.8 14.6 %all_to_all.57.got = f32[32,8,384]{2,1,0:T(8,128)S(1)} all-to-all(f32[32,8,384]{2,1,0:T(8,128)S(1)} %bitcast.12), channel_id=1, replica_groups=mesh['term_0'=8,'term_1'=2,'doc_0'=4,'doc_1'=4] {'term_1','doc_0','doc_1'}, dimensions={0} | all-to-all | bytes 786432 | tf_op jit(solution)/shard_map/all_to_all | solution.py:347
  155.4 10.1 %all_to_all.58.got = f32[8,8,384]{2,1,0:T(8,128)S(1)} all-to-all(f32[8,8,384]{2,1,0:T(8,128)S(1)} %shard_map.93), channel_id=1, replica_groups=mesh['term_0'=8,'term_1'=2,'doc_0'=4,'doc_1'=4] {'term_0'}, dimensions={0} | all-to-all | bytes 196608 | tf_op jit(solution)/shard_map/all_to_all | solution.py:347
  165.5 0.8 shard_map.94
  166.2 5.9 %all-to-all-start.9 = ((f32[32,8,384]{2,1,0:T(8,128)}), f32[32,8,384]{2,1,0:T(8,128)S(1)}, u32[]{:S(2)}, u32[]{:S(2)}) async-start(f32[32,8,384]{2,1,0:T(8,128)} %shard_map.94), calls=%async_computation.9 | async-start | bytes 786432 | tf_op jit(solution)/shard_map/all_to_all | solution.py:347
  172.2 18.1 %all-gather.2 = s16[4352,128]{1,0:T(8,128)(2,1)S(1)} all-gather(s16[272,128]{1,0:T(8,128)(2,1)S(1)} %get-tuple-element.34), channel_id=2, replica_groups=mesh['term_0'=8,'term_1'=2,'doc_0'=4,'doc_1'=4] {'term_0','term_1'}, dimensions={0}, use_global_device_ids=true | all-gather | bytes 1183744 | tf_op jit(solution)/shard_map/all_gather | solution.py:387
  190.2 0.0 all-to-all-done.9
  190.2 11.0 %shard_map.95 = (f32[2,256,256]{2,1,0:T(8,128)S(1)}, f32[256,128]{1,0:T(8,128)S(1)}) custom-call(f32[256,384]{1,0:T(8,128)S(1)} %bitcast.11), custom_call_target="tpu_custom_call" | custom-call | tf_op jit(solution)/shard_map/pallas_call | solution.py:28
  201.2 2.8 %shard_map.96 = (bf16[2048,256]{1,0:T(8,128)(2,1)}, bf16[2048,256]{1,0:T(8,128)(2,1)}) custom-call(f32[2,256,256]{2,1,0:T(8,128)S(1)} %get-tuple-element.33.inverse, bf16[16,256,128]{2,1,0:T(8,128)(2,1)S(1)} %all_to_all.55.scaled, f32[16,128]{1,0:T(8,128)S(1)} %copy-done.3, s16[16,272,128]{2,1,0:T(8,128)(2,1)S(1)} %bitcast.10, ...), custom_call_target="tpu_custom_call" | custom-call | tf_op jit(solution)/shard_map/pallas_call | solution.py:28
  (1 shorter events, 0.0 us)
Async XLA Ops:
  0.6 19.5 %copy-start.7 = (s32[1,48]{1,0:T(1,128)S(1)}, s32[1,48]{1,0:T(1,128)}, u32[]{:S(2)}) copy-start(s32[1,48]{1,0:T(1,128)} %cols.9) | copy-start | bytes 580
  0.6 19.5 %copy-start.5 = (s32[1,48]{1,0:T(1,128)S(1)}, s32[1,48]{1,0:T(1,128)}, u32[]{:S(2)}) copy-start(s32[1,48]{1,0:T(1,128)} %rows.9) | copy-start | bytes 580
  1.4 1.4 copy-start
  2.8 0.7 copy-start.4
  3.5 0.7 copy-start.6
  4.1 16.0 %copy-start.1 = (bf16[48,128,128]{2,1,0:T(8,128)(2,1)S(1)}, bf16[48,128,128]{2,1,0:T(8,128)(2,1)}, u32[]{:S(2)}) copy-start(bf16[48,128,128]{2,1,0:T(8,128)(2,1)} %values.9) | copy-start | bytes 4718596
  4.1 38.2 %copy-start.2 = (bf16[2048,256]{1,0:T(8,128)(2,1)S(1)}, bf16[2048,256]{1,0:T(8,128)(2,1)}, u32[]{:S(2)}) copy-start(bf16[2048,256]{1,0:T(8,128)(2,1)} %refs_6_.1) | copy-start | bytes 3145732
  73.1 19.0 %copy-start.3 = (f32[16,128]{1,0:T(8,128)S(1)}, f32[16,128]{1,0:T(8,128)}, u32[]{:S(2)}) copy-start(f32[16,128]{1,0:T(8,128)} %get-tuple-element.23.row_scale) | copy-start | bytes 24580
  92.1 20.1 %copy-start.8 = (f32[16,128]{1,0:T(8,128)S(1)}, f32[16,128]{1,0:T(8,128)}, u32[]{:S(2)}) copy-start(f32[16,128]{1,0:T(8,128)} %get-tuple-element.25.col_scale) | copy-start | bytes 24580
  114.4 4.4 %collective-permute-start = (s16[8,272,128]{2,1,0:T(8,128)(2,1)S(1)}, s16[8,272,128]{2,1,0:T(8,128)(2,1)S(1)}, u32[]{:S(2)}, u32[]{:S(2)}) collective-permute-start(s16[8,272,128]{2,1,0:T(8,128)(2,1)S(1)} %get-tuple-element.30), channel_id=1, source_target_pairs={{0,16},{16,0},{1,17},{17,1},{2,18},{18,2},{3,19},{19,3},{4,20},{20... | collective-permute-start | bytes 1671176 | tf_op jit(solution)/shard_map/ppermute | solution.py:380
  166.2 24.0 %all-to-all-start.9 = ((f32[32,8,384]{2,1,0:T(8,128)}), f32[32,8,384]{2,1,0:T(8,128)S(1)}, u32[]{:S(2)}, u32[]{:S(2)}) async-start(f32[32,8,384]{2,1,0:T(8,128)} %shard_map.94), calls=%async_computation.9 | async-start | bytes 786432 | tf_op jit(solution)/shard_map/all_to_all | solution.py:347

commit v6 on v5

--- a/solution.py
+++ b/solution.py
@@ -11,7 +11,7 @@
 RB = 16
 CB = 16
 CAP = 48
-GROUP = 8
+GROUP = 24
 PANEL = 64
 TERM = ("term_0", "term_1")
 DOC = ("doc_0", "doc_1")
@@ -23,15 +23,14 @@
 SMEM = pl.BlockSpec(memory_space=pltpu.SMEM)
 
 
-def call(body, inputs, outs, scratch=(), flops=1 << 20):
-    specs = [SMEM if a.dtype == jnp.int32 else VMEM for a in inputs]
+def call(body, inputs, outs, scratch=(), specs=None, mib=16):
     return pl.pallas_call(
         body,
         out_shape=[jax.ShapeDtypeStruct(s, d) for s, d in outs],
-        in_specs=specs,
-        out_specs=[SMEM if d == jnp.int32 else VMEM for _, d in outs],
-        scratch_shapes=[pltpu.VMEM(s, d) for s, d in scratch],
-        compiler_params=pltpu.CompilerParams(vmem_limit_bytes=16 * 1024 * 1024),
+        in_specs=specs or [SMEM if a.dtype == jnp.int32 else VMEM for a in inputs],
+        out_specs=[VMEM] * len(outs),
+        scratch_shapes=[pltpu.VMEM(s[0], s[1]) if isinstance(s, tuple) else s for s in scratch],
+        compiler_params=pltpu.CompilerParams(vmem_limit_bytes=int(mib * 1024 * 1024)),
     )(*inputs)
 
 
@@ -52,25 +51,31 @@
         ref[b, base : base + 16, :] = rows.astype(BF16)
 
 
-def over_tiles(count, values, source, target, src_ref, acc_ref, transposed):
+def over_tiles(count, values, source, target, src_ref, acc_ref, transposed, group, ready=None):
     acc_ref[...] = jnp.zeros(acc_ref.shape, F32)
     dims = (((1,), (1,)), ((), ())) if transposed else (((1,), (0,)), ((), ()))
 
     def visit(g, _):
         products = []
-        for u in range(GROUP):
-            s = g * GROUP + u
+        for u in range(group):
+            s = g * group + u
             tile = values[s]
             tile = jnp.where(s < count, tile, jnp.zeros_like(tile))
             products.append(
                 lax.dot_general(src_ref[source[0, s]], tile, dims, preferred_element_type=F32)
             )
-        for u in range(GROUP):
-            s = g * GROUP + u
+        for u in range(group):
+            s = g * group + u
             acc_ref[target[0, s]] += products[u]
         return 0
 
-    lax.fori_loop(0, (count + GROUP - 1) // GROUP, visit, 0)
+    if ready is None and group < CAP:
+        lax.fori_loop(0, (count + group - 1) // group, visit, 0)
+        return
+    for g in range(CAP // group):
+        if ready is not None:
+            ready(g)
+        visit(g, 0)
 
 
 def send_vector(out_ref, acc_ref):
@@ -79,11 +84,18 @@
         out_ref[i, 0:RB, :] = vec
 
 
-def first_rows(place, values, rows, cols, count, out, place_out, src, acc):
-    for i in range(3):
-        place_out[0, i] = place[0, i]
+def first_rows(values_in, rows_in, cols_in, count, out, src, acc, values, rows, cols, sems):
+    parts = CAP // GROUP
+    copies = [pltpu.make_async_copy(rows_in, rows, sems.at[0]), pltpu.make_async_copy(cols_in, cols, sems.at[1])]
+    for g in range(parts):
+        own = pl.ds(g * GROUP, GROUP)
+        copies.append(pltpu.make_async_copy(values_in.at[own], values.at[own], sems.at[2 + g]))
+    for copy in copies:
+        copy.start()
     put_thirds(src, jnp.ones((CB, TILE), F32), 0)
-    over_tiles(count[0, 0], values, cols, rows, src, acc, True)
+    copies[0].wait()
+    copies[1].wait()
+    over_tiles(count[0, 0], values, cols, rows, src, acc, True, GROUP, lambda g: copies[2 + g].wait())
     send_vector(out, acc)
 
 
@@ -91,13 +103,13 @@
     vec = 1.0 / jnp.sum(got[...], axis=0)[0:RB]
     scale[...] = vec
     put_thirds(src, vec, 0)
-    over_tiles(count[0, 0], values, rows, cols, src, acc, False)
+    over_tiles(count[0, 0], values, rows, cols, src, acc, False, CAP)
     send_vector(out, acc)
 
 
 def to_rows(values, rows, cols, count, got, start, out, src, acc):
     put_thirds(src, 1.0 / jnp.sum(got[...], axis=0), 0)
-    over_tiles(count[0, 0], values, cols, rows, src, acc, True)
+    over_tiles(count[0, 0], values, cols, rows, src, acc, True, GROUP)
     send_vector(out, acc)
     mean = jnp.sum(start[...].astype(F32), axis=0, keepdims=True)
     for i in range(16):
@@ -111,18 +123,18 @@
     scale[...] = vec
     put_thirds(src, vec, K)
     for b in range(CB):
-        block = start[b * TILE : (b + 1) * TILE, :].astype(F32).T
+        block = start[b * TILE : (b + 1) * TILE, :].T.astype(F32)
         src[b, 0:K, :] = (block * vec[b : b + 1, :]).astype(BF16)
     mean = jnp.sum(first[...], axis=0)[16:18] / docs
     mean = jnp.concatenate([jnp.broadcast_to(mean[h : h + 1], (TILE, TILE)).T for h in range(2)], axis=0)
-    over_tiles(count[0, 0], values, cols, rows, src, acc, True)
+    over_tiles(count[0, 0], values, cols, rows, src, acc, True, GROUP)
     for b in range(RB):
         weight = jnp.sum(acc[b, K : K + 16, :], axis=0, keepdims=True)
         out[b] = (acc[b, 0:K, :] - mean * weight).astype(out.dtype)
 
 
-def left_rows(place, got, row_scale, out, gram):
-    d = place[0, 1]
+def left_rows(got, row_scale, out, gram):
+    d = lax.axis_index(DOC)
     scale = row_scale[pl.ds(d, 1), :]
     left = scale * jnp.sum(got[...].astype(F32), axis=0)
     sent = (left * scale).astype(BF16)
@@ -161,9 +173,9 @@
     return jnp.exp2(code * (1.0 / STEPS)) * (1.0 / LEVELS)
 
 
-def right_product(place, values, rows, cols, count, scaled, col_scale, keep, send, acc):
-    over_tiles(count[0, 0], values, rows, cols, scaled, acc, False)
-    core = place[0, 2]
+def right_product(values, rows, cols, count, scaled, col_scale, keep, send, acc):
+    over_tiles(count[0, 0], values, rows, cols, scaled, acc, False, GROUP)
+    core = lax.axis_index("term_1")
     peak = jnp.zeros((K, TILE), F32)
     for i in range(CB // 2):
         mine, its = 2 * i + core, 2 * i + 1 - core
@@ -350,12 +362,19 @@
 def per_device(tile_values, tile_rows, tile_cols, tile_count, start_block):
     terms = float(RB * TILE * lax.axis_size(TERM))
     docs = float(CB * TILE * lax.axis_size(DOC))
-    place = jnp.stack([lax.axis_index(TERM), lax.axis_index(DOC), lax.axis_index("term_1")]).astype(jnp.int32)[None]
     tiles = (tile_values, tile_rows, tile_cols, tile_count)
     vec = [((RB, 16, TILE), BF16), ((RB, 16, TILE), F32)]
     vector = ((16, RB, TILE), F32)
     scale = ((RB, TILE), F32)
-    part, place = call(first_rows, (place, *tiles), [vector, ((1, 3), jnp.int32)], vec)
+    lists = pltpu.SMEM((1, CAP), jnp.int32)
+    (part,) = call(
+        first_rows,
+        tiles,
+        [vector],
+        [*vec, (tile_values.shape, BF16), lists, lists, pltpu.SemaphoreType.DMA((2 + CAP // GROUP,))],
+        [pl.BlockSpec(memory_space=pltpu.HBM)] * 3 + [SMEM],
+        60,
+    )
     part, _ = call(to_columns, (*tiles, exchanged(part, DOC)), [vector, scale], vec)
     (part,) = call(to_rows, (*tiles, exchanged(part, TERM), start_block), [((16, 24, TILE), F32)], vec)
     first = exchanged(part, DOC)
@@ -367,13 +386,13 @@
         [((CB, K + 16, TILE), BF16), ((RB, K + 16, TILE), F32)],
     )
     part, left_gram = call(
-        left_rows, (place, exchanged(part, DOC), row_scale), [((16, K, TILE), BF16), ((K, K), F32)]
+        left_rows, (exchanged(part, DOC), row_scale), [((16, K, TILE), BF16), ((K, K), F32)]
     )
     scaled = exchanged(part, DOC)
     half = (CB // 2, K + 16, TILE)
     keep, part = call(
         right_product,
-        (place, *tiles, scaled, col_scale),
+        (*tiles, scaled, col_scale),
         [((CB // 2, K, TILE), F32), (half, jnp.int16)],
         [((CB, K, TILE), F32)],
     )

time: 204 us -> 201 us (0.985)
  local copies, waits for them, and re-layouts: 2.75 us -> 0.02 us
    unnamed x18 -> x12, local copies, waits for them, and re-layouts: 2.75 us -> 0.02 us
where the time goes in v6:
time: 201 us; the launch traced here: 199 us
  blocking collectives  158 us (79%)
  Pallas kernels  29.3 us (15%)
  starting transfers between devices  8.87 us (4%)
    all_to_all x9, blocking collectives, exchanged(): return lax.all_to_all(x, axis, split_axis=0, concat_axis=0, tiled=True)  140 us
    pallas_call x13, Pallas kernels, call(): pl.pallas_call(body, out_shape=[jax.ShapeDtypeStruct(s, d) for s, d in ou...  29.3 us
    all_gather x1, blocking collectives, per_device(): gathered = lax.all_gather(own, TERM)  18.1 us
    all_to_all x1, starting transfers between devices, exchanged(): return lax.all_to_all(x, axis, split_axis=0, concat_axis=0, tiled=True)  5.9 us
  transfers between devices with their start and end apart: 2, of which 1 were waited for; matrix products, arithmetic and copies ran while one was open for 0% of the time, Pallas kernels for 0%

profile of v6, /device:TPU:1, one launch (start us, length us, event | category | flops | bytes accessed | tf_op | source)
XLA Modules:
  0.0 199.1 jit_solution(6345446194110127018)
XLA Ops:
  0.6 0.0 copy-start.4
  0.6 0.0 copy-start.3
  0.7 0.0 copy-start
  1.4 0.0 copy-start.1
  1.4 3.0 %shard_map.84 = f32[16,16,128]{2,1,0:T(8,128)} custom-call(bf16[48,128,128]{2,1,0:T(8,128)(2,1)} %values.7, s32[1,48]{1,0:T(1,128)} %rows.7, s32[1,48]{1,0:T(1,128)} %cols.7, s32[1,1]{1,0:T(1,128)S(6)} %copy.9.count.refs_3_), custom_call_target="tpu_custom_call" | custom-call | tf_op jit(solution)/shard_map/pallas_call | solution.py:27
  4.5 14.5 %all_to_all.50.got = f32[16,16,128]{2,1,0:T(8,128)S(1)} all-to-all(f32[16,16,128]{2,1,0:T(8,128)} %shard_map.84), channel_id=1, replica_groups=mesh['term_0'=8,'term_1'=2,'doc_0'=4,'doc_1'=4] {'doc_0','doc_1'}, dimensions={0} | all-to-all | bytes 262144 | tf_op jit(solution)/shard_map/all_to_all | solution.py:359
  18.9 0.0 copy-done.4
  18.9 0.0 copy-done.3
  18.9 0.0 copy-done
  18.9 1.6 shard_map.85
  20.5 19.5 %all_to_all.51.got = f32[16,16,128]{2,1,0:T(8,128)S(1)} all-to-all(f32[16,16,128]{2,1,0:T(8,128)S(1)} %get-tuple-element.19), channel_id=1, replica_groups=mesh['term_0'=8,'term_1'=2,'doc_0'=4,'doc_1'=4] {'term_0','term_1'}, dimensions={0} | all-to-all | bytes 262144 | tf_op jit(solution)/shard_map/all_to_all | solution.py:359
  40.0 0.0 copy-done.1
  40.0 1.4 shard_map.86
  41.4 10.5 %all_to_all.52.got.refs_5_ = f32[16,24,128]{2,1,0:T(8,128)S(1)} all-to-all(f32[16,24,128]{2,1,0:T(8,128)S(1)} %shard_map.86), channel_id=1, replica_groups=mesh['term_0'=8,'term_1'=2,'doc_0'=4,'doc_1'=4] {'doc_0','doc_1'}, dimensions={0} | all-to-all | bytes 393216 | tf_op jit(solution)/shard_map/all_to_all | solution.py:359
  51.9 1.6 shard_map.87
  53.5 12.8 %all_to_all.53.refs_4_ = f32[16,16,128]{2,1,0:T(8,128)S(1)} all-to-all(f32[16,16,128]{2,1,0:T(8,128)S(1)} %get-tuple-element.21), channel_id=1, replica_groups=mesh['term_0'=8,'term_1'=2,'doc_0'=4,'doc_1'=4] {'term_0','term_1'}, dimensions={0} | all-to-all | bytes 262144 | tf_op jit(solution)/shard_map/all_to_all | solution.py:359
  66.4 2.7 %shard_map.88 = (bf16[16,256,128]{2,1,0:T(8,128)(2,1)S(1)}, f32[16,128]{1,0:T(8,128)}) custom-call(bf16[48,128,128]{2,1,0:T(8,128)(2,1)S(1)} %copy-done, s32[1,48]{1,0:T(1,128)S(1)} %copy-done.3, s32[1,48]{1,0:T(1,128)S(1)} %copy-done.4, s32[1,1]{1,0:T(1,128)S(6)} %copy.9.count.refs_3_, f32[16,16,128]{2,1,0:T(8,128)S(1)} %all_to_all.53.refs_4_, ...), custom_call_target="tpu_custom_call" | custom-call | tf_op jit(solution)/shard_map/pallas_call | solution.py:27
  69.1 0.0 copy-start.2
  69.1 19.6 %all_to_all.54.got = bf16[16,256,128]{2,1,0:T(8,128)(2,1)S(1)} all-to-all(bf16[16,256,128]{2,1,0:T(8,128)(2,1)S(1)} %get-tuple-element.23), channel_id=1, replica_groups=mesh['term_0'=8,'term_1'=2,'doc_0'=4,'doc_1'=4] {'doc_0','doc_1'}, dimensions={0} | all-to-all | bytes 2097152 | tf_op jit(solution)/shard_map/all_to_all | solution.py:359
  88.6 0.0 copy-done.2
  88.6 0.0 copy-start.5
  88.6 0.6 shard_map.89
  89.2 19.0 %all_to_all.55.scaled = bf16[16,256,128]{2,1,0:T(8,128)(2,1)S(1)} all-to-all(bf16[16,256,128]{2,1,0:T(8,128)(2,1)S(1)} %get-tuple-element.24), channel_id=1, replica_groups=mesh['term_0'=8,'term_1'=2,'doc_0'=4,'doc_1'=4] {'doc_0','doc_1'}, dimensions={0} | all-to-all | bytes 2097152 | tf_op jit(solution)/shard_map/all_to_all | solution.py:359
  108.2 0.0 copy-done.5
  108.2 2.0 %shard_map.90 = (f32[8,256,128]{2,1,0:T(8,128)S(1)}, s16[8,272,128]{2,1,0:T(8,128)(2,1)S(1)}) custom-call(bf16[48,128,128]{2,1,0:T(8,128)(2,1)S(1)} %copy-done, s32[1,48]{1,0:T(1,128)S(1)} %copy-done.3, s32[1,48]{1,0:T(1,128)S(1)} %copy-done.4, s32[1,1]{1,0:T(1,128)S(6)} %copy.9.count.refs_3_, bf16[16,256,128]{2,1,0:T(8,128)(2,1)S(1)} %all_to_all.55.scaled, ...), custom_call_target="tpu_custom_call" | custom-call | tf_op jit(solution)/shard_map/pallas_call | solution.py:27
  110.2 3.0 %collective-permute-start = (s16[8,272,128]{2,1,0:T(8,128)(2,1)S(1)}, s16[8,272,128]{2,1,0:T(8,128)(2,1)S(1)}, u32[]{:S(2)}, u32[]{:S(2)}) collective-permute-start(s16[8,272,128]{2,1,0:T(8,128)(2,1)S(1)} %get-tuple-element.26), channel_id=1, source_target_pairs={{0,16},{16,0},{1,17},{17,1},{2,18},{18,2},{3,19},{19,3},{4,20},{20... | collective-permute-start | bytes 1671176 | tf_op jit(solution)/shard_map/ppermute | solution.py:399
  113.2 1.6 collective-permute-done.got
  114.8 0.6 shard_map.91
  115.4 20.3 %all_to_all.56.got = s16[8,272,128]{2,1,0:T(8,128)(2,1)S(1)} all-to-all(s16[8,272,128]{2,1,0:T(8,128)(2,1)S(1)} %shard_map.91), channel_id=1, replica_groups=mesh['term_0'=8,'term_1'=2,'doc_0'=4,'doc_1'=4] {'term_0'}, dimensions={0} | all-to-all | bytes 1114112 | tf_op jit(solution)/shard_map/all_to_all | solution.py:359
  135.8 1.0 shard_map.92
  136.8 13.6 %all_to_all.57.got = f32[32,8,384]{2,1,0:T(8,128)S(1)} all-to-all(f32[32,8,384]{2,1,0:T(8,128)S(1)} %bitcast.7), channel_id=1, replica_groups=mesh['term_0'=8,'term_1'=2,'doc_0'=4,'doc_1'=4] {'term_1','doc_0','doc_1'}, dimensions={0} | all-to-all | bytes 786432 | tf_op jit(solution)/shard_map/all_to_all | solution.py:359
  150.4 10.1 %all_to_all.58.got = f32[8,8,384]{2,1,0:T(8,128)S(1)} all-to-all(f32[8,8,384]{2,1,0:T(8,128)S(1)} %shard_map.93), channel_id=1, replica_groups=mesh['term_0'=8,'term_1'=2,'doc_0'=4,'doc_1'=4] {'term_0'}, dimensions={0} | all-to-all | bytes 196608 | tf_op jit(solution)/shard_map/all_to_all | solution.py:359
  160.5 0.8 shard_map.94
  161.2 5.9 %all-to-all-start.9 = ((f32[32,8,384]{2,1,0:T(8,128)}), f32[32,8,384]{2,1,0:T(8,128)S(1)}, u32[]{:S(2)}, u32[]{:S(2)}) async-start(f32[32,8,384]{2,1,0:T(8,128)} %shard_map.94), calls=%async_computation.9 | async-start | bytes 786432 | tf_op jit(solution)/shard_map/all_to_all | solution.py:359
  167.1 18.1 %all-gather.2 = s16[4352,128]{1,0:T(8,128)(2,1)S(1)} all-gather(s16[272,128]{1,0:T(8,128)(2,1)S(1)} %get-tuple-element.30), channel_id=2, replica_groups=mesh['term_0'=8,'term_1'=2,'doc_0'=4,'doc_1'=4] {'term_0','term_1'}, dimensions={0}, use_global_device_ids=true | all-gather | bytes 1183744 | tf_op jit(solution)/shard_map/all_gather | solution.py:406
  185.2 0.0 all-to-all-done.9
  185.2 11.0 %shard_map.95 = (f32[2,256,256]{2,1,0:T(8,128)S(1)}, f32[256,128]{1,0:T(8,128)S(1)}) custom-call(f32[256,384]{1,0:T(8,128)S(1)} %bitcast.6), custom_call_target="tpu_custom_call" | custom-call | tf_op jit(solution)/shard_map/pallas_call | solution.py:27
  196.2 2.9 %shard_map.96 = (bf16[2048,256]{1,0:T(8,128)(2,1)}, bf16[2048,256]{1,0:T(8,128)(2,1)}) custom-call(f32[2,256,256]{2,1,0:T(8,128)S(1)} %get-tuple-element.29.inverse, bf16[16,256,128]{2,1,0:T(8,128)(2,1)S(1)} %all_to_all.55.scaled, f32[16,128]{1,0:T(8,128)S(1)} %copy-done.2, s16[16,272,128]{2,1,0:T(8,128)(2,1)S(1)} %bitcast.5, ...), custom_call_target="tpu_custom_call" | custom-call | tf_op jit(solution)/shard_map/pallas_call | solution.py:27
  (1 shorter events, 0.0 us)
Async XLA Ops:
  0.6 18.3 %copy-start.4 = (s32[1,48]{1,0:T(1,128)S(1)}, s32[1,48]{1,0:T(1,128)}, u32[]{:S(2)}) copy-start(s32[1,48]{1,0:T(1,128)} %cols.7) | copy-start | bytes 580
  0.6 18.3 %copy-start.3 = (s32[1,48]{1,0:T(1,128)S(1)}, s32[1,48]{1,0:T(1,128)}, u32[]{:S(2)}) copy-start(s32[1,48]{1,0:T(1,128)} %rows.7) | copy-start | bytes 580
  0.7 18.3 %copy-start = (bf16[48,128,128]{2,1,0:T(8,128)(2,1)S(1)}, bf16[48,128,128]{2,1,0:T(8,128)(2,1)}, u32[]{:S(2)}) copy-start(bf16[48,128,128]{2,1,0:T(8,128)(2,1)} %values.7) | copy-start | bytes 4718596
  1.4 38.6 %copy-start.1 = (bf16[2048,256]{1,0:T(8,128)(2,1)S(1)}, bf16[2048,256]{1,0:T(8,128)(2,1)}, u32[]{:S(2)}) copy-start(bf16[2048,256]{1,0:T(8,128)(2,1)} %refs_6_.1) | copy-start | bytes 3145732
  69.1 19.6 %copy-start.2 = (f32[16,128]{1,0:T(8,128)S(1)}, f32[16,128]{1,0:T(8,128)}, u32[]{:S(2)}) copy-start(f32[16,128]{1,0:T(8,128)} %get-tuple-element.20.row_scale) | copy-start | bytes 24580
  88.6 19.6 %copy-start.5 = (f32[16,128]{1,0:T(8,128)S(1)}, f32[16,128]{1,0:T(8,128)}, u32[]{:S(2)}) copy-start(f32[16,128]{1,0:T(8,128)} %get-tuple-element.22.col_scale) | copy-start | bytes 24580
  110.2 4.6 %collective-permute-start = (s16[8,272,128]{2,1,0:T(8,128)(2,1)S(1)}, s16[8,272,128]{2,1,0:T(8,128)(2,1)S(1)}, u32[]{:S(2)}, u32[]{:S(2)}) collective-permute-start(s16[8,272,128]{2,1,0:T(8,128)(2,1)S(1)} %get-tuple-element.26), channel_id=1, source_target_pairs={{0,16},{16,0},{1,17},{17,1},{2,18},{18,2},{3,19},{19,3},{4,20},{20... | collective-permute-start | bytes 1671176 | tf_op jit(solution)/shard_map/ppermute | solution.py:399
  161.2 24.0 %all-to-all-start.9 = ((f32[32,8,384]{2,1,0:T(8,128)}), f32[32,8,384]{2,1,0:T(8,128)S(1)}, u32[]{:S(2)}, u32[]{:S(2)}) async-start(f32[32,8,384]{2,1,0:T(8,128)} %shard_map.94), calls=%async_computation.9 | async-start | bytes 786432 | tf_op jit(solution)/shard_map/all_to_all | solution.py:359

commit v7 on v6

--- a/solution.py
+++ b/solution.py
@@ -15,7 +15,6 @@
 PANEL = 64
 TERM = ("term_0", "term_1")
 DOC = ("doc_0", "doc_1")
-PLANE = ("term_1",) + DOC
 F32 = jnp.float32
 BF16 = jnp.bfloat16
 PRECISE = lax.Precision.HIGHEST
@@ -227,9 +226,36 @@
     out[:, K : K + TILE] = extra
 
 
-def sum_all(got, out):
+FINE = 64000.0
+OWN = K + 16
+MID = OWN + 48
+LOW = MID + 48
+
+
+def sum_docs(got, own, out):
+    out[0:OWN, :] = own[...]
     total = jnp.sum(got[...], axis=0)
-    for i in range(out.shape[0]):
+    code = code_of(jnp.max(jnp.abs(total), axis=1, keepdims=True))
+    steps = total * (jnp.exp2(code * (-1.0 / STEPS)) * LEVELS)
+    whole = jnp.floor(steps + 0.5)
+    part = jnp.floor((steps - whole) * FINE + 0.5)
+    for h in range(3):
+        lanes = slice(h * TILE, (h + 1) * TILE)
+        out[OWN + 16 * h : OWN + 16 * h + 16, :] = whole[:, lanes].astype(jnp.int32).astype(jnp.int16)
+        out[MID + 16 * h : MID + 16 * h + 16, :] = part[:, lanes].astype(jnp.int32).astype(jnp.int16)
+    out[LOW : LOW + 16, :] = jnp.broadcast_to(code, (16, TILE)).astype(jnp.int32).astype(jnp.int16)
+
+
+def sum_terms(got, out):
+    total = [jnp.zeros((16, TILE), F32)] * 3
+    for i in range(16):
+        step = jnp.exp2(wide(got[i, LOW : LOW + 16, :]) * (1.0 / STEPS)) * (1.0 / LEVELS)
+        for h in range(3):
+            whole = wide(got[i, OWN + 16 * h : OWN + 16 * h + 16, :])
+            part = wide(got[i, MID + 16 * h : MID + 16 * h + 16, :])
+            total[h] = total[h] + (whole + part * (1.0 / FINE)) * step
+    total = jnp.concatenate(total, axis=1)
+    for i in range(16):
         out[i] = total
 
 
@@ -403,11 +429,11 @@
         (exchanged(part, "term_0"), left_gram),
         [((K, 3 * TILE), F32), ((K + 16, TILE), jnp.int16)],
     )
-    gathered = lax.all_gather(own, TERM)
-    part = exchanged(part.reshape(32, 8, 3 * TILE), PLANE)
-    (part,) = call(sum_all, (part,), [((8, 8, 3 * TILE), F32)])
-    (part,) = call(sum_all, (exchanged(part, "term_0"),), [((32, 8, 3 * TILE), F32)])
-    grams = exchanged(part, PLANE).reshape(K, 3 * TILE)
+    part = exchanged(part.reshape(16, 16, 3 * TILE), DOC)
+    (part,) = call(sum_docs, (part, own), [((LOW + 16, TILE), jnp.int16)])
+    gathered = lax.all_gather(part, TERM)
+    (part,) = call(sum_terms, (gathered,), [((16, 16, 3 * TILE), F32)])
+    grams = exchanged(part, DOC).reshape(K, 3 * TILE)
     inverse, lean = call(
         lambda *refs: finish(terms, docs, *refs),
         (grams,),

time: 201 us -> 198 us (0.985)
  starting transfers between devices: 8.87 us -> 1.5 us
  blocking collectives: 158 us -> 162 us
    all_to_all x1 -> x0, starting transfers between devices: 5.9 us -> none  [exchanged(): return lax.all_to_all(x, axis, split_axis=0, concat_axis=0, tiled=True)]
    all_gather x1, blocking collectives: 18.1 us -> 21.8 us  [per_device(): gathered = lax.all_gather(part, TERM)]
  transfers between devices with their start and end apart: 2 -> 1, of which waited for: 1 -> 1; matrix products, arithmetic and copies ran while one was open for 0% -> 0% of each run, Pallas kernels for 0% -> 0%
where the time goes in v7:
time: 198 us
  blocking collectives  162 us (82%)
  Pallas kernels  30.9 us (16%)
    all_to_all x9, blocking collectives, exchanged(): return lax.all_to_all(x, axis, split_axis=0, concat_axis=0, tiled=True)  140 us
    pallas_call x13, Pallas kernels, call(): pl.pallas_call(body, out_shape=[jax.ShapeDtypeStruct(s, d) for s, d in ou...  30.9 us
    all_gather x1, blocking collectives, per_device(): gathered = lax.all_gather(part, TERM)  21.8 us
  transfers between devices with their start and end apart: 1, of which 1 were waited for; matrix products, arithmetic and copies ran while one was open for 0% of the time, Pallas kernels for 0%

profile of v7, /device:TPU:1, one launch (start us, length us, event | category | flops | bytes accessed | tf_op | source)
XLA Modules:
  0.0 197.5 jit_solution(16728657377547851043)
XLA Ops:
  0.6 0.0 copy-start.4
  0.6 0.0 copy-start.3
  0.7 0.0 copy-start
  1.4 0.0 copy-start.1
  1.4 3.0 %shard_map.84 = f32[16,16,128]{2,1,0:T(8,128)} custom-call(bf16[48,128,128]{2,1,0:T(8,128)(2,1)} %values.7, s32[1,48]{1,0:T(1,128)} %rows.7, s32[1,48]{1,0:T(1,128)} %cols.7, s32[1,1]{1,0:T(1,128)S(6)} %copy.9.count.refs_3_), custom_call_target="tpu_custom_call" | custom-call | tf_op jit(solution)/shard_map/pallas_call | solution.py:26
  4.4 14.5 %all_to_all.45.got = f32[16,16,128]{2,1,0:T(8,128)S(1)} all-to-all(f32[16,16,128]{2,1,0:T(8,128)} %shard_map.84), channel_id=1, replica_groups=mesh['term_0'=8,'term_1'=2,'doc_0'=4,'doc_1'=4] {'doc_0','doc_1'}, dimensions={0} | all-to-all | bytes 262144 | tf_op jit(solution)/shard_map/all_to_all | solution.py:385
  18.9 0.0 copy-done.4
  18.9 0.0 copy-done.3
  18.9 0.0 copy-done
  18.9 1.6 shard_map.85
  20.5 19.5 %all_to_all.46.got = f32[16,16,128]{2,1,0:T(8,128)S(1)} all-to-all(f32[16,16,128]{2,1,0:T(8,128)S(1)} %get-tuple-element.19), channel_id=1, replica_groups=mesh['term_0'=8,'term_1'=2,'doc_0'=4,'doc_1'=4] {'term_0','term_1'}, dimensions={0} | all-to-all | bytes 262144 | tf_op jit(solution)/shard_map/all_to_all | solution.py:385
  40.0 0.0 copy-done.1
  40.0 2.0 shard_map.86
  42.0 11.1 %all_to_all.47.got.refs_5_ = f32[16,24,128]{2,1,0:T(8,128)S(1)} all-to-all(f32[16,24,128]{2,1,0:T(8,128)S(1)} %shard_map.86), channel_id=1, replica_groups=mesh['term_0'=8,'term_1'=2,'doc_0'=4,'doc_1'=4] {'doc_0','doc_1'}, dimensions={0} | all-to-all | bytes 393216 | tf_op jit(solution)/shard_map/all_to_all | solution.py:385
  53.1 1.6 shard_map.87
  54.7 12.0 %all_to_all.48.refs_4_ = f32[16,16,128]{2,1,0:T(8,128)S(1)} all-to-all(f32[16,16,128]{2,1,0:T(8,128)S(1)} %get-tuple-element.21), channel_id=1, replica_groups=mesh['term_0'=8,'term_1'=2,'doc_0'=4,'doc_1'=4] {'term_0','term_1'}, dimensions={0} | all-to-all | bytes 262144 | tf_op jit(solution)/shard_map/all_to_all | solution.py:385
  66.7 3.8 %shard_map.88 = (bf16[16,256,128]{2,1,0:T(8,128)(2,1)S(1)}, f32[16,128]{1,0:T(8,128)}) custom-call(bf16[48,128,128]{2,1,0:T(8,128)(2,1)S(1)} %copy-done, s32[1,48]{1,0:T(1,128)S(1)} %copy-done.3, s32[1,48]{1,0:T(1,128)S(1)} %copy-done.4, s32[1,1]{1,0:T(1,128)S(6)} %copy.9.count.refs_3_, f32[16,16,128]{2,1,0:T(8,128)S(1)} %all_to_all.48.refs_4_, ...), custom_call_target="tpu_custom_call" | custom-call | tf_op jit(solution)/shard_map/pallas_call | solution.py:26
  70.4 0.0 copy-start.2
  70.4 19.8 %all_to_all.49.got = bf16[16,256,128]{2,1,0:T(8,128)(2,1)S(1)} all-to-all(bf16[16,256,128]{2,1,0:T(8,128)(2,1)S(1)} %get-tuple-element.23), channel_id=1, replica_groups=mesh['term_0'=8,'term_1'=2,'doc_0'=4,'doc_1'=4] {'doc_0','doc_1'}, dimensions={0} | all-to-all | bytes 2097152 | tf_op jit(solution)/shard_map/all_to_all | solution.py:385
  90.2 0.0 copy-done.2
  90.2 0.0 copy-start.5
  90.2 0.6 shard_map.89
  90.8 18.9 %all_to_all.50.scaled = bf16[16,256,128]{2,1,0:T(8,128)(2,1)S(1)} all-to-all(bf16[16,256,128]{2,1,0:T(8,128)(2,1)S(1)} %get-tuple-element.24), channel_id=1, replica_groups=mesh['term_0'=8,'term_1'=2,'doc_0'=4,'doc_1'=4] {'doc_0','doc_1'}, dimensions={0} | all-to-all | bytes 2097152 | tf_op jit(solution)/shard_map/all_to_all | solution.py:385
  109.6 0.0 copy-done.5
  109.6 2.7 %shard_map.90 = (f32[8,256,128]{2,1,0:T(8,128)S(1)}, s16[8,272,128]{2,1,0:T(8,128)(2,1)S(1)}) custom-call(bf16[48,128,128]{2,1,0:T(8,128)(2,1)S(1)} %copy-done, s32[1,48]{1,0:T(1,128)S(1)} %copy-done.3, s32[1,48]{1,0:T(1,128)S(1)} %copy-done.4, s32[1,1]{1,0:T(1,128)S(6)} %copy.9.count.refs_3_, bf16[16,256,128]{2,1,0:T(8,128)(2,1)S(1)} %all_to_all.50.scaled, ...), custom_call_target="tpu_custom_call" | custom-call | tf_op jit(solution)/shard_map/pallas_call | solution.py:26
  112.3 1.5 collective-permute-start
  113.8 1.6 collective-permute-done.got
  115.4 0.6 shard_map.91
  116.1 20.6 %all_to_all.51.got = s16[8,272,128]{2,1,0:T(8,128)(2,1)S(1)} all-to-all(s16[8,272,128]{2,1,0:T(8,128)(2,1)S(1)} %shard_map.91), channel_id=1, replica_groups=mesh['term_0'=8,'term_1'=2,'doc_0'=4,'doc_1'=4] {'term_0'}, dimensions={0} | all-to-all | bytes 1114112 | tf_op jit(solution)/shard_map/all_to_all | solution.py:385
  136.7 1.0 shard_map.92
  137.7 11.6 %all_to_all.52.got = f32[16,16,384]{2,1,0:T(8,128)S(1)} all-to-all(f32[16,16,384]{2,1,0:T(8,128)S(1)} %bitcast.8), channel_id=1, replica_groups=mesh['term_0'=8,'term_1'=2,'doc_0'=4,'doc_1'=4] {'doc_0','doc_1'}, dimensions={0} | all-to-all | bytes 786432 | tf_op jit(solution)/shard_map/all_to_all | solution.py:385
  149.3 0.1 shard_map.93
  149.5 21.8 %all-gather.2 = s16[6144,128]{1,0:T(8,128)(2,1)S(1)} all-gather(s16[384,128]{1,0:T(8,128)(2,1)S(1)} %shard_map.93), channel_id=2, replica_groups=mesh['term_0'=8,'term_1'=2,'doc_0'=4,'doc_1'=4] {'term_0','term_1'}, dimensions={0}, use_global_device_ids=true | all-gather | bytes 1671168 | tf_op jit(solution)/shard_map/all_gather | solution.py:434
  171.3 0.1 shard_map.94
  171.4 12.3 %all_to_all.53 = f32[16,16,384]{2,1,0:T(8,128)S(1)} all-to-all(f32[16,16,384]{2,1,0:T(8,128)S(1)} %shard_map.94), channel_id=1, replica_groups=mesh['term_0'=8,'term_1'=2,'doc_0'=4,'doc_1'=4] {'doc_0','doc_1'}, dimensions={0} | all-to-all | bytes 786432 | tf_op jit(solution)/shard_map/all_to_all | solution.py:385
  183.7 11.0 %shard_map.95 = (f32[2,256,256]{2,1,0:T(8,128)S(1)}, f32[256,128]{1,0:T(8,128)S(1)}) custom-call(f32[256,384]{1,0:T(8,128)S(1)} %bitcast.7), custom_call_target="tpu_custom_call" | custom-call | tf_op jit(solution)/shard_map/pallas_call | solution.py:26
  194.7 2.8 %shard_map.96 = (bf16[2048,256]{1,0:T(8,128)(2,1)}, bf16[2048,256]{1,0:T(8,128)(2,1)}) custom-call(f32[2,256,256]{2,1,0:T(8,128)S(1)} %get-tuple-element.30.inverse, bf16[16,256,128]{2,1,0:T(8,128)(2,1)S(1)} %all_to_all.50.scaled, f32[16,128]{1,0:T(8,128)S(1)} %copy-done.2, s16[16,384,128]{2,1,0:T(8,128)(2,1)S(1)} %bitcast.6, ...), custom_call_target="tpu_custom_call" | custom-call | tf_op jit(solution)/shard_map/pallas_call | solution.py:26
Async XLA Ops:
  0.6 18.3 %copy-start.4 = (s32[1,48]{1,0:T(1,128)S(1)}, s32[1,48]{1,0:T(1,128)}, u32[]{:S(2)}) copy-start(s32[1,48]{1,0:T(1,128)} %cols.7) | copy-start | bytes 580
  0.6 18.3 %copy-start.3 = (s32[1,48]{1,0:T(1,128)S(1)}, s32[1,48]{1,0:T(1,128)}, u32[]{:S(2)}) copy-start(s32[1,48]{1,0:T(1,128)} %rows.7) | copy-start | bytes 580
  0.7 18.3 %copy-start = (bf16[48,128,128]{2,1,0:T(8,128)(2,1)S(1)}, bf16[48,128,128]{2,1,0:T(8,128)(2,1)}, u32[]{:S(2)}) copy-start(bf16[48,128,128]{2,1,0:T(8,128)(2,1)} %values.7) | copy-start | bytes 4718596
  1.4 38.6 %copy-start.1 = (bf16[2048,256]{1,0:T(8,128)(2,1)S(1)}, bf16[2048,256]{1,0:T(8,128)(2,1)}, u32[]{:S(2)}) copy-start(bf16[2048,256]{1,0:T(8,128)(2,1)} %refs_6_.1) | copy-start | bytes 3145732
  70.4 19.8 %copy-start.2 = (f32[16,128]{1,0:T(8,128)S(1)}, f32[16,128]{1,0:T(8,128)}, u32[]{:S(2)}) copy-start(f32[16,128]{1,0:T(8,128)} %get-tuple-element.20.row_scale) | copy-start | bytes 24580
  90.2 19.5 %copy-start.5 = (f32[16,128]{1,0:T(8,128)S(1)}, f32[16,128]{1,0:T(8,128)}, u32[]{:S(2)}) copy-start(f32[16,128]{1,0:T(8,128)} %get-tuple-element.22.col_scale) | copy-start | bytes 24580
  112.3 3.1 %collective-permute-start = (s16[8,272,128]{2,1,0:T(8,128)(2,1)S(1)}, s16[8,272,128]{2,1,0:T(8,128)(2,1)S(1)}, u32[]{:S(2)}, u32[]{:S(2)}) collective-permute-start(s16[8,272,128]{2,1,0:T(8,128)(2,1)S(1)} %get-tuple-element.26), channel_id=1, source_target_pairs={{0,16},{16,0},{1,17},{17,1},{2,18},{18,2},{3,19},{19,3},{4,20},{20... | collective-permute-start | bytes 1671176 | tf_op jit(solution)/shard_map/ppermute | solution.py:425

commit v8 on v7

--- a/solution.py
+++ b/solution.py
@@ -22,12 +22,12 @@
 SMEM = pl.BlockSpec(memory_space=pltpu.SMEM)
 
 
-def call(body, inputs, outs, scratch=(), specs=None, mib=16):
+def call(body, inputs, outs, scratch=(), specs=None, mib=16, out_specs=None):
     return pl.pallas_call(
         body,
         out_shape=[jax.ShapeDtypeStruct(s, d) for s, d in outs],
         in_specs=specs or [SMEM if a.dtype == jnp.int32 else VMEM for a in inputs],
-        out_specs=[VMEM] * len(outs),
+        out_specs=out_specs or [VMEM] * len(outs),
         scratch_shapes=[pltpu.VMEM(s[0], s[1]) if isinstance(s, tuple) else s for s in scratch],
         compiler_params=pltpu.CompilerParams(vmem_limit_bytes=int(mib * 1024 * 1024)),
     )(*inputs)
@@ -126,7 +126,7 @@
         src[b, 0:K, :] = (block * vec[b : b + 1, :]).astype(BF16)
     mean = jnp.sum(first[...], axis=0)[16:18] / docs
     mean = jnp.concatenate([jnp.broadcast_to(mean[h : h + 1], (TILE, TILE)).T for h in range(2)], axis=0)
-    over_tiles(count[0, 0], values, cols, rows, src, acc, True, GROUP)
+    over_tiles(count[0, 0], values, cols, rows, src, acc, True, CAP)
     for b in range(RB):
         weight = jnp.sum(acc[b, K : K + 16, :], axis=0, keepdims=True)
         out[b] = (acc[b, 0:K, :] - mean * weight).astype(out.dtype)
@@ -173,7 +173,7 @@
 
 
 def right_product(values, rows, cols, count, scaled, col_scale, keep, send, acc):
-    over_tiles(count[0, 0], values, rows, cols, scaled, acc, False, GROUP)
+    over_tiles(count[0, 0], values, rows, cols, scaled, acc, False, CAP)
     core = lax.axis_index("term_1")
     peak = jnp.zeros((K, TILE), F32)
     for i in range(CB // 2):
@@ -264,37 +264,38 @@
 
 
 def eliminate(blocks, at):
-    blocks = list(blocks)
+    blocks = [list(b) for b in blocks]
     sub = lax.broadcasted_iota(jnp.int32, (2, 8, TILE), 1)
     for g in range(len(blocks)):
         lead = blocks[g]
         lanes = [at + 8 * g + b for b in range(8)]
-        head = [spread(lead, l) for l in lanes]
+        head = [spread(lead[0], l) for l in lanes]
         pivots = jnp.ones((2, 8, TILE), F32)
         lines, inverses, entries = [], [], []
         for a in range(8):
             pivot = head[a][:, a : a + 1]
             inv = 1.0 / pivot
-            line = lead[:, a : a + 1]
+            line = [x[:, a : a + 1] for x in lead]
             entry = [head[b][:, a : a + 1] for b in range(8)]
             lines.append(line)
             inverses.append(inv)
             entries.append(entry)
             pivots = jnp.where(sub == a, pivot, pivots)
-            f = jnp.where(sub > a, head[a] * inv, 0.0)
-            lead = lead - f * line
+            f = jnp.where(sub > a, head[a], 0.0) * inv
+            lead = [x - f * y for x, y in zip(lead, line)]
             for b in range(a + 1, 8):
                 head[b] = head[b] - f * entry[b]
         for j in range(g + 1, len(blocks)):
-            cols = [spread(blocks[j], l) for l in lanes]
+            cols = [spread(blocks[j][0], l) for l in lanes]
             total = blocks[j]
             for a in range(8):
                 f = cols[a] * inverses[a]
-                total = total - f * lines[a]
+                total = [x - f * y for x, y in zip(total, lines[a])]
                 for b in range(a + 1, 8):
                     cols[b] = cols[b] - f * entries[a][b]
             blocks[j] = total
-        blocks[g] = lead * lax.rsqrt(pivots)
+        root = lax.rsqrt(pivots)
+        blocks[g] = [x * root for x in lead]
     return blocks
 
 
@@ -314,14 +315,17 @@
         other = PANEL - at
         unit = jnp.where(lane == line + other, 1.0, 0.0)
         here = (lane >= at) & (lane < at + PANEL)
-        block = jnp.where(here, own, unit)
-        done = jnp.concatenate(eliminate([block[:, 8 * j : 8 * j + 8] for j in range(PANEL // 8)], at), axis=1)
-        inverses = [done[m, :, other : other + PANEL] for m in range(2)]
+        parts = [jnp.where(here, own, unit)]
+        then = (end // TILE) * TILE
         if end < K:
-            then = (end // TILE) * TILE
+            parts.append(own if then == first else work[:, start:end, then : then + TILE])
+        done = eliminate([[x[:, 8 * j : 8 * j + 8] for x in parts] for j in range(PANEL // 8)], at)
+        done = [jnp.concatenate([b[i] for b in done], axis=1) for i in range(len(parts))]
+        inverses = [done[0][m, :, other : other + PANEL] for m in range(2)]
+        if end < K:
             ahead = []
             for m in range(2):
-                upper = precise(inverses[m], work[m, start:end, then : then + TILE])
+                upper = done[1][m]
                 cut = upper[:, end - then : end - then + PANEL]
                 ahead.append(work[m, end : end + PANEL, then : then + TILE] - precise(cut, upper, 0))
             own = jnp.stack(ahead)
@@ -360,14 +364,22 @@
     return sum(jnp.dot(a, b, preferred_element_type=F32) for a, b in zip(lhs, rhs))
 
 
-def bases(inverse, scaled, row_scale, gathered, lean, left_out, right_out):
+def bases(inverse, scaled, row_scale, gathered, lean, left_out, right_out, left_held, right_held, sems):
+    copies = []
+
+    def send(rows, out, b):
+        own = pl.ds(b * TILE, 2 * TILE)
+        copies.append(pltpu.make_async_copy(rows.at[own], out.at[own], sems.at[len(copies)]))
+        copies[-1].start()
+
     hi, low = halves(inverse[0])
     for b in range(0, RB, 2):
         pair = jnp.concatenate([scaled[b], scaled[b + 1]], axis=1)
         total = mixed((hi, low), (pair, pair))
         for u in range(2):
             basis = total[:, u * TILE : (u + 1) * TILE] / row_scale[b + u : b + u + 1, :]
-            left_out[(b + u) * TILE : (b + u + 1) * TILE, :] = basis.T.astype(BF16)
+            left_held[(b + u) * TILE : (b + u + 1) * TILE, :] = basis.T.astype(BF16)
+        send(left_held, left_out, b)
     hi, low = halves(inverse[1])
     step = steps_of(gathered, 16)
     mean = lean[:, 0:1]
@@ -378,7 +390,10 @@
         top, rest = halves(pair)
         total = mixed((hi, low, hi), (top, top, rest))
         for u in range(2):
-            right_out[(b + u) * TILE : (b + u + 1) * TILE, :] = total[:, u * TILE : (u + 1) * TILE].T.astype(BF16)
+            right_held[(b + u) * TILE : (b + u + 1) * TILE, :] = total[:, u * TILE : (u + 1) * TILE].T.astype(BF16)
+        send(right_held, right_out, b)
+    for copy in copies:
+        copy.wait()
 
 
 def exchanged(x, axis):
@@ -444,6 +459,8 @@
         bases,
         (inverse, scaled, row_scale, gathered, lean),
         [((RB * TILE, K), BF16), ((CB * TILE, K), BF16)],
+        [((RB * TILE, K), BF16), ((CB * TILE, K), BF16), pltpu.SemaphoreType.DMA((16,))],
+        out_specs=[pl.BlockSpec(memory_space=pltpu.HBM)] * 2,
     )
     return (row_scale.reshape(-1), col_scale.reshape(-1), left_basis, right_basis)
 

time: 198 us -> 197 us (level)
  Pallas kernels: 30.9 us -> 28.6 us
    pallas_call x13, Pallas kernels: 30.9 us -> 28.6 us  [call(): pl.pallas_call(body, out_shape=[jax.ShapeDtypeStruct(s, d) for s, d in ou...]
where the time goes in v8:
time: 197 us
  blocking collectives  163 us (83%)
  Pallas kernels  28.6 us (15%)
  starting transfers between devices  2.02 us (1%)
    all_to_all x9, blocking collectives, exchanged(): return lax.all_to_all(x, axis, split_axis=0, concat_axis=0, tiled=True)  142 us
    pallas_call x13, Pallas kernels, call(): pl.pallas_call(body, out_shape=[jax.ShapeDtypeStruct(s, d) for s, d in ou...  28.6 us
    all_gather x1, blocking collectives, per_device(): gathered = lax.all_gather(part, TERM)  21.6 us
  transfers between devices with their start and end apart: 1, of which 1 were waited for; matrix products, arithmetic and copies ran while one was open for 0% of the time, Pallas kernels for 0%

profile of v8, /device:TPU:1, one launch (start us, length us, event | category | flops | bytes accessed | tf_op | source)
XLA Modules:
  0.0 197.1 jit_solution(11207667364622729862)
XLA Ops:
  0.6 0.0 copy-start.4
  0.6 0.0 copy-start.3
  0.7 0.0 copy-start
  1.4 0.0 copy-start.1
  1.4 3.0 %shard_map.84 = f32[16,16,128]{2,1,0:T(8,128)} custom-call(bf16[48,128,128]{2,1,0:T(8,128)(2,1)} %values.7, s32[1,48]{1,0:T(1,128)} %rows.7, s32[1,48]{1,0:T(1,128)} %cols.7, s32[1,1]{1,0:T(1,128)S(6)} %copy.9.count.refs_3_), custom_call_target="tpu_custom_call" | custom-call | tf_op jit(solution)/shard_map/pallas_call | solution.py:26
  4.4 14.5 %all_to_all.45.got = f32[16,16,128]{2,1,0:T(8,128)S(1)} all-to-all(f32[16,16,128]{2,1,0:T(8,128)} %shard_map.84), channel_id=1, replica_groups=mesh['term_0'=8,'term_1'=2,'doc_0'=4,'doc_1'=4] {'doc_0','doc_1'}, dimensions={0} | all-to-all | bytes 262144 | tf_op jit(solution)/shard_map/all_to_all | solution.py:400
  18.9 0.0 copy-done.4
  18.9 0.0 copy-done.3
  18.9 0.0 copy-done
  18.9 1.6 shard_map.85
  20.5 19.5 %all_to_all.46.got = f32[16,16,128]{2,1,0:T(8,128)S(1)} all-to-all(f32[16,16,128]{2,1,0:T(8,128)S(1)} %get-tuple-element.19), channel_id=1, replica_groups=mesh['term_0'=8,'term_1'=2,'doc_0'=4,'doc_1'=4] {'term_0','term_1'}, dimensions={0} | all-to-all | bytes 262144 | tf_op jit(solution)/shard_map/all_to_all | solution.py:400
  40.0 0.0 copy-done.1
  40.0 1.4 shard_map.86
  41.5 11.3 %all_to_all.47.got.refs_5_ = f32[16,24,128]{2,1,0:T(8,128)S(1)} all-to-all(f32[16,24,128]{2,1,0:T(8,128)S(1)} %shard_map.86), channel_id=1, replica_groups=mesh['term_0'=8,'term_1'=2,'doc_0'=4,'doc_1'=4] {'doc_0','doc_1'}, dimensions={0} | all-to-all | bytes 393216 | tf_op jit(solution)/shard_map/all_to_all | solution.py:400
  52.8 1.6 shard_map.87
  54.4 12.5 %all_to_all.48.refs_4_ = f32[16,16,128]{2,1,0:T(8,128)S(1)} all-to-all(f32[16,16,128]{2,1,0:T(8,128)S(1)} %get-tuple-element.21), channel_id=1, replica_groups=mesh['term_0'=8,'term_1'=2,'doc_0'=4,'doc_1'=4] {'term_0','term_1'}, dimensions={0} | all-to-all | bytes 262144 | tf_op jit(solution)/shard_map/all_to_all | solution.py:400
  66.9 3.3 %shard_map.88 = (bf16[16,256,128]{2,1,0:T(8,128)(2,1)S(1)}, f32[16,128]{1,0:T(8,128)}) custom-call(bf16[48,128,128]{2,1,0:T(8,128)(2,1)S(1)} %copy-done, s32[1,48]{1,0:T(1,128)S(1)} %copy-done.3, s32[1,48]{1,0:T(1,128)S(1)} %copy-done.4, s32[1,1]{1,0:T(1,128)S(6)} %copy.9.count.refs_3_, f32[16,16,128]{2,1,0:T(8,128)S(1)} %all_to_all.48.refs_4_, ...), custom_call_target="tpu_custom_call" | custom-call | tf_op jit(solution)/shard_map/pallas_call | solution.py:26
  70.2 0.0 copy-start.2
  70.2 19.9 %all_to_all.49.got = bf16[16,256,128]{2,1,0:T(8,128)(2,1)S(1)} all-to-all(bf16[16,256,128]{2,1,0:T(8,128)(2,1)S(1)} %get-tuple-element.23), channel_id=1, replica_groups=mesh['term_0'=8,'term_1'=2,'doc_0'=4,'doc_1'=4] {'doc_0','doc_1'}, dimensions={0} | all-to-all | bytes 2097152 | tf_op jit(solution)/shard_map/all_to_all | solution.py:400
  90.1 0.0 copy-done.2
  90.1 0.0 copy-start.5
  90.1 0.6 shard_map.89
  90.7 19.3 %all_to_all.50.scaled = bf16[16,256,128]{2,1,0:T(8,128)(2,1)S(1)} all-to-all(bf16[16,256,128]{2,1,0:T(8,128)(2,1)S(1)} %get-tuple-element.24), channel_id=1, replica_groups=mesh['term_0'=8,'term_1'=2,'doc_0'=4,'doc_1'=4] {'doc_0','doc_1'}, dimensions={0} | all-to-all | bytes 2097152 | tf_op jit(solution)/shard_map/all_to_all | solution.py:400
  110.0 0.0 copy-done.5
  110.0 2.5 %shard_map.90 = (f32[8,256,128]{2,1,0:T(8,128)S(1)}, s16[8,272,128]{2,1,0:T(8,128)(2,1)S(1)}) custom-call(bf16[48,128,128]{2,1,0:T(8,128)(2,1)S(1)} %copy-done, s32[1,48]{1,0:T(1,128)S(1)} %copy-done.3, s32[1,48]{1,0:T(1,128)S(1)} %copy-done.4, s32[1,1]{1,0:T(1,128)S(6)} %copy.9.count.refs_3_, bf16[16,256,128]{2,1,0:T(8,128)(2,1)S(1)} %all_to_all.50.scaled, ...), custom_call_target="tpu_custom_call" | custom-call | tf_op jit(solution)/shard_map/pallas_call | solution.py:26
  112.5 2.0 %collective-permute-start = (s16[8,272,128]{2,1,0:T(8,128)(2,1)S(1)}, s16[8,272,128]{2,1,0:T(8,128)(2,1)S(1)}, u32[]{:S(2)}, u32[]{:S(2)}) collective-permute-start(s16[8,272,128]{2,1,0:T(8,128)(2,1)S(1)} %get-tuple-element.26), channel_id=1, source_target_pairs={{0,16},{16,0},{1,17},{17,1},{2,18},{18,2},{3,19},{19,3},{4,20},{20... | collective-permute-start | bytes 1671176 | tf_op jit(solution)/shard_map/ppermute | solution.py:440
  114.5 1.6 collective-permute-done.got
  116.1 0.6 shard_map.91
  116.7 20.7 %all_to_all.51.got = s16[8,272,128]{2,1,0:T(8,128)(2,1)S(1)} all-to-all(s16[8,272,128]{2,1,0:T(8,128)(2,1)S(1)} %shard_map.91), channel_id=1, replica_groups=mesh['term_0'=8,'term_1'=2,'doc_0'=4,'doc_1'=4] {'term_0'}, dimensions={0} | all-to-all | bytes 1114112 | tf_op jit(solution)/shard_map/all_to_all | solution.py:400
  137.4 1.0 shard_map.92
  138.4 11.7 %all_to_all.52.got = f32[16,16,384]{2,1,0:T(8,128)S(1)} all-to-all(f32[16,16,384]{2,1,0:T(8,128)S(1)} %bitcast.8), channel_id=1, replica_groups=mesh['term_0'=8,'term_1'=2,'doc_0'=4,'doc_1'=4] {'doc_0','doc_1'}, dimensions={0} | all-to-all | bytes 786432 | tf_op jit(solution)/shard_map/all_to_all | solution.py:400
  150.1 0.1 shard_map.93
  150.2 21.6 %all-gather.2 = s16[6144,128]{1,0:T(8,128)(2,1)S(1)} all-gather(s16[384,128]{1,0:T(8,128)(2,1)S(1)} %shard_map.93), channel_id=2, replica_groups=mesh['term_0'=8,'term_1'=2,'doc_0'=4,'doc_1'=4] {'term_0','term_1'}, dimensions={0}, use_global_device_ids=true | all-gather | bytes 1671168 | tf_op jit(solution)/shard_map/all_gather | solution.py:449
  171.8 0.1 shard_map.94
  171.9 12.3 %all_to_all.53 = f32[16,16,384]{2,1,0:T(8,128)S(1)} all-to-all(f32[16,16,384]{2,1,0:T(8,128)S(1)} %shard_map.94), channel_id=1, replica_groups=mesh['term_0'=8,'term_1'=2,'doc_0'=4,'doc_1'=4] {'doc_0','doc_1'}, dimensions={0} | all-to-all | bytes 786432 | tf_op jit(solution)/shard_map/all_to_all | solution.py:400
  184.2 10.0 %shard_map.95 = (f32[2,256,256]{2,1,0:T(8,128)S(1)}, f32[256,128]{1,0:T(8,128)S(1)}) custom-call(f32[256,384]{1,0:T(8,128)S(1)} %bitcast.7), custom_call_target="tpu_custom_call" | custom-call | tf_op jit(solution)/shard_map/pallas_call | solution.py:26
  194.3 2.7 %shard_map.96 = (bf16[2048,256]{1,0:T(8,128)(2,1)}, bf16[2048,256]{1,0:T(8,128)(2,1)}) custom-call(f32[2,256,256]{2,1,0:T(8,128)S(1)} %get-tuple-element.30.inverse, bf16[16,256,128]{2,1,0:T(8,128)(2,1)S(1)} %all_to_all.50.scaled, f32[16,128]{1,0:T(8,128)S(1)} %copy-done.2, s16[16,384,128]{2,1,0:T(8,128)(2,1)S(1)} %bitcast.6, ...), custom_call_target="tpu_custom_call" | custom-call | tf_op jit(solution)/shard_map/pallas_call | solution.py:26
Async XLA Ops:
  0.6 18.3 %copy-start.4 = (s32[1,48]{1,0:T(1,128)S(1)}, s32[1,48]{1,0:T(1,128)}, u32[]{:S(2)}) copy-start(s32[1,48]{1,0:T(1,128)} %cols.7) | copy-start | bytes 580
  0.6 18.3 %copy-start.3 = (s32[1,48]{1,0:T(1,128)S(1)}, s32[1,48]{1,0:T(1,128)}, u32[]{:S(2)}) copy-start(s32[1,48]{1,0:T(1,128)} %rows.7) | copy-start | bytes 580
  0.7 18.3 %copy-start = (bf16[48,128,128]{2,1,0:T(8,128)(2,1)S(1)}, bf16[48,128,128]{2,1,0:T(8,128)(2,1)}, u32[]{:S(2)}) copy-start(bf16[48,128,128]{2,1,0:T(8,128)(2,1)} %values.7) | copy-start | bytes 4718596
  1.4 38.6 %copy-start.1 = (bf16[2048,256]{1,0:T(8,128)(2,1)S(1)}, bf16[2048,256]{1,0:T(8,128)(2,1)}, u32[]{:S(2)}) copy-start(bf16[2048,256]{1,0:T(8,128)(2,1)} %refs_6_.1) | copy-start | bytes 3145732
  70.2 19.9 %copy-start.2 = (f32[16,128]{1,0:T(8,128)S(1)}, f32[16,128]{1,0:T(8,128)}, u32[]{:S(2)}) copy-start(f32[16,128]{1,0:T(8,128)} %get-tuple-element.20.row_scale) | copy-start | bytes 24580
  90.1 19.9 %copy-start.5 = (f32[16,128]{1,0:T(8,128)S(1)}, f32[16,128]{1,0:T(8,128)}, u32[]{:S(2)}) copy-start(f32[16,128]{1,0:T(8,128)} %get-tuple-element.22.col_scale) | copy-start | bytes 24580
  112.5 3.6 %collective-permute-start = (s16[8,272,128]{2,1,0:T(8,128)(2,1)S(1)}, s16[8,272,128]{2,1,0:T(8,128)(2,1)S(1)}, u32[]{:S(2)}, u32[]{:S(2)}) collective-permute-start(s16[8,272,128]{2,1,0:T(8,128)(2,1)S(1)} %get-tuple-element.26), channel_id=1, source_target_pairs={{0,16},{16,0},{1,17},{17,1},{2,18},{18,2},{3,19},{19,3},{4,20},{20... | collective-permute-start | bytes 1671176 | tf_op jit(solution)/shard_map/ppermute | solution.py:440

commit v9 on v8

--- a/solution.py
+++ b/solution.py
@@ -126,7 +126,7 @@
         src[b, 0:K, :] = (block * vec[b : b + 1, :]).astype(BF16)
     mean = jnp.sum(first[...], axis=0)[16:18] / docs
     mean = jnp.concatenate([jnp.broadcast_to(mean[h : h + 1], (TILE, TILE)).T for h in range(2)], axis=0)
-    over_tiles(count[0, 0], values, cols, rows, src, acc, True, CAP)
+    over_tiles(count[0, 0], values, cols, rows, src, acc, True, GROUP)
     for b in range(RB):
         weight = jnp.sum(acc[b, K : K + 16, :], axis=0, keepdims=True)
         out[b] = (acc[b, 0:K, :] - mean * weight).astype(out.dtype)
@@ -173,7 +173,7 @@
 
 
 def right_product(values, rows, cols, count, scaled, col_scale, keep, send, acc):
-    over_tiles(count[0, 0], values, rows, cols, scaled, acc, False, CAP)
+    over_tiles(count[0, 0], values, rows, cols, scaled, acc, False, GROUP)
     core = lax.axis_index("term_1")
     peak = jnp.zeros((K, TILE), F32)
     for i in range(CB // 2):
@@ -309,8 +309,8 @@
     own = work[:, 0:PANEL, 0:TILE]
     for start in range(0, K, PANEL):
         first = (start // TILE) * TILE
-        span = slice(first, first + 3 * TILE)
         end = start + PANEL
+        span = slice(first if end < K else K, first + 3 * TILE)
         at = start - first
         other = PANEL - at
         unit = jnp.where(lane == line + other, 1.0, 0.0)

time: 197 us -> 197 us (level)
  no operation moved by 1% of the time
where the time goes in v9:
time: 197 us
  blocking collectives  163 us (83%)
  Pallas kernels  29.6 us (15%)
    all_to_all x9, blocking collectives, exchanged(): return lax.all_to_all(x, axis, split_axis=0, concat_axis=0, tiled=True)  141 us
    pallas_call x13, Pallas kernels, call(): pl.pallas_call(body, out_shape=[jax.ShapeDtypeStruct(s, d) for s, d in ou...  29.6 us
    all_gather x1, blocking collectives, per_device(): gathered = lax.all_gather(part, TERM)  21.6 us
  transfers between devices with their start and end apart: 1, of which 1 were waited for; matrix products, arithmetic and copies ran while one was open for 0% of the time, Pallas kernels for 0%

profile of v9, /device:TPU:1, one launch (start us, length us, event | category | flops | bytes accessed | tf_op | source)
XLA Modules:
  0.0 197.2 jit_solution(15648846416914571263)
XLA Ops:
  0.6 0.0 copy-start.4
  0.6 0.0 copy-start.3
  0.7 0.0 copy-start
  1.4 0.0 copy-start.1
  1.4 3.0 %shard_map.84 = f32[16,16,128]{2,1,0:T(8,128)} custom-call(bf16[48,128,128]{2,1,0:T(8,128)(2,1)} %values.7, s32[1,48]{1,0:T(1,128)} %rows.7, s32[1,48]{1,0:T(1,128)} %cols.7, s32[1,1]{1,0:T(1,128)S(6)} %copy.9.count.refs_3_), custom_call_target="tpu_custom_call" | custom-call | tf_op jit(solution)/shard_map/pallas_call | solution.py:26
  4.5 14.5 %all_to_all.45.got = f32[16,16,128]{2,1,0:T(8,128)S(1)} all-to-all(f32[16,16,128]{2,1,0:T(8,128)} %shard_map.84), channel_id=1, replica_groups=mesh['term_0'=8,'term_1'=2,'doc_0'=4,'doc_1'=4] {'doc_0','doc_1'}, dimensions={0} | all-to-all | bytes 262144 | tf_op jit(solution)/shard_map/all_to_all | solution.py:400
  18.9 0.0 copy-done.4
  18.9 0.0 copy-done.3
  18.9 0.0 copy-done
  18.9 1.6 shard_map.85
  20.5 19.5 %all_to_all.46.got = f32[16,16,128]{2,1,0:T(8,128)S(1)} all-to-all(f32[16,16,128]{2,1,0:T(8,128)S(1)} %get-tuple-element.19), channel_id=1, replica_groups=mesh['term_0'=8,'term_1'=2,'doc_0'=4,'doc_1'=4] {'term_0','term_1'}, dimensions={0} | all-to-all | bytes 262144 | tf_op jit(solution)/shard_map/all_to_all | solution.py:400
  40.0 0.0 copy-done.1
  40.0 2.0 shard_map.86
  42.0 10.5 %all_to_all.47.got.refs_5_ = f32[16,24,128]{2,1,0:T(8,128)S(1)} all-to-all(f32[16,24,128]{2,1,0:T(8,128)S(1)} %shard_map.86), channel_id=1, replica_groups=mesh['term_0'=8,'term_1'=2,'doc_0'=4,'doc_1'=4] {'doc_0','doc_1'}, dimensions={0} | all-to-all | bytes 393216 | tf_op jit(solution)/shard_map/all_to_all | solution.py:400
  52.5 1.6 shard_map.87
  54.1 12.6 %all_to_all.48.refs_4_ = f32[16,16,128]{2,1,0:T(8,128)S(1)} all-to-all(f32[16,16,128]{2,1,0:T(8,128)S(1)} %get-tuple-element.21), channel_id=1, replica_groups=mesh['term_0'=8,'term_1'=2,'doc_0'=4,'doc_1'=4] {'term_0','term_1'}, dimensions={0} | all-to-all | bytes 262144 | tf_op jit(solution)/shard_map/all_to_all | solution.py:400
  66.7 3.8 %shard_map.88 = (bf16[16,256,128]{2,1,0:T(8,128)(2,1)S(1)}, f32[16,128]{1,0:T(8,128)}) custom-call(bf16[48,128,128]{2,1,0:T(8,128)(2,1)S(1)} %copy-done, s32[1,48]{1,0:T(1,128)S(1)} %copy-done.3, s32[1,48]{1,0:T(1,128)S(1)} %copy-done.4, s32[1,1]{1,0:T(1,128)S(6)} %copy.9.count.refs_3_, f32[16,16,128]{2,1,0:T(8,128)S(1)} %all_to_all.48.refs_4_, ...), custom_call_target="tpu_custom_call" | custom-call | tf_op jit(solution)/shard_map/pallas_call | solution.py:26
  70.5 0.0 copy-start.2
  70.5 19.7 %all_to_all.49.got = bf16[16,256,128]{2,1,0:T(8,128)(2,1)S(1)} all-to-all(bf16[16,256,128]{2,1,0:T(8,128)(2,1)S(1)} %get-tuple-element.23), channel_id=1, replica_groups=mesh['term_0'=8,'term_1'=2,'doc_0'=4,'doc_1'=4] {'doc_0','doc_1'}, dimensions={0} | all-to-all | bytes 2097152 | tf_op jit(solution)/shard_map/all_to_all | solution.py:400
  90.2 0.0 copy-done.2
  90.2 0.0 copy-start.5
  90.2 0.6 shard_map.89
  90.8 19.2 %all_to_all.50.scaled = bf16[16,256,128]{2,1,0:T(8,128)(2,1)S(1)} all-to-all(bf16[16,256,128]{2,1,0:T(8,128)(2,1)S(1)} %get-tuple-element.24), channel_id=1, replica_groups=mesh['term_0'=8,'term_1'=2,'doc_0'=4,'doc_1'=4] {'doc_0','doc_1'}, dimensions={0} | all-to-all | bytes 2097152 | tf_op jit(solution)/shard_map/all_to_all | solution.py:400
  110.0 0.0 copy-done.5
  110.0 2.7 %shard_map.90 = (f32[8,256,128]{2,1,0:T(8,128)S(1)}, s16[8,272,128]{2,1,0:T(8,128)(2,1)S(1)}) custom-call(bf16[48,128,128]{2,1,0:T(8,128)(2,1)S(1)} %copy-done, s32[1,48]{1,0:T(1,128)S(1)} %copy-done.3, s32[1,48]{1,0:T(1,128)S(1)} %copy-done.4, s32[1,1]{1,0:T(1,128)S(6)} %copy.9.count.refs_3_, bf16[16,256,128]{2,1,0:T(8,128)(2,1)S(1)} %all_to_all.50.scaled, ...), custom_call_target="tpu_custom_call" | custom-call | tf_op jit(solution)/shard_map/pallas_call | solution.py:26
  112.7 1.4 collective-permute-start
  114.1 1.6 collective-permute-done.got
  115.7 0.6 shard_map.91
  116.3 20.7 %all_to_all.51.got = s16[8,272,128]{2,1,0:T(8,128)(2,1)S(1)} all-to-all(s16[8,272,128]{2,1,0:T(8,128)(2,1)S(1)} %shard_map.91), channel_id=1, replica_groups=mesh['term_0'=8,'term_1'=2,'doc_0'=4,'doc_1'=4] {'term_0'}, dimensions={0} | all-to-all | bytes 1114112 | tf_op jit(solution)/shard_map/all_to_all | solution.py:400
  137.0 1.0 shard_map.92
  138.0 12.3 %all_to_all.52.got = f32[16,16,384]{2,1,0:T(8,128)S(1)} all-to-all(f32[16,16,384]{2,1,0:T(8,128)S(1)} %bitcast.8), channel_id=1, replica_groups=mesh['term_0'=8,'term_1'=2,'doc_0'=4,'doc_1'=4] {'doc_0','doc_1'}, dimensions={0} | all-to-all | bytes 786432 | tf_op jit(solution)/shard_map/all_to_all | solution.py:400
  150.3 0.1 shard_map.93
  150.4 21.6 %all-gather.2 = s16[6144,128]{1,0:T(8,128)(2,1)S(1)} all-gather(s16[384,128]{1,0:T(8,128)(2,1)S(1)} %shard_map.93), channel_id=2, replica_groups=mesh['term_0'=8,'term_1'=2,'doc_0'=4,'doc_1'=4] {'term_0','term_1'}, dimensions={0}, use_global_device_ids=true | all-gather | bytes 1671168 | tf_op jit(solution)/shard_map/all_gather | solution.py:449
  172.0 0.1 shard_map.94
  172.1 12.3 %all_to_all.53 = f32[16,16,384]{2,1,0:T(8,128)S(1)} all-to-all(f32[16,16,384]{2,1,0:T(8,128)S(1)} %shard_map.94), channel_id=1, replica_groups=mesh['term_0'=8,'term_1'=2,'doc_0'=4,'doc_1'=4] {'doc_0','doc_1'}, dimensions={0} | all-to-all | bytes 786432 | tf_op jit(solution)/shard_map/all_to_all | solution.py:400
  184.5 9.9 %shard_map.95 = (f32[2,256,256]{2,1,0:T(8,128)S(1)}, f32[256,128]{1,0:T(8,128)S(1)}) custom-call(f32[256,384]{1,0:T(8,128)S(1)} %bitcast.7), custom_call_target="tpu_custom_call" | custom-call | tf_op jit(solution)/shard_map/pallas_call | solution.py:26
  194.3 2.7 %shard_map.96 = (bf16[2048,256]{1,0:T(8,128)(2,1)}, bf16[2048,256]{1,0:T(8,128)(2,1)}) custom-call(f32[2,256,256]{2,1,0:T(8,128)S(1)} %get-tuple-element.30.inverse, bf16[16,256,128]{2,1,0:T(8,128)(2,1)S(1)} %all_to_all.50.scaled, f32[16,128]{1,0:T(8,128)S(1)} %copy-done.2, s16[16,384,128]{2,1,0:T(8,128)(2,1)S(1)} %bitcast.6, ...), custom_call_target="tpu_custom_call" | custom-call | tf_op jit(solution)/shard_map/pallas_call | solution.py:26
Async XLA Ops:
  0.6 18.3 %copy-start.4 = (s32[1,48]{1,0:T(1,128)S(1)}, s32[1,48]{1,0:T(1,128)}, u32[]{:S(2)}) copy-start(s32[1,48]{1,0:T(1,128)} %cols.7) | copy-start | bytes 580
  0.6 18.3 %copy-start.3 = (s32[1,48]{1,0:T(1,128)S(1)}, s32[1,48]{1,0:T(1,128)}, u32[]{:S(2)}) copy-start(s32[1,48]{1,0:T(1,128)} %rows.7) | copy-start | bytes 580
  0.7 18.3 %copy-start = (bf16[48,128,128]{2,1,0:T(8,128)(2,1)S(1)}, bf16[48,128,128]{2,1,0:T(8,128)(2,1)}, u32[]{:S(2)}) copy-start(bf16[48,128,128]{2,1,0:T(8,128)(2,1)} %values.7) | copy-start | bytes 4718596
  1.4 38.6 %copy-start.1 = (bf16[2048,256]{1,0:T(8,128)(2,1)S(1)}, bf16[2048,256]{1,0:T(8,128)(2,1)}, u32[]{:S(2)}) copy-start(bf16[2048,256]{1,0:T(8,128)(2,1)} %refs_6_.1) | copy-start | bytes 3145732
  70.5 19.7 %copy-start.2 = (f32[16,128]{1,0:T(8,128)S(1)}, f32[16,128]{1,0:T(8,128)}, u32[]{:S(2)}) copy-start(f32[16,128]{1,0:T(8,128)} %get-tuple-element.20.row_scale) | copy-start | bytes 24580
  90.2 19.8 %copy-start.5 = (f32[16,128]{1,0:T(8,128)S(1)}, f32[16,128]{1,0:T(8,128)}, u32[]{:S(2)}) copy-start(f32[16,128]{1,0:T(8,128)} %get-tuple-element.22.col_scale) | copy-start | bytes 24580
  112.7 3.0 %collective-permute-start = (s16[8,272,128]{2,1,0:T(8,128)(2,1)S(1)}, s16[8,272,128]{2,1,0:T(8,128)(2,1)S(1)}, u32[]{:S(2)}, u32[]{:S(2)}) collective-permute-start(s16[8,272,128]{2,1,0:T(8,128)(2,1)S(1)} %get-tuple-element.26), channel_id=1, source_target_pairs={{0,16},{16,0},{1,17},{17,1},{2,18},{18,2},{3,19},{19,3},{4,20},{20... | collective-permute-start | bytes 1671176 | tf_op jit(solution)/shard_map/ppermute | solution.py:440
